TPU v7x, 256 devices: a whole 4x4x8 slice. The times are simulated.
256 devices in a mesh: slab: 64 (over x, y, z_lo), rep: 4 (over z_hi, core).
Axes of the slice: x: 4, y: 4, z: 8 (z_hi: 2, z_lo: 4; z = z_hi * 4 + z_lo), core: 2. Of those that a mesh axis runs over, the one named last changes fastest.
Arguments:
- cubes: bfloat16 [4, 256, 32, 32, 64], P('rep', 'slab'), may hold values from -6 to 6
- weight_a: bfloat16 [3, 3, 3, 64, 128], replicated, may hold values from -0.15625 to 0.15625
- weight_b: bfloat16 [3, 3, 3, 128, 256], replicated, may hold values from -0.109375 to 0.109375
- cotangent: bfloat16 [4, 64, 8, 8, 256], P('rep', 'slab'), may hold values from -6 to 6
Outputs:
- features: bfloat16 [4, 64, 8, 8, 256], P('rep', 'slab')
- grad_cubes: bfloat16 [4, 256, 32, 32, 64], P('rep', 'slab')
- grad_weight_a: float32 [3, 3, 3, 64, 128], replicated
- grad_weight_b: float32 [3, 3, 3, 128, 256], replicated
All inputs are finite; a program needn't handle non-finite values.
Results may differ from a plain program's by a relative error of at most 0.015.
Values may be sent and summed in bfloat16 or wider, within the bound.
No kernel may reach another device: no remote copies, remote signals or barrier semaphores. Data moves between devices by JAX's collectives and lax.ppermute only.
A program may use at most 128 MiB of HBM per device.

v0:
```python
import jax
import jax.numpy as jnp
from jax import lax
from jax.experimental import pallas as pl
from jax.experimental.pallas import tpu as pltpu
from jax.sharding import PartitionSpec as P

BF16 = jnp.bfloat16
F32 = jnp.float32
ROOM = 50 * 1024 * 1024
SCALAR = pl.BlockSpec(memory_space=pltpu.SMEM)
WHOLE = pl.BlockSpec(memory_space=pltpu.VMEM)


def nt_dot(lhs, rhs):
    return lax.dot_general(lhs, rhs, (((1,), (1,)), ((), ())), preferred_element_type=F32)


def nn_dot(lhs, rhs):
    return jnp.dot(lhs, rhs, preferred_element_type=F32)


def next_rows(value, period):
    rows = value.shape[0]
    row = lax.broadcasted_iota(jnp.int32, value.shape, 0) % period
    return jnp.where(row == period - 1, 0.0, pltpu.roll(value, rows - 1, 0))


def previous_rows(value, period):
    row = lax.broadcasted_iota(jnp.int32, value.shape, 0) % period
    return jnp.where(row == 0, 0.0, pltpu.roll(value, 1, 0))


def low_lanes(shape):
    return lax.broadcasted_iota(jnp.int32, shape, 1) < 64


def forward_a_kernel(left_ref, cells_ref, right_ref, weight_ref, window_ref, slope_ref, pooled_ref):
    edge = jnp.zeros((16, 256), BF16)
    for layer in range(6):
        if layer == 0:
            pairs = left_ref[...]
        elif layer == 5:
            pairs = right_ref[...]
        else:
            pairs = cells_ref[layer - 1]
        wide = pairs.astype(F32)
        outer = jnp.where(low_lanes(wide.shape), next_rows(wide, 16), previous_rows(wide, 16))
        window_ref[layer, 0:16, :] = edge
        window_ref[layer, 528:544, :] = edge
        window_ref[layer, 16:528, 0:128] = pairs
        window_ref[layer, 16:528, 128:256] = outer.astype(BF16)
    for half in range(2):
        total = None
        for tap in range(9):
            shift_x, shift_y = tap // 3, tap % 3
            first = 2 * half + shift_x
            window = window_ref[first : first + 2, 16 * shift_y : 16 * shift_y + 512, :]
            term = nn_dot(window.reshape(1024, 256), weight_ref[tap])
            total = term if total is None else total + term
        sigma = 1.0 / (1.0 + jnp.exp(-total))
        active = total * sigma
        slope = sigma * (1.0 + total * (1.0 - sigma))
        slope_ref[2 * half : 2 * half + 2] = slope.astype(BF16).reshape(2, 512, 256)
        blocks = active.reshape(2, 16, 2, 16, 256)
        blocks = (blocks[0] + blocks[1])
        blocks = blocks[:, 0] + blocks[:, 1]
        pooled = (blocks[:, :, :128] + blocks[:, :, 128:]) * 0.125
        pooled_ref[half] = pooled.astype(BF16).reshape(256, 128)


def forward_a(left, cells, right, weight):
    return pl.pallas_call(
        forward_a_kernel,
        out_shape=(
            jax.ShapeDtypeStruct((6, 544, 256), BF16),
            jax.ShapeDtypeStruct((4, 512, 256), BF16),
            jax.ShapeDtypeStruct((2, 256, 128), BF16),
        ),
        compiler_params=pltpu.CompilerParams(vmem_limit_bytes=ROOM),
        cost_estimate=pl.CostEstimate(flops=2 * 2048 * 2304 * 256, bytes_accessed=6 * 10**6, transcendentals=10**6),
    )(left, cells, right, weight)


def block_b_kernel(core_ref, left_ref, cells_ref, right_ref, weight_ref, cot_ref, features_ref, keep_ref, send_ref, grad_ref, window, grads, column):
    edge = jnp.zeros((16, 384), BF16)
    for layer in range(6):
        if layer < 2:
            cells = left_ref[layer]
        elif layer < 4:
            cells = cells_ref[layer - 2]
        else:
            cells = right_ref[layer - 4]
        wide = cells.astype(F32)
        window[layer, 0:16, :] = edge
        window[layer, 272:288, :] = edge
        window[layer, 16:272, 0:128] = previous_rows(wide, 16).astype(BF16)
        window[layer, 16:272, 128:256] = cells
        window[layer, 16:272, 256:384] = next_rows(wide, 16).astype(BF16)
    total = None
    for tap in range(9):
        shift_x, shift_y = tap // 3, tap % 3
        view = window[shift_x : shift_x + 4, 16 * shift_y : 16 * shift_y + 256, :]
        term = nn_dot(view.reshape(1024, 384), weight_ref[tap])
        total = term if total is None else total + term
    sigma = 1.0 / (1.0 + jnp.exp(-total))
    active = (total * sigma)[256:768].reshape(2, 8, 2, 16, 256)
    active = active[0] + active[1]
    active = (active[:, 0] + active[:, 1]).reshape(128, 256)
    for part in range(2):
        lanes = slice(128 * part, 128 * part + 128)
        column[part] = active[:, lanes]
        pooled = column[part, pl.ds(0, 64, stride=2), :] + column[part, pl.ds(1, 64, stride=2), :]
        features_ref[:, lanes] = (pooled * 0.125).astype(BF16)
    slope = sigma * (1.0 + total * (1.0 - sigma))
    for layer in range(4):
        spread = cot_ref[(layer + 1) // 2].astype(F32).reshape(8, 1, 16, 256) * 0.125
        spread = jnp.broadcast_to(spread, (8, 2, 16, 256)).reshape(256, 256)
        grads[layer, 0:16, :] = edge[:, :256]
        grads[layer, 272:288, :] = edge[:, :256]
        grads[layer, 16:272, :] = (spread * slope[256 * layer : 256 * layer + 256]).astype(BF16)
    core = core_ref[0]
    own = grads[1:3, 16:272, :].reshape(512, 256)
    turned = own.T
    for tap in range(9):
        shift_x, shift_y = tap // 3, tap % 3
        view = window[1 + shift_x : 3 + shift_x, 16 * shift_y : 16 * shift_y + 256, :].reshape(512, 384)
        terms = (nn_dot(turned, view) * 0.25).T.astype(BF16)
        keep_ref[tap] = jnp.where(core == 0, terms[:, :128], terms[:, 128:])
        send_ref[tap] = jnp.where(core == 0, terms[:, 128:], terms[:, :128])
    total = None
    for tap in range(9):
        shift_x, shift_y = tap // 3, tap % 3
        view = grads[2 - shift_x : 4 - shift_x, 32 - 16 * shift_y : 288 - 16 * shift_y, :].reshape(512, 256)
        term = nt_dot(view, weight_ref[tap])
        total = term if total is None else total + term
    result = next_rows(total[:, 0:128], 16) + total[:, 128:256] + previous_rows(total[:, 256:384], 16)
    grad_ref[...] = result.astype(BF16).reshape(2, 256, 128)


def block_b(core, left, cells, right, weight, cot):
    return pl.pallas_call(
        block_b_kernel,
        in_specs=[SCALAR] + [WHOLE] * 5,
        out_shape=(
            jax.ShapeDtypeStruct((64, 256), BF16),
            jax.ShapeDtypeStruct((9, 384, 128), BF16),
            jax.ShapeDtypeStruct((9, 384, 128), BF16),
            jax.ShapeDtypeStruct((2, 256, 128), BF16),
        ),
        scratch_shapes=[
            pltpu.VMEM((6, 288, 384), BF16),
            pltpu.VMEM((4, 288, 256), BF16),
            pltpu.VMEM((2, 128, 128), F32),
        ],
        compiler_params=pltpu.CompilerParams(vmem_limit_bytes=ROOM),
        cost_estimate=pl.CostEstimate(flops=4 * 2 * 512 * 3456 * 256, bytes_accessed=5 * 10**6, transcendentals=5 * 10**5),
    )(core, left, cells, right, weight, cot)


def kernel_a_kernel(core_ref, grad_ref, slope_ref, window_ref, pre_ref, keep_ref, send_ref):
    core = core_ref[0]
    for layer in range(4):
        spread = grad_ref[layer // 2].astype(F32).reshape(16, 1, 16, 128) * 0.125
        spread = jnp.broadcast_to(spread, (16, 2, 16, 128)).reshape(512, 128)
        slope = slope_ref[layer].astype(F32)
        pre_ref[layer, :, 0:128] = (spread * slope[:, 0:128]).astype(BF16)
        pre_ref[layer, :, 128:256] = (spread * slope[:, 128:256]).astype(BF16)
    turned = pre_ref[...].reshape(2048, 256).T
    for tap in range(9):
        shift_x, shift_y = tap // 3, tap % 3
        view = window_ref[shift_x : shift_x + 4, 16 * shift_y : 16 * shift_y + 512, :].reshape(2048, 256)
        terms = nn_dot(turned, view)
        terms = (terms[:128] + pltpu.roll(terms[128:], 192, 1)) * 0.25
        terms = terms.T.astype(BF16)
        first = jnp.concatenate([terms[192:256], terms[0:32]])
        second = terms[32:128]
        keep_ref[tap] = jnp.where(core == 0, first, second)
        send_ref[tap] = jnp.where(core == 0, second, first)


def kernel_a(core, grad, slope, window):
    return pl.pallas_call(
        kernel_a_kernel,
        in_specs=[SCALAR] + [WHOLE] * 3,
        out_shape=(
            jax.ShapeDtypeStruct((4, 512, 256), BF16),
            jax.ShapeDtypeStruct((9, 96, 128), BF16),
            jax.ShapeDtypeStruct((9, 96, 128), BF16),
        ),
        compiler_params=pltpu.CompilerParams(vmem_limit_bytes=ROOM),
        cost_estimate=pl.CostEstimate(flops=2 * 2048 * 2304 * 256, bytes_accessed=6 * 10**6, transcendentals=0),
    )(core, grad, slope, window)


def back_a_kernel(left_ref, cells_ref, right_ref, weight_ref, out_ref, grads):
    edge = jnp.zeros((16, 256), BF16)
    for layer in range(6):
        grads[layer, 0:16, :] = edge
        grads[layer, 528:544, :] = edge
        if layer == 0:
            grads[layer, 16:528, :] = left_ref[...]
        elif layer == 5:
            grads[layer, 16:528, :] = right_ref[...]
        else:
            grads[layer, 16:528, :] = cells_ref[layer - 1]
    for half in range(2):
        total = None
        for tap in range(9):
            shift_x, shift_y = tap // 3, tap % 3
            first = 2 * half + 2 - shift_x
            view = grads[first : first + 2, 32 - 16 * shift_y : 544 - 16 * shift_y, :].reshape(1024, 256)
            term = nt_dot(view, weight_ref[tap])
            total = term if total is None else total + term
        outer = total[:, 128:256]
        outer = jnp.where(low_lanes(outer.shape), previous_rows(outer, 16), next_rows(outer, 16))
        out_ref[2 * half : 2 * half + 2] = (total[:, 0:128] + outer).astype(BF16).reshape(2, 512, 128)


def back_a(left, cells, right, weight):
    return pl.pallas_call(
        back_a_kernel,
        out_shape=jax.ShapeDtypeStruct((4, 512, 128), BF16),
        scratch_shapes=[pltpu.VMEM((6, 544, 256), BF16)],
        compiler_params=pltpu.CompilerParams(vmem_limit_bytes=ROOM),
        cost_estimate=pl.CostEstimate(flops=2 * 2048 * 2304 * 256, bytes_accessed=5 * 10**6, transcendentals=0),
    )(left, cells, right, weight)


def paired_weight(weight):
    taps = weight.reshape(9, 3, 64, 128)
    none = jnp.zeros((9, 64, 128), weight.dtype)
    even = jnp.concatenate([taps[:, 1], taps[:, 2], none, taps[:, 0]], axis=1)
    odd = jnp.concatenate([taps[:, 0], taps[:, 1], taps[:, 2], none], axis=1)
    return jnp.concatenate([even, odd], axis=2)


def unpack_kernel(core_ref, mine_ref, away_ref, sum_a_ref, sum_b_ref):
    core = core_ref[0]
    for tap in range(9):
        rows = slice(96 * tap, 96 * tap + 96)
        mine, away = mine_ref[rows].astype(F32), away_ref[rows].astype(F32)
        sum_a_ref[tap, 0] = jnp.where(core == 0, mine, away)
        sum_a_ref[tap, 1] = jnp.where(core == 0, away, mine)
        rows = slice(864 + 384 * tap, 1248 + 384 * tap)
        mine, away = mine_ref[rows].astype(F32), away_ref[rows].astype(F32)
        sum_b_ref[tap, :, 0:128] = jnp.where(core == 0, mine, away)
        sum_b_ref[tap, :, 128:256] = jnp.where(core == 0, away, mine)


def unpack(core, mine, away):
    return pl.pallas_call(
        unpack_kernel,
        in_specs=[SCALAR] + [WHOLE] * 2,
        out_shape=(
            jax.ShapeDtypeStruct((9, 2, 96, 128), F32),
            jax.ShapeDtypeStruct((9, 384, 256), F32),
        ),
        compiler_params=pltpu.CompilerParams(vmem_limit_bytes=ROOM),
        cost_estimate=pl.CostEstimate(flops=0, bytes_accessed=7 * 10**6, transcendentals=0),
    )(core, mine, away)


AXES = ("slab", "rep")
ACROSS = [[((16 * x + 4 * y + z) * 4 + rep) for x in range(4) for y in range(4)] for z in range(4) for rep in range(4)]
ALONG = [[((4 * plane + z) * 4 + 2 * far + core) for far in range(2) for z in range(4)] for plane in range(16) for core in range(2)]
CORES = [(device, device ^ 1) for device in range(256)]


def other_core(value):
    return lax.ppermute(value, AXES, CORES)


def exchange(blocks, groups):
    return lax.all_to_all(blocks, AXES, 0, 0, axis_index_groups=groups, tiled=True)


def total_of(blocks):
    return jnp.sum(blocks.astype(F32), axis=0).astype(BF16)


def reduce_over_chips(rows):
    part = total_of(exchange(rows.reshape(16, 272, 128), ACROSS))
    part = total_of(exchange(jnp.broadcast_to(part, (8, 272, 128)), ALONG))
    return exchange(jnp.broadcast_to(part, (16, 272, 128)), ACROSS).reshape(4352, 128)


def neighbours(to_left, to_right):
    count = lax.axis_size("slab")
    up = [(i, i + 1) for i in range(count - 1)]
    down = [(i + 1, i) for i in range(count - 1)]
    return lax.ppermute(to_right, "slab", up), lax.ppermute(to_left, "slab", down)


def shards(cubes, weight_a, weight_b, cotangent):
    core = (lax.axis_index("rep") % 2).reshape(1)
    pair_weight = paired_weight(weight_a)
    taps_b = weight_b.reshape(9, 384, 256)
    cells = cubes.reshape(4, 512, 128)
    cot = cotangent.reshape(64, 256)
    cot_rows = [cot[:, :128], cot[:, 128:]]
    left, right = neighbours(jnp.concatenate([cells[0]] + cot_rows), jnp.concatenate([cells[3]] + cot_rows))
    window, slope_a, pooled = forward_a(left[:512], cells, right[:512], pair_weight)
    pooled_left, pooled_right = neighbours(pooled, pooled)
    cots = [jnp.concatenate([side[512:576], side[576:640]], axis=1) for side in (left, right)]
    cots = jnp.stack([cots[0], cot, cots[1]])
    cots = jnp.broadcast_to(cots[:, :, None, :], (3, 64, 2, 256)).reshape(3, 128, 256)
    features, keep_b, send_b, grad_pooled = block_b(core, pooled_left, pooled, pooled_right, taps_b, cots)
    other_b = other_core(send_b)
    grad_pre, keep_a, send_a = kernel_a(core, grad_pooled, slope_a, window)
    other_a = other_core(send_a)
    grad_left, grad_right = neighbours(grad_pre[0], grad_pre[3])
    rows = [
        (keep.astype(F32) + other.astype(F32)).astype(BF16).reshape(-1, 128)
        for keep, other in ((keep_a, other_a), (keep_b, other_b))
    ]
    mine = reduce_over_chips(jnp.concatenate(rows + [jnp.zeros((32, 128), BF16)]))
    away = other_core(mine)
    grad_cubes = back_a(grad_left, grad_pre, grad_right, pair_weight)
    sum_a, sum_b = unpack(core, mine, away)
    return (
        features.reshape(1, 1, 8, 8, 256),
        grad_cubes.reshape(1, 4, 32, 32, 64),
        sum_a.reshape(3, 3, 3, 64, 128),
        sum_b.reshape(3, 3, 3, 128, 256),
    )


def solution(mesh):
    return jax.shard_map(
        shards,
        mesh=mesh,
        in_specs=(P("rep", "slab", None, None, None), P(), P(), P("rep", "slab", None, None, None)),
        out_specs=(
            P("rep", "slab", None, None, None),
            P("rep", "slab", None, None, None),
            P(),
            P(),
        ),
        check_vma=False,
    )
```

profile of v0, /device:TPU:2, one launch (start us, length us, event | category | flops | bytes accessed | tf_op | source)
XLA Modules:
  0.0 155.9 jit_solution(12575980589597975711)
XLA Ops:
  0.6 0.8 fusion.3
  1.5 1.1 fusion
  2.7 0.1 squeeze.24
  2.9 9.0 %collective-permute-start.1 = (bf16[640,128]{1,0:T(8,128)(2,1)S(1)}, bf16[640,128]{1,0:T(8,128)(2,1)S(1)}, u32[]{:S(2)}, u32[]{:S(2)}) collective-permute-start(bf16[640,128]{1,0:T(8,128)(2,1)S(1)} %get-tuple-element.39), channel_id=1, source_target_pairs={{4,0},{8,4},{12,8},{16,12},{20,16},{24,20},{28,24},{32,28},{36,32}... | collective-permute-start | bytes 491528 | tf_op jit(solution)/shard_map/ppermute | solution.py:292
  11.8 1.9 %collective-permute-start = (bf16[640,128]{1,0:T(8,128)(2,1)S(1)}, bf16[640,128]{1,0:T(8,128)(2,1)S(1)}, u32[]{:S(2)}, u32[]{:S(2)}) collective-permute-start(bf16[640,128]{1,0:T(8,128)(2,1)S(1)} %get-tuple-element.40), channel_id=1, source_target_pairs={{0,4},{4,8},{8,12},{12,16},{16,20},{20,24},{24,28},{28,32},{32,36}... | collective-permute-start | bytes 491528 | tf_op jit(solution)/shard_map/ppermute | solution.py:292
  13.8 0.5 reshape.57.cells_ref
  14.5 1.9 %collective-permute-done.1 = bf16[640,128]{1,0:T(8,128)(2,1)S(1)} collective-permute-done((bf16[640,128]{1,0:T(8,128)(2,1)S(1)}, bf16[640,128]{1,0:T(8,128)(2,1)S(1)}, u32[]{:S(2)}, u32[]{:S(2)}) %collective-permute-start.1) | collective-permute-done | bytes 163872 | tf_op jit(solution)/shard_map/ppermute | solution.py:292
  16.4 7.8 %collective-permute-done = bf16[640,128]{1,0:T(8,128)(2,1)S(1)} collective-permute-done((bf16[640,128]{1,0:T(8,128)(2,1)S(1)}, bf16[640,128]{1,0:T(8,128)(2,1)S(1)}, u32[]{:S(2)}, u32[]{:S(2)}) %collective-permute-start) | collective-permute-done | bytes 163872 | tf_op jit(solution)/shard_map/ppermute | solution.py:292
  24.2 3.4 %shard_map.75 = (bf16[6,544,256]{2,1,0:T(8,128)(2,1)}, bf16[4,512,256]{2,1,0:T(8,128)(2,1)S(1)}, bf16[2,256,128]{2,1,0:T(8,128)(2,1)S(1)}) custom-call(bf16[512,128]{1,0:T(8,128)(2,1)S(1)} %slice.67.left_ref, bf16[4,512,128]{2,1,0:T(8,128)(2,1)S(1)} %reshape.57.cells_ref, bf16[512,128]{1,0:T(8,128)(2,1)S(1)} %slice.68.right_ref, ...), custom_call_target="tpu_custom_call" | custom-call | flops 2415919104 | bytes 6000000 | tf_op jit(solution)/shard_map/pallas_call | solution.py:73
  27.7 1.9 %collective-permute-start.3 = (bf16[2,256,128]{2,1,0:T(8,128)(2,1)S(1)}, bf16[2,256,128]{2,1,0:T(8,128)(2,1)S(1)}, u32[]{:S(2)}, u32[]{:S(2)}) collective-permute-start(bf16[2,256,128]{2,1,0:T(8,128)(2,1)S(1)} %get-tuple-element.16.cells_ref), channel_id=1, source_target_pairs={{4,0},{8,4},{12,8},{16,12},{20,16},{24,20},{28,24},{32,28},{36,32}... | collective-permute-start | bytes 393224 | tf_op jit(solution)/shard_map/ppermute | solution.py:292
  29.6 3.9 %collective-permute-start.2 = (bf16[2,256,128]{2,1,0:T(8,128)(2,1)S(1)}, bf16[2,256,128]{2,1,0:T(8,128)(2,1)S(1)}, u32[]{:S(2)}, u32[]{:S(2)}) collective-permute-start(bf16[2,256,128]{2,1,0:T(8,128)(2,1)S(1)} %get-tuple-element.16.cells_ref), channel_id=1, source_target_pairs={{0,4},{4,8},{8,12},{12,16},{16,20},{20,24},{24,28},{28,32},{32,36}... | collective-permute-start | bytes 393224 | tf_op jit(solution)/shard_map/ppermute | solution.py:292
  33.8 2.6 %collective-permute-done.3.right_ref = bf16[2,256,128]{2,1,0:T(8,128)(2,1)S(1)} collective-permute-done((bf16[2,256,128]{2,1,0:T(8,128)(2,1)S(1)}, bf16[2,256,128]{2,1,0:T(8,128)(2,1)S(1)}, u32[]{:S(2)}, u32[]{:S(2)}) %collective-permute-start.3) | collective-permute-done | bytes 131104 | tf_op jit(solution)/shard_map/ppermute | solution.py:292
  36.4 4.8 %collective-permute-done.2.left_ref = bf16[2,256,128]{2,1,0:T(8,128)(2,1)S(1)} collective-permute-done((bf16[2,256,128]{2,1,0:T(8,128)(2,1)S(1)}, bf16[2,256,128]{2,1,0:T(8,128)(2,1)S(1)}, u32[]{:S(2)}, u32[]{:S(2)}) %collective-permute-start.2) | collective-permute-done | bytes 131104 | tf_op jit(solution)/shard_map/ppermute | solution.py:292
  41.2 11.6 %shard_map.76 = (bf16[64,256]{1,0:T(8,128)(2,1)}, bf16[9,384,128]{2,1,0:T(8,128)(2,1)S(1)}, bf16[9,384,128]{2,1,0:T(8,128)(2,1)S(1)}, bf16[2,256,128]{2,1,0:T(8,128)(2,1)S(1)}) custom-call(s32[1]{0:T(128)} %bitcast.core_ref, bf16[2,256,128]{2,1,0:T(8,128)(2,1)S(1)} %collective-permute-done.2.left_ref, bf16[2,256,128]{2,1,0:T(8,128)(2,1)S(1)} %get-tuple-element.16.cells_ref, ...), custom_call_target="tpu_custom_call" | custom-call | flops 3623878656 | bytes 5000000 | tf_op jit(solution)/shard_map/pallas_call | solution.py:142
  52.8 0.3 collective-permute-start.7
  53.1 4.4 %shard_map.77 = (bf16[4,512,256]{2,1,0:T(8,128)(2,1)S(1)}, bf16[9,96,128]{2,1,0:T(8,128)(2,1)S(1)}, bf16[9,96,128]{2,1,0:T(8,128)(2,1)S(1)}) custom-call(s32[1]{0:T(128)} %bitcast.core_ref, bf16[2,256,128]{2,1,0:T(8,128)(2,1)S(1)} %get-tuple-element.18.grad_ref, bf16[4,512,256]{2,1,0:T(8,128)(2,1)S(1)} %get-tuple-element.19.slope_ref, ...), custom_call_target="tpu_custom_call" | custom-call | flops 2415919104 | bytes 6000000 | tf_op jit(solution)/shard_map/pallas_call | solution.py:183
  57.5 0.6 collective-permute-start.6
  58.2 1.0 collective-permute-done.6
  59.3 0.2 add_convert_fusion
  59.6 3.8 %maximum_maximum_fusion.1 = bf16[4352,128]{1,0:T(8,128)(2,1)S(1)} fusion(bf16[3456,128]{1,0:T(8,128)(2,1)S(1)} %bitcast.35, bf16[864,128]{1,0:T(8,128)(2,1)S(1)} %bitcast.37, bf16[4352]{0:T(1024)(128)(2,1)S(1)} %pad.2.clone), kind=kLoop, calls=%fused_computation.2 | loop fusion | flops 3342336 | bytes 2228736 | tf_op jit(solution)/shard_map/concatenate | solution.py:317
  63.4 21.6 %all_to_all.15 = bf16[16,272,128]{2,1,0:T(8,128)(2,1)S(1)} all-to-all(bf16[16,272,128]{2,1,0:T(8,128)(2,1)S(1)} %bitcast.34), channel_id=1, replica_groups={{0,16,32,48,64,80,96,112,128,144,160,176,192,208,224,240},{1,17,33,49,6..., dimensions={0} | all-to-all | bytes 2228224 | tf_op jit(solution)/shard_map/all_to_all | solution.py:275
  85.0 0.2 reduce_sum.24
  85.3 22.8 %all_to_all.16 = bf16[8,272,128]{2,1,0:T(8,128)(2,1)S(1)} all-to-all(bf16[8,272,128]{2,1,0:T(8,128)(2,1)S(1)} %broadcast_in_dim.21), channel_id=1, replica_groups={{0,4,8,12,2,6,10,14},{1,5,9,13,3,7,11,15},{16,20,24,28,18,22,26,30},{17..., dimensions={0} | all-to-all | bytes 1114112 | tf_op jit(solution)/shard_map/all_to_all | solution.py:275
  108.4 18.9 %all_to_all.17 = bf16[16,272,128]{2,1,0:T(8,128)(2,1)S(1)} all-to-all(bf16[16,272,128]{2,1,0:T(8,128)(2,1)S(1)} %broadcast_in_dim.22), channel_id=1, replica_groups={{0,16,32,48,64,80,96,112,128,144,160,176,192,208,224,240},{1,17,33,49,6..., dimensions={0} | all-to-all | bytes 2228224 | tf_op jit(solution)/shard_map/all_to_all | solution.py:275
  127.3 5.1 %collective-permute-start.5 = (bf16[512,256]{1,0:T(8,128)(2,1)S(1)}, bf16[512,256]{1,0:T(8,128)(2,1)S(1)}, u32[]{:S(2)}, u32[]{:S(2)}) collective-permute-start(bf16[512,256]{1,0:T(8,128)(2,1)S(1)} %get-tuple-element.28), channel_id=1, source_target_pairs={{4,0},{8,4},{12,8},{16,12},{20,16},{24,20},{28,24},{32,28},{36,32}... | collective-permute-start | bytes 786440 | tf_op jit(solution)/shard_map/ppermute | solution.py:292
  132.4 1.9 %collective-permute-start.4 = (bf16[512,256]{1,0:T(8,128)(2,1)S(1)}, bf16[512,256]{1,0:T(8,128)(2,1)S(1)}, u32[]{:S(2)}, u32[]{:S(2)}) collective-permute-start(bf16[512,256]{1,0:T(8,128)(2,1)S(1)} %get-tuple-element.29), channel_id=1, source_target_pairs={{0,4},{4,8},{8,12},{12,16},{16,20},{20,24},{24,28},{28,32},{32,36}... | collective-permute-start | bytes 786440 | tf_op jit(solution)/shard_map/ppermute | solution.py:292
  134.4 4.7 %collective-permute-done.5.right_ref = bf16[512,256]{1,0:T(8,128)(2,1)S(1)} collective-permute-done((bf16[512,256]{1,0:T(8,128)(2,1)S(1)}, bf16[512,256]{1,0:T(8,128)(2,1)S(1)}, u32[]{:S(2)}, u32[]{:S(2)}) %collective-permute-start.5) | collective-permute-done | bytes 262176 | tf_op jit(solution)/shard_map/ppermute | solution.py:292
  139.1 8.5 %collective-permute-done.4.left_ref = bf16[512,256]{1,0:T(8,128)(2,1)S(1)} collective-permute-done((bf16[512,256]{1,0:T(8,128)(2,1)S(1)}, bf16[512,256]{1,0:T(8,128)(2,1)S(1)}, u32[]{:S(2)}, u32[]{:S(2)}) %collective-permute-start.4) | collective-permute-done | bytes 262176 | tf_op jit(solution)/shard_map/ppermute | solution.py:292
  147.6 2.7 %shard_map.78 = bf16[4,512,128]{2,1,0:T(8,128)(2,1)S(1)} custom-call(bf16[512,256]{1,0:T(8,128)(2,1)S(1)} %collective-permute-done.4.left_ref, bf16[4,512,256]{2,1,0:T(8,128)(2,1)S(1)} %copy-done.2, bf16[512,256]{1,0:T(8,128)(2,1)S(1)} %collective-permute-done.5.right_ref, bf16[9,256,256]{2,1,0:T(8,128)(2,1)S(1)} %maximum_maximum_fusion.weight_ref), custom_call_target="tpu_custom_call" | custom-call | flops 2415919104 | bytes 5000000 | tf_op jit(solution)/shard_map/pallas_call | solution.py:221
  150.3 0.8 copy-done
  151.1 2.4 %reshape.62 = bf16[1,4,32,32,64]{4,3,2,1,0:T(8,128)(2,1)} reshape(bf16[4,512,128]{2,1,0:T(8,128)(2,1)} %copy-done) | data formatting | bytes 1048576 | tf_op jit(solution)/shard_map/reshape | solution.py:323
  153.4 2.4 %shard_map.79 = (f32[9,2,96,128]{3,2,1,0:T(8,128)}, f32[9,384,256]{2,1,0:T(8,128)}) custom-call(s32[1]{0:T(128)} %bitcast.core_ref, bf16[4352,128]{1,0:T(8,128)(2,1)S(1)} %bitcast.33, bf16[4352,128]{1,0:T(8,128)(2,1)S(1)} %collective-permute-done.8.away_ref), custom_call_target="tpu_custom_call" | custom-call | bytes 7000000 | tf_op jit(solution)/shard_map/pallas_call | solution.py:252
  (35 shorter events, 1.1 us)
Async XLA Ops:
  0.6 13.2 %copy-start.3 = (bf16[1,4,32,32,64]{4,3,2,1,0:T(8,128)(2,1)S(1)}, bf16[1,4,32,32,64]{4,3,2,1,0:T(8,128)(2,1)}, u32[]{:S(2)}) copy-start(bf16[1,4,32,32,64]{4,3,2,1,0:T(8,128)(2,1)} %param.4) | copy-start | bytes 1572868
  2.5 11.7 %copy-start.4 = (bf16[3,3,3,64,128]{4,3,2,1,0:T(8,128)(2,1)S(1)}, bf16[3,3,3,64,128]{4,3,2,1,0:T(8,128)(2,1)}, u32[]{:S(2)}) copy-start(bf16[3,3,3,64,128]{4,3,2,1,0:T(8,128)(2,1)} %param.5) | copy-start | bytes 1327108
  2.9 13.5 %collective-permute-start.1 = (bf16[640,128]{1,0:T(8,128)(2,1)S(1)}, bf16[640,128]{1,0:T(8,128)(2,1)S(1)}, u32[]{:S(2)}, u32[]{:S(2)}) collective-permute-start(bf16[640,128]{1,0:T(8,128)(2,1)S(1)} %get-tuple-element.39), channel_id=1, source_target_pairs={{4,0},{8,4},{12,8},{16,12},{20,16},{24,20},{28,24},{32,28},{36,32}... | collective-permute-start | bytes 491528 | tf_op jit(solution)/shard_map/ppermute | solution.py:292
  11.8 12.4 %collective-permute-start = (bf16[640,128]{1,0:T(8,128)(2,1)S(1)}, bf16[640,128]{1,0:T(8,128)(2,1)S(1)}, u32[]{:S(2)}, u32[]{:S(2)}) collective-permute-start(bf16[640,128]{1,0:T(8,128)(2,1)S(1)} %get-tuple-element.40), channel_id=1, source_target_pairs={{0,4},{4,8},{8,12},{12,16},{16,20},{20,24},{24,28},{28,32},{32,36}... | collective-permute-start | bytes 491528 | tf_op jit(solution)/shard_map/ppermute | solution.py:292
  24.2 9.3 %copy-start.5 = (bf16[1,1,8,8,256]{4,3,2,1,0:T(8,128)(2,1)S(1)}, bf16[1,1,8,8,256]{4,3,2,1,0:T(8,128)(2,1)}, u32[]{:S(2)}) copy-start(bf16[1,1,8,8,256]{4,3,2,1,0:T(8,128)(2,1)} %param.7) | copy-start | bytes 98308
  27.7 8.7 %collective-permute-start.3 = (bf16[2,256,128]{2,1,0:T(8,128)(2,1)S(1)}, bf16[2,256,128]{2,1,0:T(8,128)(2,1)S(1)}, u32[]{:S(2)}, u32[]{:S(2)}) collective-permute-start(bf16[2,256,128]{2,1,0:T(8,128)(2,1)S(1)} %get-tuple-element.16.cells_ref), channel_id=1, source_target_pairs={{4,0},{8,4},{12,8},{16,12},{20,16},{24,20},{28,24},{32,28},{36,32}... | collective-permute-start | bytes 393224 | tf_op jit(solution)/shard_map/ppermute | solution.py:292
  29.6 11.7 %collective-permute-start.2 = (bf16[2,256,128]{2,1,0:T(8,128)(2,1)S(1)}, bf16[2,256,128]{2,1,0:T(8,128)(2,1)S(1)}, u32[]{:S(2)}, u32[]{:S(2)}) collective-permute-start(bf16[2,256,128]{2,1,0:T(8,128)(2,1)S(1)} %get-tuple-element.16.cells_ref), channel_id=1, source_target_pairs={{0,4},{4,8},{8,12},{12,16},{16,20},{20,24},{24,28},{28,32},{32,36}... | collective-permute-start | bytes 393224 | tf_op jit(solution)/shard_map/ppermute | solution.py:292
  52.8 6.5 %collective-permute-start.7 = (bf16[9,384,128]{2,1,0:T(8,128)(2,1)S(1)}, bf16[9,384,128]{2,1,0:T(8,128)(2,1)S(1)}, u32[]{:S(2)}, u32[]{:S(2)}) collective-permute-start(bf16[9,384,128]{2,1,0:T(8,128)(2,1)S(1)} %get-tuple-element.25), channel_id=1, source_target_pairs={{0,1},{1,0},{2,3},{3,2},{4,5},{5,4},{6,7},{7,6},{8,9},{9,8},{10,11... | collective-permute-start | bytes 2654216 | tf_op jit(solution)/shard_map/ppermute | solution.py:271
  57.5 5.9 %copy-start.1 = (bf16[4,512,256]{2,1,0:T(8,128)(2,1)}, bf16[4,512,256]{2,1,0:T(8,128)(2,1)S(1)}, u32[]{:S(2)}) copy-start(bf16[4,512,256]{2,1,0:T(8,128)(2,1)S(1)} %get-tuple-element.21.cells_ref) | copy-start | bytes 3145732
  57.5 1.7 %collective-permute-start.6 = (bf16[9,96,128]{2,1,0:T(8,128)(2,1)S(1)}, bf16[9,96,128]{2,1,0:T(8,128)(2,1)S(1)}, u32[]{:S(2)}, u32[]{:S(2)}) collective-permute-start(bf16[9,96,128]{2,1,0:T(8,128)(2,1)S(1)} %get-tuple-element.23), channel_id=1, source_target_pairs={{0,1},{1,0},{2,3},{3,2},{4,5},{5,4},{6,7},{7,6},{8,9},{9,8},{10,11... | collective-permute-start | bytes 663560 | tf_op jit(solution)/shard_map/ppermute | solution.py:271
  108.2 19.1 %copy-start.2 = (bf16[4,512,256]{2,1,0:T(8,128)(2,1)S(1)}, bf16[4,512,256]{2,1,0:T(8,128)(2,1)}, u32[]{:S(2)}) copy-start(bf16[4,512,256]{2,1,0:T(8,128)(2,1)} %copy-done.1) | copy-start | bytes 3145732
  127.2 26.2 %collective-permute-start.8 = (bf16[4352,128]{1,0:T(8,128)(2,1)S(1)}, bf16[4352,128]{1,0:T(8,128)(2,1)S(1)}, u32[]{:S(2)}, u32[]{:S(2)}) collective-permute-start(bf16[4352,128]{1,0:T(8,128)(2,1)S(1)} %bitcast.32), channel_id=1, source_target_pairs={{0,1},{1,0},{2,3},{3,2},{4,5},{5,4},{6,7},{7,6},{8,9},{9,8},{10,11... | collective-permute-start | bytes 3342344 | tf_op jit(solution)/shard_map/ppermute | solution.py:271
  127.3 11.8 %collective-permute-start.5 = (bf16[512,256]{1,0:T(8,128)(2,1)S(1)}, bf16[512,256]{1,0:T(8,128)(2,1)S(1)}, u32[]{:S(2)}, u32[]{:S(2)}) collective-permute-start(bf16[512,256]{1,0:T(8,128)(2,1)S(1)} %get-tuple-element.28), channel_id=1, source_target_pairs={{4,0},{8,4},{12,8},{16,12},{20,16},{24,20},{28,24},{32,28},{36,32}... | collective-permute-start | bytes 786440 | tf_op jit(solution)/shard_map/ppermute | solution.py:292
  132.4 15.1 %collective-permute-start.4 = (bf16[512,256]{1,0:T(8,128)(2,1)S(1)}, bf16[512,256]{1,0:T(8,128)(2,1)S(1)}, u32[]{:S(2)}, u32[]{:S(2)}) collective-permute-start(bf16[512,256]{1,0:T(8,128)(2,1)S(1)} %get-tuple-element.29), channel_id=1, source_target_pairs={{0,4},{4,8},{8,12},{12,16},{16,20},{20,24},{24,28},{28,32},{32,36}... | collective-permute-start | bytes 786440 | tf_op jit(solution)/shard_map/ppermute | solution.py:292
  150.3 0.8 copy-start
where the time goes:
time: 156 us
  blocking collectives  63.4 us (41%)
  waiting for transfers between devices  31.4 us (20%)
  starting transfers between devices  24.6 us (16%)
  Pallas kernels  24.5 us (16%)
  local copies, waits for them, and re-layouts  6.48 us (4%)
  other arithmetic  4.53 us (3%)
    all_to_all x3, blocking collectives, exchange(): lax.all_to_all(blocks, AXES, 0, 0, axis_index_groups=groups, tiled=True)  63.4 us
    ppermute x3, waiting for transfers between devices, neighbours(): lax.ppermute(to_right, 'slab', up)  21.1 us
    ppermute x3, starting transfers between devices, neighbours(): lax.ppermute(to_left, 'slab', down)  16 us
    pallas_call x1, Pallas kernels, block_b(): pl.pallas_call(block_b_kernel, in_specs=[SCALAR] + [WHOLE] * 5, out_shape...  11.6 us
    ppermute x3, waiting for transfers between devices, neighbours(): lax.ppermute(to_left, 'slab', down)  9.23 us
    ppermute x3, starting transfers between devices, neighbours(): lax.ppermute(to_right, 'slab', up)  7.76 us
    pallas_call x1, Pallas kernels, kernel_a(): pl.pallas_call(kernel_a_kernel, in_specs=[SCALAR] + [WHOLE] * 3, out_shap...  4.44 us
    concatenate x1, other arithmetic, shards(): jnp.concatenate(rows + [jnp.zeros((32, 128), BF16)])  3.83 us
  transfers between devices with their start and end apart: 9, of which 7 were waited for; matrix products, arithmetic and copies ran while one was open for 2% of the time, Pallas kernels for 5%

commit v1 on v0

--- a/solution.py
+++ b/solution.py
@@ -235,6 +235,24 @@
     return jnp.concatenate([even, odd], axis=2)
 
 
+def merge_kernel(keep_a_ref, other_a_ref, keep_b_ref, other_b_ref, rows_ref):
+    for tap in range(9):
+        rows = keep_a_ref[tap].astype(F32) + other_a_ref[tap].astype(F32)
+        rows_ref[96 * tap : 96 * tap + 96] = rows.astype(BF16)
+        rows = keep_b_ref[tap].astype(F32) + other_b_ref[tap].astype(F32)
+        rows_ref[864 + 384 * tap : 1248 + 384 * tap] = rows.astype(BF16)
+    rows_ref[4320:4352] = jnp.zeros((32, 128), BF16)
+
+
+def merge(keep_a, other_a, keep_b, other_b):
+    return pl.pallas_call(
+        merge_kernel,
+        out_shape=jax.ShapeDtypeStruct((4352, 128), BF16),
+        compiler_params=pltpu.CompilerParams(vmem_limit_bytes=ROOM),
+        cost_estimate=pl.CostEstimate(flops=0, bytes_accessed=4 * 10**6, transcendentals=0),
+    )(keep_a, other_a, keep_b, other_b)
+
+
 def unpack_kernel(core_ref, mine_ref, away_ref, sum_a_ref, sum_b_ref):
     core = core_ref[0]
     for tap in range(9):
@@ -263,8 +281,9 @@
 
 AXES = ("slab", "rep")
 ACROSS = [[((16 * x + 4 * y + z) * 4 + rep) for x in range(4) for y in range(4)] for z in range(4) for rep in range(4)]
-ALONG = [[((4 * plane + z) * 4 + 2 * far + core) for far in range(2) for z in range(4)] for plane in range(16) for core in range(2)]
+LINES = [[((4 * plane + z) * 4 + rep) for z in range(4)] for plane in range(16) for rep in range(4)]
 CORES = [(device, device ^ 1) for device in range(256)]
+FAR = [(device, device ^ 2) for device in range(256)]
 
 
 def other_core(value):
@@ -279,9 +298,11 @@
     return jnp.sum(blocks.astype(F32), axis=0).astype(BF16)
 
 
-def reduce_over_chips(rows):
-    part = total_of(exchange(rows.reshape(16, 272, 128), ACROSS))
-    part = total_of(exchange(jnp.broadcast_to(part, (8, 272, 128)), ALONG))
+def reduce_over_chips(blocks):
+    part = total_of(blocks)
+    part = total_of(exchange(part.reshape(4, 68, 128), LINES))
+    part = (part.astype(F32) + lax.ppermute(part, AXES, FAR).astype(F32)).astype(BF16)
+    part = exchange(jnp.broadcast_to(part, (4, 68, 128)), LINES).reshape(272, 128)
     return exchange(jnp.broadcast_to(part, (16, 272, 128)), ACROSS).reshape(4352, 128)
 
 
@@ -310,11 +331,10 @@
     grad_pre, keep_a, send_a = kernel_a(core, grad_pooled, slope_a, window)
     other_a = other_core(send_a)
     grad_left, grad_right = neighbours(grad_pre[0], grad_pre[3])
-    rows = [
-        (keep.astype(F32) + other.astype(F32)).astype(BF16).reshape(-1, 128)
-        for keep, other in ((keep_a, other_a), (keep_b, other_b))
-    ]
-    mine = reduce_over_chips(jnp.concatenate(rows + [jnp.zeros((32, 128), BF16)]))
+    rows = merge(keep_a, other_a, keep_b, other_b)
+    blocks = exchange(rows.reshape(16, 272, 128), ACROSS)
+    blocks, grad_left, grad_right = lax.optimization_barrier((blocks, grad_left, grad_right))
+    mine = reduce_over_chips(blocks)
     away = other_core(mine)
     grad_cubes = back_a(grad_left, grad_pre, grad_right, pair_weight)
     sum_a, sum_b = unpack(core, mine, away)

time: 156 us -> 141 us (0.904)
  the two profiles are of different devices: /device:TPU:2 before, /device:TPU:1 now
where the time goes in v1:
time: 141 us; the launch traced here: 140 us
  starting transfers between devices  53 us (38%)
  blocking collectives  32.5 us (23%)
  Pallas kernels  25.8 us (18%)
  waiting for transfers between devices  18.6 us (13%)
  local copies, waits for them, and re-layouts  9.18 us (7%)
    all_to_all x3, blocking collectives, exchange(): lax.all_to_all(blocks, AXES, 0, 0, axis_index_groups=groups, tiled=True)  32.5 us
    all_to_all x1, starting transfers between devices, exchange(): lax.all_to_all(blocks, AXES, 0, 0, axis_index_groups=groups, tiled=True)  19.8 us
    ppermute x3, starting transfers between devices, neighbours(): lax.ppermute(to_right, 'slab', up)  13.7 us
    pallas_call x1, Pallas kernels, block_b(): pl.pallas_call(block_b_kernel, in_specs=[SCALAR] + [WHOLE] * 5, out_shape...  11.6 us
    ppermute x3, starting transfers between devices, other_core(): return lax.ppermute(value, AXES, CORES)  11.2 us
    all_to_all x1, waiting for transfers between devices, exchange(): lax.all_to_all(blocks, AXES, 0, 0, axis_index_groups=groups, tiled=True)  8.24 us
    pallas_call x1, Pallas kernels, kernel_a(): pl.pallas_call(kernel_a_kernel, in_specs=[SCALAR] + [WHOLE] * 3, out_shap...  4.44 us
    ppermute x1, starting transfers between devices, reduce_over_chips(): lax.ppermute(part, AXES, FAR).astype(F32)  4.3 us
  transfers between devices with their start and end apart: 11, of which 7 were waited for; matrix products, arithmetic and copies ran while one was open for 3% of the time, Pallas kernels for 5%

profile of v1, /device:TPU:1, one launch (start us, length us, event | category | flops | bytes accessed | tf_op | source)
XLA Modules:
  0.0 140.3 jit_solution(12572223188570050573)
XLA Ops:
  0.6 0.8 fusion.3
  1.5 1.1 fusion
  2.9 1.3 collective-permute-start.1
  4.2 5.0 %collective-permute-start = (bf16[640,128]{1,0:T(8,128)(2,1)S(1)}, bf16[640,128]{1,0:T(8,128)(2,1)S(1)}, u32[]{:S(2)}, u32[]{:S(2)}) collective-permute-start(bf16[640,128]{1,0:T(8,128)(2,1)S(1)} %get-tuple-element.46), channel_id=1, source_target_pairs={{0,4},{4,8},{8,12},{12,16},{16,20},{20,24},{24,28},{28,32},{32,36}... | collective-permute-start | bytes 491528 | tf_op jit(solution)/shard_map/ppermute | solution.py:313
  10.0 1.5 %collective-permute-done = bf16[640,128]{1,0:T(8,128)(2,1)S(1)} collective-permute-done((bf16[640,128]{1,0:T(8,128)(2,1)S(1)}, bf16[640,128]{1,0:T(8,128)(2,1)S(1)}, u32[]{:S(2)}, u32[]{:S(2)}) %collective-permute-start) | collective-permute-done | bytes 163872 | tf_op jit(solution)/shard_map/ppermute | solution.py:313
  12.1 3.4 %shard_map.75 = (bf16[6,544,256]{2,1,0:T(8,128)(2,1)}, bf16[4,512,256]{2,1,0:T(8,128)(2,1)S(1)}, bf16[2,256,128]{2,1,0:T(8,128)(2,1)S(1)}) custom-call(bf16[512,128]{1,0:T(8,128)(2,1)S(1)} %slice.67.left_ref, bf16[4,512,128]{2,1,0:T(8,128)(2,1)S(1)} %reshape.57.cells_ref, bf16[512,128]{1,0:T(8,128)(2,1)S(1)} %slice.68.right_ref, ...), custom_call_target="tpu_custom_call" | custom-call | flops 2415919104 | bytes 6000000 | tf_op jit(solution)/shard_map/pallas_call | solution.py:73
  15.6 1.3 collective-permute-start.3
  16.8 4.7 %collective-permute-start.2 = (bf16[2,256,128]{2,1,0:T(8,128)(2,1)S(1)}, bf16[2,256,128]{2,1,0:T(8,128)(2,1)S(1)}, u32[]{:S(2)}, u32[]{:S(2)}) collective-permute-start(bf16[2,256,128]{2,1,0:T(8,128)(2,1)S(1)} %get-tuple-element.19.cells_ref), channel_id=1, source_target_pairs={{0,4},{4,8},{8,12},{12,16},{16,20},{20,24},{24,28},{28,32},{32,36}... | collective-permute-start | bytes 393224 | tf_op jit(solution)/shard_map/ppermute | solution.py:313
  21.6 0.7 fusion.1
  22.6 0.9 collective-permute-done.2.left_ref
  23.5 11.6 %shard_map.76 = (bf16[64,256]{1,0:T(8,128)(2,1)}, bf16[9,384,128]{2,1,0:T(8,128)(2,1)S(1)}, bf16[9,384,128]{2,1,0:T(8,128)(2,1)S(1)}, bf16[2,256,128]{2,1,0:T(8,128)(2,1)S(1)}) custom-call(s32[1]{0:T(128)} %bitcast.core_ref, bf16[2,256,128]{2,1,0:T(8,128)(2,1)S(1)} %collective-permute-done.2.left_ref, bf16[2,256,128]{2,1,0:T(8,128)(2,1)S(1)} %get-tuple-element.19.cells_ref, ...), custom_call_target="tpu_custom_call" | custom-call | flops 3623878656 | bytes 5000000 | tf_op jit(solution)/shard_map/pallas_call | solution.py:142
  35.1 4.5 %collective-permute-start.5 = (bf16[9,384,128]{2,1,0:T(8,128)(2,1)S(1)}, bf16[9,384,128]{2,1,0:T(8,128)(2,1)S(1)}, u32[]{:S(2)}, u32[]{:S(2)}) collective-permute-start(bf16[9,384,128]{2,1,0:T(8,128)(2,1)S(1)} %get-tuple-element.27), channel_id=1, source_target_pairs={{0,1},{1,0},{2,3},{3,2},{4,5},{5,4},{6,7},{7,6},{8,9},{9,8},{10,11... | collective-permute-start | bytes 2654216 | tf_op jit(solution)/shard_map/ppermute | solution.py:290
  39.6 4.4 %shard_map.77 = (bf16[4,512,256]{2,1,0:T(8,128)(2,1)S(1)}, bf16[9,96,128]{2,1,0:T(8,128)(2,1)S(1)}, bf16[9,96,128]{2,1,0:T(8,128)(2,1)S(1)}) custom-call(s32[1]{0:T(128)} %bitcast.core_ref, bf16[2,256,128]{2,1,0:T(8,128)(2,1)S(1)} %get-tuple-element.21.grad_ref, bf16[4,512,256]{2,1,0:T(8,128)(2,1)S(1)} %get-tuple-element.22.slope_ref, ...), custom_call_target="tpu_custom_call" | custom-call | flops 2415919104 | bytes 6000000 | tf_op jit(solution)/shard_map/pallas_call | solution.py:183
  44.1 1.5 %collective-permute-done.4.other_a_ref = bf16[9,96,128]{2,1,0:T(8,128)(2,1)S(1)} collective-permute-done((bf16[9,96,128]{2,1,0:T(8,128)(2,1)S(1)}, bf16[9,96,128]{2,1,0:T(8,128)(2,1)S(1)}, u32[]{:S(2)}, u32[]{:S(2)}) %collective-permute-start.4) | collective-permute-done | bytes 221216 | tf_op jit(solution)/shard_map/ppermute | solution.py:290
  45.6 1.2 shard_map.78
  46.8 19.8 %all-to-all-start = ((bf16[16,272,128]{2,1,0:T(8,128)(2,1)}), bf16[16,272,128]{2,1,0:T(8,128)(2,1)S(1)}, u32[]{:S(2)}, u32[]{:S(2)}) async-start(bf16[16,272,128]{2,1,0:T(8,128)(2,1)} %bitcast.11), calls=%async_computation | async-start | bytes 2228224 | tf_op jit(solution)/shard_map/all_to_all | solution.py:294
  66.7 1.3 collective-permute-start.7
  68.0 4.0 %collective-permute-start.6 = (bf16[512,256]{1,0:T(8,128)(2,1)S(1)}, bf16[512,256]{1,0:T(8,128)(2,1)S(1)}, u32[]{:S(2)}, u32[]{:S(2)}) collective-permute-start(bf16[512,256]{1,0:T(8,128)(2,1)S(1)} %get-tuple-element.35), channel_id=1, source_target_pairs={{0,4},{4,8},{8,12},{12,16},{16,20},{20,24},{24,28},{28,32},{32,36}... | collective-permute-start | bytes 786440 | tf_op jit(solution)/shard_map/ppermute | solution.py:313
  72.0 4.0 %collective-permute-done.7.right_ref = bf16[512,256]{1,0:T(8,128)(2,1)S(1)} collective-permute-done((bf16[512,256]{1,0:T(8,128)(2,1)S(1)}, bf16[512,256]{1,0:T(8,128)(2,1)S(1)}, u32[]{:S(2)}, u32[]{:S(2)}) %collective-permute-start.7) | collective-permute-done | bytes 262176 | tf_op jit(solution)/shard_map/ppermute | solution.py:313
  76.1 0.7 copy-done.3
  76.9 0.7 copy-done.5
  77.6 8.2 %all-to-all-done = bf16[16,272,128]{2,1,0:T(8,128)(2,1)S(1)} async-done(((bf16[16,272,128]{2,1,0:T(8,128)(2,1)}), bf16[16,272,128]{2,1,0:T(8,128)(2,1)S(1)}, u32[]{:S(2)}, u32[]{:S(2)}) %all-to-all-start) | async-done | bytes 1114144 | tf_op jit(solution)/shard_map/all_to_all | solution.py:294
  86.1 7.0 %all_to_all.20 = bf16[4,68,128]{2,1,0:T(8,128)(2,1)S(1)} all-to-all(bf16[4,68,128]{2,1,0:T(8,128)(2,1)S(1)} %reshape.64), channel_id=1, replica_groups={{0,4,8,12},{1,5,9,13},{2,6,10,14},{3,7,11,15},{16,20,24,28},{17,21,25,2..., dimensions={0} | all-to-all | bytes 139264 | tf_op jit(solution)/shard_map/all_to_all | solution.py:294
  93.1 4.3 %collective-permute-start.8 = (bf16[68,128]{1,0:T(8,128)(2,1)S(1)}, bf16[68,128]{1,0:T(8,128)(2,1)S(1)}, u32[]{:S(2)}, u32[]{:S(2)}) collective-permute-start(bf16[68,128]{1,0:T(8,128)(2,1)S(1)} %reduce_sum.25), channel_id=1, source_target_pairs={{0,2},{1,3},{2,0},{3,1},{4,6},{5,7},{6,4},{7,5},{8,10},{9,11},{10,... | collective-permute-start | bytes 52232 | tf_op jit(solution)/shard_map/ppermute | solution.py:304
  97.4 2.3 %collective-permute-done.8 = bf16[68,128]{1,0:T(8,128)(2,1)S(1)} collective-permute-done((bf16[68,128]{1,0:T(8,128)(2,1)S(1)}, bf16[68,128]{1,0:T(8,128)(2,1)S(1)}, u32[]{:S(2)}, u32[]{:S(2)}) %collective-permute-start.8) | collective-permute-done | bytes 17440 | tf_op jit(solution)/shard_map/ppermute | solution.py:304
  99.7 7.0 %all_to_all.21 = bf16[4,68,128]{2,1,0:T(8,128)(2,1)S(1)} all-to-all(bf16[4,68,128]{2,1,0:T(8,128)(2,1)S(1)} %broadcast_in_dim.17), channel_id=1, replica_groups={{0,4,8,12},{1,5,9,13},{2,6,10,14},{3,7,11,15},{16,20,24,28},{17,21,25,2..., dimensions={0} | all-to-all | bytes 139264 | tf_op jit(solution)/shard_map/all_to_all | solution.py:294
  106.9 18.5 %all_to_all.22 = bf16[16,272,128]{2,1,0:T(8,128)(2,1)S(1)} all-to-all(bf16[16,272,128]{2,1,0:T(8,128)(2,1)S(1)} %broadcast_in_dim.18), channel_id=1, replica_groups={{0,16,32,48,64,80,96,112,128,144,160,176,192,208,224,240},{1,17,33,49,6..., dimensions={0} | all-to-all | bytes 2228224 | tf_op jit(solution)/shard_map/all_to_all | solution.py:294
  125.4 6.7 %collective-permute-start.9 = (bf16[4352,128]{1,0:T(8,128)(2,1)S(1)}, bf16[4352,128]{1,0:T(8,128)(2,1)S(1)}, u32[]{:S(2)}, u32[]{:S(2)}) collective-permute-start(bf16[4352,128]{1,0:T(8,128)(2,1)S(1)} %bitcast.30), channel_id=1, source_target_pairs={{0,1},{1,0},{2,3},{3,2},{4,5},{5,4},{6,7},{7,6},{8,9},{9,8},{10,11... | collective-permute-start | bytes 3342344 | tf_op jit(solution)/shard_map/ppermute | solution.py:290
  132.1 2.7 %shard_map.79 = bf16[4,512,128]{2,1,0:T(8,128)(2,1)S(1)} custom-call(bf16[512,256]{1,0:T(8,128)(2,1)S(1)} %copy-done.6, bf16[4,512,256]{2,1,0:T(8,128)(2,1)S(1)} %copy-done.2, bf16[512,256]{1,0:T(8,128)(2,1)S(1)} %copy-done.4, bf16[9,256,256]{2,1,0:T(8,128)(2,1)S(1)} %maximum_maximum_fusion.weight_ref), custom_call_target="tpu_custom_call" | custom-call | flops 2415919104 | bytes 5000000 | tf_op jit(solution)/shard_map/pallas_call | solution.py:221
  134.8 0.8 copy-done
  135.5 2.4 %reshape.63 = bf16[1,4,32,32,64]{4,3,2,1,0:T(8,128)(2,1)} reshape(bf16[4,512,128]{2,1,0:T(8,128)(2,1)} %copy-done) | data formatting | bytes 1048576 | tf_op jit(solution)/shard_map/reshape | solution.py:343
  137.9 2.4 %shard_map.80 = (f32[9,2,96,128]{3,2,1,0:T(8,128)}, f32[9,384,256]{2,1,0:T(8,128)}) custom-call(s32[1]{0:T(128)} %bitcast.core_ref, bf16[4352,128]{1,0:T(8,128)(2,1)S(1)} %bitcast.31, bf16[4352,128]{1,0:T(8,128)(2,1)S(1)} %collective-permute-done.9.away_ref), custom_call_target="tpu_custom_call" | custom-call | bytes 7000000 | tf_op jit(solution)/shard_map/pallas_call | solution.py:270
  (48 shorter events, 2.6 us)
Async XLA Ops:
  0.6 8.6 %copy-start.7 = (bf16[1,4,32,32,64]{4,3,2,1,0:T(8,128)(2,1)S(1)}, bf16[1,4,32,32,64]{4,3,2,1,0:T(8,128)(2,1)}, u32[]{:S(2)}) copy-start(bf16[1,4,32,32,64]{4,3,2,1,0:T(8,128)(2,1)} %param.4) | copy-start | bytes 1572868
  2.5 7.2 %copy-start.8 = (bf16[3,3,3,64,128]{4,3,2,1,0:T(8,128)(2,1)S(1)}, bf16[3,3,3,64,128]{4,3,2,1,0:T(8,128)(2,1)}, u32[]{:S(2)}) copy-start(bf16[3,3,3,64,128]{4,3,2,1,0:T(8,128)(2,1)} %param.5) | copy-start | bytes 1327108
  2.9 7.1 %collective-permute-start.1 = (bf16[640,128]{1,0:T(8,128)(2,1)S(1)}, bf16[640,128]{1,0:T(8,128)(2,1)S(1)}, u32[]{:S(2)}, u32[]{:S(2)}) collective-permute-start(bf16[640,128]{1,0:T(8,128)(2,1)S(1)} %get-tuple-element.45), channel_id=1, source_target_pairs={{4,0},{8,4},{12,8},{16,12},{20,16},{24,20},{28,24},{32,28},{36,32}... | collective-permute-start | bytes 491528 | tf_op jit(solution)/shard_map/ppermute | solution.py:313
  4.2 7.3 %collective-permute-start = (bf16[640,128]{1,0:T(8,128)(2,1)S(1)}, bf16[640,128]{1,0:T(8,128)(2,1)S(1)}, u32[]{:S(2)}, u32[]{:S(2)}) collective-permute-start(bf16[640,128]{1,0:T(8,128)(2,1)S(1)} %get-tuple-element.46), channel_id=1, source_target_pairs={{0,4},{4,8},{8,12},{12,16},{16,20},{20,24},{24,28},{28,32},{32,36}... | collective-permute-start | bytes 491528 | tf_op jit(solution)/shard_map/ppermute | solution.py:313
  11.4 0.7 copy-start.9
  12.1 10.2 %copy-start.10 = (bf16[1,1,8,8,256]{4,3,2,1,0:T(8,128)(2,1)S(1)}, bf16[1,1,8,8,256]{4,3,2,1,0:T(8,128)(2,1)}, u32[]{:S(2)}) copy-start(bf16[1,1,8,8,256]{4,3,2,1,0:T(8,128)(2,1)} %param.7) | copy-start | bytes 98308
  15.6 7.0 %collective-permute-start.3 = (bf16[2,256,128]{2,1,0:T(8,128)(2,1)S(1)}, bf16[2,256,128]{2,1,0:T(8,128)(2,1)S(1)}, u32[]{:S(2)}, u32[]{:S(2)}) collective-permute-start(bf16[2,256,128]{2,1,0:T(8,128)(2,1)S(1)} %get-tuple-element.19.cells_ref), channel_id=1, source_target_pairs={{4,0},{8,4},{12,8},{16,12},{20,16},{24,20},{28,24},{32,28},{36,32}... | collective-permute-start | bytes 393224 | tf_op jit(solution)/shard_map/ppermute | solution.py:313
  16.8 6.7 %collective-permute-start.2 = (bf16[2,256,128]{2,1,0:T(8,128)(2,1)S(1)}, bf16[2,256,128]{2,1,0:T(8,128)(2,1)S(1)}, u32[]{:S(2)}, u32[]{:S(2)}) collective-permute-start(bf16[2,256,128]{2,1,0:T(8,128)(2,1)S(1)} %get-tuple-element.19.cells_ref), channel_id=1, source_target_pairs={{0,4},{4,8},{8,12},{12,16},{16,20},{20,24},{24,28},{28,32},{32,36}... | collective-permute-start | bytes 393224 | tf_op jit(solution)/shard_map/ppermute | solution.py:313
  35.1 10.5 %collective-permute-start.5 = (bf16[9,384,128]{2,1,0:T(8,128)(2,1)S(1)}, bf16[9,384,128]{2,1,0:T(8,128)(2,1)S(1)}, u32[]{:S(2)}, u32[]{:S(2)}) collective-permute-start(bf16[9,384,128]{2,1,0:T(8,128)(2,1)S(1)} %get-tuple-element.27), channel_id=1, source_target_pairs={{0,1},{1,0},{2,3},{3,2},{4,5},{5,4},{6,7},{7,6},{8,9},{9,8},{10,11... | collective-permute-start | bytes 2654216 | tf_op jit(solution)/shard_map/ppermute | solution.py:290
  44.0 22.7 %copy-start.1 = (bf16[4,512,256]{2,1,0:T(8,128)(2,1)}, bf16[4,512,256]{2,1,0:T(8,128)(2,1)S(1)}, u32[]{:S(2)}) copy-start(bf16[4,512,256]{2,1,0:T(8,128)(2,1)S(1)} %get-tuple-element.28.cells_ref) | copy-start | bytes 3145732
  44.0 1.6 %collective-permute-start.4 = (bf16[9,96,128]{2,1,0:T(8,128)(2,1)S(1)}, bf16[9,96,128]{2,1,0:T(8,128)(2,1)S(1)}, u32[]{:S(2)}, u32[]{:S(2)}) collective-permute-start(bf16[9,96,128]{2,1,0:T(8,128)(2,1)S(1)} %get-tuple-element.25), channel_id=1, source_target_pairs={{0,1},{1,0},{2,3},{3,2},{4,5},{5,4},{6,7},{7,6},{8,9},{9,8},{10,11... | collective-permute-start | bytes 663560 | tf_op jit(solution)/shard_map/ppermute | solution.py:290
  46.8 39.1 %all-to-all-start = ((bf16[16,272,128]{2,1,0:T(8,128)(2,1)}), bf16[16,272,128]{2,1,0:T(8,128)(2,1)S(1)}, u32[]{:S(2)}, u32[]{:S(2)}) async-start(bf16[16,272,128]{2,1,0:T(8,128)(2,1)} %bitcast.11), calls=%async_computation | async-start | bytes 2228224 | tf_op jit(solution)/shard_map/all_to_all | solution.py:294
  66.7 9.3 %collective-permute-start.7 = (bf16[512,256]{1,0:T(8,128)(2,1)S(1)}, bf16[512,256]{1,0:T(8,128)(2,1)S(1)}, u32[]{:S(2)}, u32[]{:S(2)}) collective-permute-start(bf16[512,256]{1,0:T(8,128)(2,1)S(1)} %get-tuple-element.34), channel_id=1, source_target_pairs={{4,0},{8,4},{12,8},{16,12},{20,16},{24,20},{28,24},{32,28},{36,32}... | collective-permute-start | bytes 786440 | tf_op jit(solution)/shard_map/ppermute | solution.py:313
  68.0 8.9 %collective-permute-start.6 = (bf16[512,256]{1,0:T(8,128)(2,1)S(1)}, bf16[512,256]{1,0:T(8,128)(2,1)S(1)}, u32[]{:S(2)}, u32[]{:S(2)}) collective-permute-start(bf16[512,256]{1,0:T(8,128)(2,1)S(1)} %get-tuple-element.35), channel_id=1, source_target_pairs={{0,4},{4,8},{8,12},{12,16},{16,20},{20,24},{24,28},{28,32},{32,36}... | collective-permute-start | bytes 786440 | tf_op jit(solution)/shard_map/ppermute | solution.py:313
  76.1 0.7 copy-start.3
  76.9 0.7 copy-start.5
  93.1 6.6 %collective-permute-start.8 = (bf16[68,128]{1,0:T(8,128)(2,1)S(1)}, bf16[68,128]{1,0:T(8,128)(2,1)S(1)}, u32[]{:S(2)}, u32[]{:S(2)}) collective-permute-start(bf16[68,128]{1,0:T(8,128)(2,1)S(1)} %reduce_sum.25), channel_id=1, source_target_pairs={{0,2},{1,3},{2,0},{3,1},{4,6},{5,7},{6,4},{7,5},{8,10},{9,11},{10,... | collective-permute-start | bytes 52232 | tf_op jit(solution)/shard_map/ppermute | solution.py:304
  106.7 25.3 %copy-start.2 = (bf16[4,512,256]{2,1,0:T(8,128)(2,1)S(1)}, bf16[4,512,256]{2,1,0:T(8,128)(2,1)}, u32[]{:S(2)}) copy-start(bf16[4,512,256]{2,1,0:T(8,128)(2,1)} %copy-done.1) | copy-start | bytes 3145732
  106.7 25.3 %copy-start.4 = (bf16[512,256]{1,0:T(8,128)(2,1)S(1)}, bf16[512,256]{1,0:T(8,128)(2,1)}, u32[]{:S(2)}) copy-start(bf16[512,256]{1,0:T(8,128)(2,1)} %copy-done.3) | copy-start | bytes 786436
  106.7 25.3 %copy-start.6 = (bf16[512,256]{1,0:T(8,128)(2,1)S(1)}, bf16[512,256]{1,0:T(8,128)(2,1)}, u32[]{:S(2)}) copy-start(bf16[512,256]{1,0:T(8,128)(2,1)} %copy-done.5) | copy-start | bytes 786436
  125.4 12.5 %collective-permute-start.9 = (bf16[4352,128]{1,0:T(8,128)(2,1)S(1)}, bf16[4352,128]{1,0:T(8,128)(2,1)S(1)}, u32[]{:S(2)}, u32[]{:S(2)}) collective-permute-start(bf16[4352,128]{1,0:T(8,128)(2,1)S(1)} %bitcast.30), channel_id=1, source_target_pairs={{0,1},{1,0},{2,3},{3,2},{4,5},{5,4},{6,7},{7,6},{8,9},{9,8},{10,11... | collective-permute-start | bytes 3342344 | tf_op jit(solution)/shard_map/ppermute | solution.py:290
  134.7 0.8 copy-start

commit v2 on v1

--- a/solution.py
+++ b/solution.py
@@ -18,6 +18,10 @@
 
 def nn_dot(lhs, rhs):
     return jnp.dot(lhs, rhs, preferred_element_type=F32)
+
+
+def tn_dot(lhs, rhs):
+    return lax.dot_general(lhs, rhs, (((0,), (0,)), ((), ())), preferred_element_type=F32)
 
 
 def next_rows(value, period):
@@ -97,45 +101,48 @@
         window[layer, 16:272, 0:128] = previous_rows(wide, 16).astype(BF16)
         window[layer, 16:272, 128:256] = cells
         window[layer, 16:272, 256:384] = next_rows(wide, 16).astype(BF16)
-    total = None
-    for tap in range(9):
-        shift_x, shift_y = tap // 3, tap % 3
-        view = window[shift_x : shift_x + 4, 16 * shift_y : 16 * shift_y + 256, :]
-        term = nn_dot(view.reshape(1024, 384), weight_ref[tap])
-        total = term if total is None else total + term
-    sigma = 1.0 / (1.0 + jnp.exp(-total))
-    active = (total * sigma)[256:768].reshape(2, 8, 2, 16, 256)
-    active = active[0] + active[1]
-    active = (active[:, 0] + active[:, 1]).reshape(128, 256)
+    active = None
+    for layer in range(4):
+        total = None
+        for tap in range(9):
+            shift_x, shift_y = tap // 3, tap % 3
+            view = window[layer + shift_x, 16 * shift_y : 16 * shift_y + 256, :]
+            term = nn_dot(view, weight_ref[tap])
+            total = term if total is None else total + term
+        sigma = 1.0 / (1.0 + jnp.exp(-total))
+        slope = sigma * (1.0 + total * (1.0 - sigma))
+        spread = cot_ref[(layer + 1) // 2].astype(F32).reshape(8, 1, 16, 256) * 0.125
+        spread = jnp.broadcast_to(spread, (8, 2, 16, 256)).reshape(256, 256)
+        grads[layer, 0:16, :] = edge[:, :256]
+        grads[layer, 272:288, :] = edge[:, :256]
+        grads[layer, 16:272, :] = (spread * slope).astype(BF16)
+        if layer in (1, 2):
+            blocks = (total * sigma).reshape(8, 2, 16, 256)
+            blocks = blocks[:, 0] + blocks[:, 1]
+            active = blocks if active is None else active + blocks
+    active = active.reshape(128, 256)
     for part in range(2):
         lanes = slice(128 * part, 128 * part + 128)
         column[part] = active[:, lanes]
         pooled = column[part, pl.ds(0, 64, stride=2), :] + column[part, pl.ds(1, 64, stride=2), :]
         features_ref[:, lanes] = (pooled * 0.125).astype(BF16)
-    slope = sigma * (1.0 + total * (1.0 - sigma))
-    for layer in range(4):
-        spread = cot_ref[(layer + 1) // 2].astype(F32).reshape(8, 1, 16, 256) * 0.125
-        spread = jnp.broadcast_to(spread, (8, 2, 16, 256)).reshape(256, 256)
-        grads[layer, 0:16, :] = edge[:, :256]
-        grads[layer, 272:288, :] = edge[:, :256]
-        grads[layer, 16:272, :] = (spread * slope[256 * layer : 256 * layer + 256]).astype(BF16)
     core = core_ref[0]
     own = grads[1:3, 16:272, :].reshape(512, 256)
-    turned = own.T
     for tap in range(9):
         shift_x, shift_y = tap // 3, tap % 3
         view = window[1 + shift_x : 3 + shift_x, 16 * shift_y : 16 * shift_y + 256, :].reshape(512, 384)
-        terms = (nn_dot(turned, view) * 0.25).T.astype(BF16)
+        terms = (tn_dot(view, own) * 0.25).astype(BF16)
         keep_ref[tap] = jnp.where(core == 0, terms[:, :128], terms[:, 128:])
         send_ref[tap] = jnp.where(core == 0, terms[:, 128:], terms[:, :128])
-    total = None
-    for tap in range(9):
-        shift_x, shift_y = tap // 3, tap % 3
-        view = grads[2 - shift_x : 4 - shift_x, 32 - 16 * shift_y : 288 - 16 * shift_y, :].reshape(512, 256)
-        term = nt_dot(view, weight_ref[tap])
-        total = term if total is None else total + term
-    result = next_rows(total[:, 0:128], 16) + total[:, 128:256] + previous_rows(total[:, 256:384], 16)
-    grad_ref[...] = result.astype(BF16).reshape(2, 256, 128)
+    for layer in range(2):
+        total = None
+        for tap in range(9):
+            shift_x, shift_y = tap // 3, tap % 3
+            view = grads[layer + 2 - shift_x, 32 - 16 * shift_y : 288 - 16 * shift_y, :]
+            term = nt_dot(view, weight_ref[tap])
+            total = term if total is None else total + term
+        result = next_rows(total[:, 0:128], 16) + total[:, 128:256] + previous_rows(total[:, 256:384], 16)
+        grad_ref[layer] = result.astype(BF16)
 
 
 def block_b(core, left, cells, right, weight, cot):
@@ -160,21 +167,23 @@
 
 def kernel_a_kernel(core_ref, grad_ref, slope_ref, window_ref, pre_ref, keep_ref, send_ref):
     core = core_ref[0]
+    edge = jnp.zeros((16, 256), BF16)
     for layer in range(4):
         spread = grad_ref[layer // 2].astype(F32).reshape(16, 1, 16, 128) * 0.125
         spread = jnp.broadcast_to(spread, (16, 2, 16, 128)).reshape(512, 128)
         slope = slope_ref[layer].astype(F32)
-        pre_ref[layer, :, 0:128] = (spread * slope[:, 0:128]).astype(BF16)
-        pre_ref[layer, :, 128:256] = (spread * slope[:, 128:256]).astype(BF16)
-    turned = pre_ref[...].reshape(2048, 256).T
+        pre_ref[layer, 0:16, :] = edge
+        pre_ref[layer, 528:544, :] = edge
+        pre_ref[layer, 16:528, 0:128] = (spread * slope[:, 0:128]).astype(BF16)
+        pre_ref[layer, 16:528, 128:256] = (spread * slope[:, 128:256]).astype(BF16)
+    grads = pre_ref[:, 16:528, :].reshape(2048, 256)
     for tap in range(9):
         shift_x, shift_y = tap // 3, tap % 3
         view = window_ref[shift_x : shift_x + 4, 16 * shift_y : 16 * shift_y + 512, :].reshape(2048, 256)
-        terms = nn_dot(turned, view)
-        terms = (terms[:128] + pltpu.roll(terms[128:], 192, 1)) * 0.25
-        terms = terms.T.astype(BF16)
-        first = jnp.concatenate([terms[192:256], terms[0:32]])
-        second = terms[32:128]
+        terms = tn_dot(view, grads) * 0.25
+        even, odd = terms[:, :128], terms[:, 128:]
+        first = jnp.concatenate([even[192:256] + odd[0:64], even[0:32] + odd[64:96]]).astype(BF16)
+        second = (even[32:128] + odd[96:192]).astype(BF16)
         keep_ref[tap] = jnp.where(core == 0, first, second)
         send_ref[tap] = jnp.where(core == 0, second, first)
 
@@ -184,7 +193,7 @@
         kernel_a_kernel,
         in_specs=[SCALAR] + [WHOLE] * 3,
         out_shape=(
-            jax.ShapeDtypeStruct((4, 512, 256), BF16),
+            jax.ShapeDtypeStruct((4, 544, 256), BF16),
             jax.ShapeDtypeStruct((9, 96, 128), BF16),
             jax.ShapeDtypeStruct((9, 96, 128), BF16),
         ),
@@ -193,38 +202,38 @@
     )(core, grad, slope, window)
 
 
-def back_a_kernel(left_ref, cells_ref, right_ref, weight_ref, out_ref, grads):
-    edge = jnp.zeros((16, 256), BF16)
-    for layer in range(6):
-        grads[layer, 0:16, :] = edge
-        grads[layer, 528:544, :] = edge
-        if layer == 0:
-            grads[layer, 16:528, :] = left_ref[...]
-        elif layer == 5:
-            grads[layer, 16:528, :] = right_ref[...]
-        else:
-            grads[layer, 16:528, :] = cells_ref[layer - 1]
-    for half in range(2):
+def back_a_kernel(grads_ref, weight_ref, inner_ref, to_left_ref, to_right_ref):
+    for layer in range(-1, 5):
         total = None
         for tap in range(9):
             shift_x, shift_y = tap // 3, tap % 3
-            first = 2 * half + 2 - shift_x
-            view = grads[first : first + 2, 32 - 16 * shift_y : 544 - 16 * shift_y, :].reshape(1024, 256)
-            term = nt_dot(view, weight_ref[tap])
-            total = term if total is None else total + term
+            source = layer + 1 - shift_x
+            if 0 <= source < 4:
+                view = grads_ref[source, 32 - 16 * shift_y : 544 - 16 * shift_y, :]
+                term = nt_dot(view, weight_ref[tap])
+                total = term if total is None else total + term
         outer = total[:, 128:256]
         outer = jnp.where(low_lanes(outer.shape), previous_rows(outer, 16), next_rows(outer, 16))
-        out_ref[2 * half : 2 * half + 2] = (total[:, 0:128] + outer).astype(BF16).reshape(2, 512, 128)
-
-
-def back_a(left, cells, right, weight):
+        result = (total[:, 0:128] + outer).astype(BF16)
+        if layer == -1:
+            to_left_ref[...] = result
+        elif layer == 4:
+            to_right_ref[...] = result
+        else:
+            inner_ref[layer] = result
+
+
+def back_a(grads, weight):
     return pl.pallas_call(
         back_a_kernel,
-        out_shape=jax.ShapeDtypeStruct((4, 512, 128), BF16),
-        scratch_shapes=[pltpu.VMEM((6, 544, 256), BF16)],
-        compiler_params=pltpu.CompilerParams(vmem_limit_bytes=ROOM),
-        cost_estimate=pl.CostEstimate(flops=2 * 2048 * 2304 * 256, bytes_accessed=5 * 10**6, transcendentals=0),
-    )(left, cells, right, weight)
+        out_shape=(
+            jax.ShapeDtypeStruct((4, 512, 128), BF16),
+            jax.ShapeDtypeStruct((512, 128), BF16),
+            jax.ShapeDtypeStruct((512, 128), BF16),
+        ),
+        compiler_params=pltpu.CompilerParams(vmem_limit_bytes=ROOM),
+        cost_estimate=pl.CostEstimate(flops=2 * 2048 * 2304 * 256, bytes_accessed=4 * 10**6, transcendentals=0),
+    )(grads, weight)
 
 
 def paired_weight(weight):
@@ -281,9 +290,8 @@
 
 AXES = ("slab", "rep")
 ACROSS = [[((16 * x + 4 * y + z) * 4 + rep) for x in range(4) for y in range(4)] for z in range(4) for rep in range(4)]
-LINES = [[((4 * plane + z) * 4 + rep) for z in range(4)] for plane in range(16) for rep in range(4)]
+ALONG = [[((4 * plane + z) * 4 + 2 * far + core) for far in range(2) for z in range(4)] for plane in range(16) for core in range(2)]
 CORES = [(device, device ^ 1) for device in range(256)]
-FAR = [(device, device ^ 2) for device in range(256)]
 
 
 def other_core(value):
@@ -300,9 +308,7 @@
 
 def reduce_over_chips(blocks):
     part = total_of(blocks)
-    part = total_of(exchange(part.reshape(4, 68, 128), LINES))
-    part = (part.astype(F32) + lax.ppermute(part, AXES, FAR).astype(F32)).astype(BF16)
-    part = exchange(jnp.broadcast_to(part, (4, 68, 128)), LINES).reshape(272, 128)
+    part = total_of(exchange(jnp.broadcast_to(part, (8, 272, 128)), ALONG))
     return exchange(jnp.broadcast_to(part, (16, 272, 128)), ACROSS).reshape(4352, 128)
 
 
@@ -330,13 +336,16 @@
     other_b = other_core(send_b)
     grad_pre, keep_a, send_a = kernel_a(core, grad_pooled, slope_a, window)
     other_a = other_core(send_a)
-    grad_left, grad_right = neighbours(grad_pre[0], grad_pre[3])
+    inner, to_left, to_right = back_a(grad_pre, pair_weight)
+    from_left, from_right = neighbours(to_left, to_right)
     rows = merge(keep_a, other_a, keep_b, other_b)
     blocks = exchange(rows.reshape(16, 272, 128), ACROSS)
-    blocks, grad_left, grad_right = lax.optimization_barrier((blocks, grad_left, grad_right))
+    blocks, from_left, from_right = lax.optimization_barrier((blocks, from_left, from_right))
     mine = reduce_over_chips(blocks)
     away = other_core(mine)
-    grad_cubes = back_a(grad_left, grad_pre, grad_right, pair_weight)
+    first = (inner[:1].astype(F32) + from_left.astype(F32)).astype(BF16)
+    last = (inner[3:].astype(F32) + from_right.astype(F32)).astype(BF16)
+    grad_cubes = jnp.concatenate([first, inner[1:3], last])
     sum_a, sum_b = unpack(core, mine, away)
     return (
         features.reshape(1, 1, 8, 8, 256),

time: 141 us -> 130 us (0.922)
  starting transfers between devices: 53 us -> 26 us
  blocking collectives: 32.5 us -> 43.9 us
  waiting for transfers between devices: 18.6 us -> 29.7 us
  Pallas kernels: 25.8 us -> 20.6 us
  local copies, waits for them, and re-layouts: 9.18 us -> 6.1 us
  other arithmetic: 0.35 us -> 1.79 us
    ppermute x3, waiting for transfers between devices: 4.04 us -> 19 us  [neighbours(): lax.ppermute(to_left, 'slab', down)]
    all_to_all x1, starting transfers between devices: 19.8 us -> 6.81 us  [exchange(): lax.all_to_all(blocks, AXES, 0, 0, axis_index_groups=groups, tiled=True)]
    all_to_all x3 -> x2, blocking collectives: 32.5 us -> 43.9 us  [exchange(): lax.all_to_all(blocks, AXES, 0, 0, axis_index_groups=groups, tiled=True)]
    ppermute x3, starting transfers between devices: 13.7 us -> 8.85 us  [neighbours(): lax.ppermute(to_right, 'slab', up)]
    pallas_call x1, Pallas kernels: 11.6 us -> 6.66 us  [block_b(): pl.pallas_call(block_b_kernel, in_specs=[SCALAR] + [WHOLE] * 5, out_shape...]
    ppermute x3, starting transfers between devices: 11.2 us -> 6.5 us  [other_core(): return lax.ppermute(value, AXES, CORES)]
    ppermute x1 -> x0, starting transfers between devices: 4.3 us -> none  [reduce_over_chips(): lax.ppermute(part, AXES, FAR).astype(F32)]
    all_to_all x1, waiting for transfers between devices: 8.24 us -> 5.77 us  [exchange(): lax.all_to_all(blocks, AXES, 0, 0, axis_index_groups=groups, tiled=True)]
  transfers between devices with their start and end apart: 11 -> 10, of which waited for: 7 -> 9; matrix products, arithmetic and copies ran while one was open for 3% -> 2% of each run, Pallas kernels for 5% -> 5%
where the time goes in v2:
time: 130 us; the launch traced here: 129 us
  blocking collectives  43.9 us (34%)
  waiting for transfers between devices  29.7 us (23%)
  starting transfers between devices  26 us (20%)
  Pallas kernels  20.6 us (16%)
  local copies, waits for them, and re-layouts  6.1 us (5%)
  other arithmetic  1.79 us (1%)
    all_to_all x2, blocking collectives, exchange(): lax.all_to_all(blocks, AXES, 0, 0, axis_index_groups=groups, tiled=True)  43.9 us
    ppermute x3, waiting for transfers between devices, neighbours(): lax.ppermute(to_left, 'slab', down)  19 us
    ppermute x3, starting transfers between devices, neighbours(): lax.ppermute(to_right, 'slab', up)  8.85 us
    all_to_all x1, starting transfers between devices, exchange(): lax.all_to_all(blocks, AXES, 0, 0, axis_index_groups=groups, tiled=True)  6.81 us
    pallas_call x1, Pallas kernels, block_b(): pl.pallas_call(block_b_kernel, in_specs=[SCALAR] + [WHOLE] * 5, out_shape...  6.66 us
    ppermute x3, starting transfers between devices, other_core(): return lax.ppermute(value, AXES, CORES)  6.5 us
    all_to_all x1, waiting for transfers between devices, exchange(): lax.all_to_all(blocks, AXES, 0, 0, axis_index_groups=groups, tiled=True)  5.77 us
    pallas_call x1, Pallas kernels, kernel_a(): pl.pallas_call(kernel_a_kernel, in_specs=[SCALAR] + [WHOLE] * 3, out_shap...  4.22 us
  transfers between devices with their start and end apart: 10, of which 9 were waited for; matrix products, arithmetic and copies ran while one was open for 2% of the time, Pallas kernels for 5%

profile of v2, /device:TPU:1, one launch (start us, length us, event | category | flops | bytes accessed | tf_op | source)
XLA Modules:
  0.0 129.1 jit_solution(139730155527418857)
XLA Ops:
  0.7 1.2 fusion.2
  2.2 4.4 %collective-permute-start = (bf16[640,128]{1,0:T(8,128)(2,1)S(1)}, bf16[640,128]{1,0:T(8,128)(2,1)S(1)}, u32[]{:S(2)}, u32[]{:S(2)}) collective-permute-start(bf16[640,128]{1,0:T(8,128)(2,1)S(1)} %get-tuple-element.52), channel_id=1, source_target_pairs={{0,4},{4,8},{8,12},{12,16},{16,20},{20,24},{24,28},{28,32},{32,36}... | collective-permute-start | bytes 491528 | tf_op jit(solution)/shard_map/ppermute | solution.py:319
  6.6 1.3 %collective-permute-start.1 = (bf16[640,128]{1,0:T(8,128)(2,1)S(1)}, bf16[640,128]{1,0:T(8,128)(2,1)S(1)}, u32[]{:S(2)}, u32[]{:S(2)}) collective-permute-start(bf16[640,128]{1,0:T(8,128)(2,1)S(1)} %get-tuple-element.51), channel_id=1, source_target_pairs={{4,0},{8,4},{12,8},{16,12},{20,16},{24,20},{28,24},{32,28},{36,32}... | collective-permute-start | bytes 491528 | tf_op jit(solution)/shard_map/ppermute | solution.py:319
  7.9 0.5 reshape.51.cells_ref
  8.6 0.8 collective-permute-done
  9.4 8.0 %collective-permute-done.1 = bf16[640,128]{1,0:T(8,128)(2,1)S(1)} collective-permute-done((bf16[640,128]{1,0:T(8,128)(2,1)S(1)}, bf16[640,128]{1,0:T(8,128)(2,1)S(1)}, u32[]{:S(2)}, u32[]{:S(2)}) %collective-permute-start.1) | collective-permute-done | bytes 163872 | tf_op jit(solution)/shard_map/ppermute | solution.py:319
  17.4 3.4 %shard_map.75 = (bf16[6,544,256]{2,1,0:T(8,128)(2,1)}, bf16[4,512,256]{2,1,0:T(8,128)(2,1)S(1)}, bf16[2,256,128]{2,1,0:T(8,128)(2,1)S(1)}) custom-call(bf16[512,128]{1,0:T(8,128)(2,1)S(1)} %slice.71.left_ref, bf16[4,512,128]{2,1,0:T(8,128)(2,1)S(1)} %reshape.51.cells_ref, bf16[512,128]{1,0:T(8,128)(2,1)S(1)} %slice.72.right_ref, ...), custom_call_target="tpu_custom_call" | custom-call | flops 2415919104 | bytes 6000000 | tf_op jit(solution)/shard_map/pallas_call | solution.py:77
  20.9 2.2 %collective-permute-start.2 = (bf16[2,256,128]{2,1,0:T(8,128)(2,1)S(1)}, bf16[2,256,128]{2,1,0:T(8,128)(2,1)S(1)}, u32[]{:S(2)}, u32[]{:S(2)}) collective-permute-start(bf16[2,256,128]{2,1,0:T(8,128)(2,1)S(1)} %get-tuple-element.22.cells_ref), channel_id=1, source_target_pairs={{0,4},{4,8},{8,12},{12,16},{16,20},{20,24},{24,28},{28,32},{32,36}... | collective-permute-start | bytes 393224 | tf_op jit(solution)/shard_map/ppermute | solution.py:319
  23.1 1.3 %collective-permute-start.3 = (bf16[2,256,128]{2,1,0:T(8,128)(2,1)S(1)}, bf16[2,256,128]{2,1,0:T(8,128)(2,1)S(1)}, u32[]{:S(2)}, u32[]{:S(2)}) collective-permute-start(bf16[2,256,128]{2,1,0:T(8,128)(2,1)S(1)} %get-tuple-element.22.cells_ref), channel_id=1, source_target_pairs={{4,0},{8,4},{12,8},{16,12},{20,16},{24,20},{28,24},{32,28},{36,32}... | collective-permute-start | bytes 393224 | tf_op jit(solution)/shard_map/ppermute | solution.py:319
  24.6 0.8 collective-permute-done.2.left_ref
  25.4 7.1 %collective-permute-done.3.right_ref = bf16[2,256,128]{2,1,0:T(8,128)(2,1)S(1)} collective-permute-done((bf16[2,256,128]{2,1,0:T(8,128)(2,1)S(1)}, bf16[2,256,128]{2,1,0:T(8,128)(2,1)S(1)}, u32[]{:S(2)}, u32[]{:S(2)}) %collective-permute-start.3) | collective-permute-done | bytes 131104 | tf_op jit(solution)/shard_map/ppermute | solution.py:319
  32.5 6.7 %shard_map.76 = (bf16[64,256]{1,0:T(8,128)(2,1)}, bf16[9,384,128]{2,1,0:T(8,128)(2,1)S(1)}, bf16[9,384,128]{2,1,0:T(8,128)(2,1)S(1)}, bf16[2,256,128]{2,1,0:T(8,128)(2,1)S(1)}) custom-call(s32[1]{0:T(128)} %bitcast.core_ref, bf16[2,256,128]{2,1,0:T(8,128)(2,1)S(1)} %collective-permute-done.2.left_ref, bf16[2,256,128]{2,1,0:T(8,128)(2,1)S(1)} %get-tuple-element.22.cells_ref, ...), custom_call_target="tpu_custom_call" | custom-call | flops 3623878656 | bytes 5000000 | tf_op jit(solution)/shard_map/pallas_call | solution.py:149
  39.1 1.3 collective-permute-start.5
  40.4 4.2 %shard_map.77 = (bf16[4,544,256]{2,1,0:T(8,128)(2,1)S(1)}, bf16[9,96,128]{2,1,0:T(8,128)(2,1)S(1)}, bf16[9,96,128]{2,1,0:T(8,128)(2,1)S(1)}) custom-call(s32[1]{0:T(128)} %bitcast.core_ref, bf16[2,256,128]{2,1,0:T(8,128)(2,1)S(1)} %get-tuple-element.24.grad_ref, bf16[4,512,256]{2,1,0:T(8,128)(2,1)S(1)} %get-tuple-element.25.slope_ref, ...), custom_call_target="tpu_custom_call" | custom-call | flops 2415919104 | bytes 6000000 | tf_op jit(solution)/shard_map/pallas_call | solution.py:192
  44.7 1.0 copy-done
  45.7 1.5 %collective-permute-done.4.other_a_ref = bf16[9,96,128]{2,1,0:T(8,128)(2,1)S(1)} collective-permute-done((bf16[9,96,128]{2,1,0:T(8,128)(2,1)S(1)}, bf16[9,96,128]{2,1,0:T(8,128)(2,1)S(1)}, u32[]{:S(2)}, u32[]{:S(2)}) %collective-permute-start.4) | collective-permute-done | bytes 221216 | tf_op jit(solution)/shard_map/ppermute | solution.py:298
  47.1 1.2 shard_map.79
  48.4 6.8 %all-to-all-start = ((bf16[16,272,128]{2,1,0:T(8,128)(2,1)}), bf16[16,272,128]{2,1,0:T(8,128)(2,1)}, u32[]{:S(2)}, u32[]{:S(2)}) async-start(bf16[16,272,128]{2,1,0:T(8,128)(2,1)} %bitcast.11), calls=%async_computation | async-start | bytes 2228224 | tf_op jit(solution)/shard_map/all_to_all | solution.py:302
  55.2 1.2 copy-done.1
  56.4 2.6 %shard_map.78 = (bf16[4,512,128]{2,1,0:T(8,128)(2,1)S(1)}, bf16[512,128]{1,0:T(8,128)(2,1)S(1)}, bf16[512,128]{1,0:T(8,128)(2,1)S(1)}) custom-call(bf16[4,544,256]{2,1,0:T(8,128)(2,1)S(1)} %copy-done.1, bf16[9,256,256]{2,1,0:T(8,128)(2,1)S(1)} %maximum_maximum_fusion.weight_ref), custom_call_target="tpu_custom_call" | custom-call | flops 2415919104 | bytes 4000000 | tf_op jit(solution)/shard_map/pallas_call | solution.py:227
  59.1 2.3 %collective-permute-start.6 = (bf16[512,128]{1,0:T(8,128)(2,1)S(1)}, bf16[512,128]{1,0:T(8,128)(2,1)S(1)}, u32[]{:S(2)}, u32[]{:S(2)}) collective-permute-start(bf16[512,128]{1,0:T(8,128)(2,1)S(1)} %get-tuple-element.33), channel_id=1, source_target_pairs={{0,4},{4,8},{8,12},{12,16},{16,20},{20,24},{24,28},{28,32},{32,36}... | collective-permute-start | bytes 393224 | tf_op jit(solution)/shard_map/ppermute | solution.py:319
  61.4 1.3 %collective-permute-start.7 = (bf16[512,128]{1,0:T(8,128)(2,1)S(1)}, bf16[512,128]{1,0:T(8,128)(2,1)S(1)}, u32[]{:S(2)}, u32[]{:S(2)}) collective-permute-start(bf16[512,128]{1,0:T(8,128)(2,1)S(1)} %get-tuple-element.34), channel_id=1, source_target_pairs={{4,0},{8,4},{12,8},{16,12},{20,16},{24,20},{28,24},{32,28},{36,32}... | collective-permute-start | bytes 393224 | tf_op jit(solution)/shard_map/ppermute | solution.py:319
  62.7 1.1 collective-permute-done.6
  63.8 3.9 %collective-permute-done.7 = bf16[512,128]{1,0:T(8,128)(2,1)S(1)} collective-permute-done((bf16[512,128]{1,0:T(8,128)(2,1)S(1)}, bf16[512,128]{1,0:T(8,128)(2,1)S(1)}, u32[]{:S(2)}, u32[]{:S(2)}) %collective-permute-start.7) | collective-permute-done | bytes 131104 | tf_op jit(solution)/shard_map/ppermute | solution.py:319
  67.7 5.8 %all-to-all-done = bf16[16,272,128]{2,1,0:T(8,128)(2,1)} async-done(((bf16[16,272,128]{2,1,0:T(8,128)(2,1)}), bf16[16,272,128]{2,1,0:T(8,128)(2,1)}, u32[]{:S(2)}, u32[]{:S(2)}) %all-to-all-start) | async-done | bytes 1114144 | tf_op jit(solution)/shard_map/all_to_all | solution.py:302
  73.5 1.4 %reduce_sum.24 = bf16[272,128]{1,0:T(8,128)(2,1)S(1)} reduce(bf16[16,272,128]{2,1,0:T(8,128)(2,1)} %all-to-all-done, bf16[]{:T(256)} %constant.21.clone.1), dimensions={0}, to_apply=%region_0.1 | reduce | flops 522240 | bytes 1183746 | tf_op jit(solution)/shard_map/reduce_sum | solution.py:306
  75.0 23.4 %all_to_all.15 = bf16[8,272,128]{2,1,0:T(8,128)(2,1)S(1)} all-to-all(bf16[8,272,128]{2,1,0:T(8,128)(2,1)S(1)} %broadcast_in_dim.33), channel_id=1, replica_groups={{0,4,8,12,2,6,10,14},{1,5,9,13,3,7,11,15},{16,20,24,28,18,22,26,30},{17..., dimensions={0} | all-to-all | bytes 1114112 | tf_op jit(solution)/shard_map/all_to_all | solution.py:302
  98.6 20.5 %all_to_all.16 = bf16[16,272,128]{2,1,0:T(8,128)(2,1)S(1)} all-to-all(bf16[16,272,128]{2,1,0:T(8,128)(2,1)S(1)} %broadcast_in_dim.34), channel_id=1, replica_groups={{0,16,32,48,64,80,96,112,128,144,160,176,192,208,224,240},{1,17,33,49,6..., dimensions={0} | all-to-all | bytes 2228224 | tf_op jit(solution)/shard_map/all_to_all | solution.py:302
  119.1 5.2 %collective-permute-start.8 = (bf16[4352,128]{1,0:T(8,128)(2,1)S(1)}, bf16[4352,128]{1,0:T(8,128)(2,1)S(1)}, u32[]{:S(2)}, u32[]{:S(2)}) collective-permute-start(bf16[4352,128]{1,0:T(8,128)(2,1)S(1)} %bitcast.32), channel_id=1, source_target_pairs={{0,1},{1,0},{2,3},{3,2},{4,5},{5,4},{6,7},{7,6},{8,9},{9,8},{10,11... | collective-permute-start | bytes 3342344 | tf_op jit(solution)/shard_map/ppermute | solution.py:298
  124.5 1.4 %reshape.57 = bf16[1,4,32,32,64]{4,3,2,1,0:T(8,128)(2,1)} reshape(bf16[4,512,128]{2,1,0:T(8,128)(2,1)S(1)} %pad_maximum_fusion) | data formatting | bytes 1048576 | tf_op jit(solution)/shard_map/reshape | solution.py:352
  125.8 0.8 collective-permute-done.8.away_ref
  126.7 2.4 %shard_map.80 = (f32[9,2,96,128]{3,2,1,0:T(8,128)}, f32[9,384,256]{2,1,0:T(8,128)}) custom-call(s32[1]{0:T(128)} %bitcast.core_ref, bf16[4352,128]{1,0:T(8,128)(2,1)S(1)} %bitcast.33, bf16[4352,128]{1,0:T(8,128)(2,1)S(1)} %collective-permute-done.8.away_ref), custom_call_target="tpu_custom_call" | custom-call | bytes 7000000 | tf_op jit(solution)/shard_map/pallas_call | solution.py:279
  (32 shorter events, 1.3 us)
Async XLA Ops:
  0.6 7.3 %copy-start.2 = (bf16[1,4,32,32,64]{4,3,2,1,0:T(8,128)(2,1)S(1)}, bf16[1,4,32,32,64]{4,3,2,1,0:T(8,128)(2,1)}, u32[]{:S(2)}) copy-start(bf16[1,4,32,32,64]{4,3,2,1,0:T(8,128)(2,1)} %param.4) | copy-start | bytes 1572868
  0.6 1.5 %copy-start.4 = (bf16[1,1,8,8,256]{4,3,2,1,0:T(8,128)(2,1)S(1)}, bf16[1,1,8,8,256]{4,3,2,1,0:T(8,128)(2,1)}, u32[]{:S(2)}) copy-start(bf16[1,1,8,8,256]{4,3,2,1,0:T(8,128)(2,1)} %param.7) | copy-start | bytes 98308
  1.8 6.6 %copy-start.3 = (bf16[3,3,3,64,128]{4,3,2,1,0:T(8,128)(2,1)S(1)}, bf16[3,3,3,64,128]{4,3,2,1,0:T(8,128)(2,1)}, u32[]{:S(2)}) copy-start(bf16[3,3,3,64,128]{4,3,2,1,0:T(8,128)(2,1)} %param.5) | copy-start | bytes 1327108
  2.2 7.2 %collective-permute-start = (bf16[640,128]{1,0:T(8,128)(2,1)S(1)}, bf16[640,128]{1,0:T(8,128)(2,1)S(1)}, u32[]{:S(2)}, u32[]{:S(2)}) collective-permute-start(bf16[640,128]{1,0:T(8,128)(2,1)S(1)} %get-tuple-element.52), channel_id=1, source_target_pairs={{0,4},{4,8},{8,12},{12,16},{16,20},{20,24},{24,28},{28,32},{32,36}... | collective-permute-start | bytes 491528 | tf_op jit(solution)/shard_map/ppermute | solution.py:319
  6.6 10.9 %collective-permute-start.1 = (bf16[640,128]{1,0:T(8,128)(2,1)S(1)}, bf16[640,128]{1,0:T(8,128)(2,1)S(1)}, u32[]{:S(2)}, u32[]{:S(2)}) collective-permute-start(bf16[640,128]{1,0:T(8,128)(2,1)S(1)} %get-tuple-element.51), channel_id=1, source_target_pairs={{4,0},{8,4},{12,8},{16,12},{20,16},{24,20},{28,24},{32,28},{36,32}... | collective-permute-start | bytes 491528 | tf_op jit(solution)/shard_map/ppermute | solution.py:319
  20.9 4.5 %collective-permute-start.2 = (bf16[2,256,128]{2,1,0:T(8,128)(2,1)S(1)}, bf16[2,256,128]{2,1,0:T(8,128)(2,1)S(1)}, u32[]{:S(2)}, u32[]{:S(2)}) collective-permute-start(bf16[2,256,128]{2,1,0:T(8,128)(2,1)S(1)} %get-tuple-element.22.cells_ref), channel_id=1, source_target_pairs={{0,4},{4,8},{8,12},{12,16},{16,20},{20,24},{24,28},{28,32},{32,36}... | collective-permute-start | bytes 393224 | tf_op jit(solution)/shard_map/ppermute | solution.py:319
  23.1 9.4 %collective-permute-start.3 = (bf16[2,256,128]{2,1,0:T(8,128)(2,1)S(1)}, bf16[2,256,128]{2,1,0:T(8,128)(2,1)S(1)}, u32[]{:S(2)}, u32[]{:S(2)}) collective-permute-start(bf16[2,256,128]{2,1,0:T(8,128)(2,1)S(1)} %get-tuple-element.22.cells_ref), channel_id=1, source_target_pairs={{4,0},{8,4},{12,8},{16,12},{20,16},{24,20},{28,24},{32,28},{36,32}... | collective-permute-start | bytes 393224 | tf_op jit(solution)/shard_map/ppermute | solution.py:319
  39.1 8.0 %collective-permute-start.5 = (bf16[9,384,128]{2,1,0:T(8,128)(2,1)S(1)}, bf16[9,384,128]{2,1,0:T(8,128)(2,1)S(1)}, u32[]{:S(2)}, u32[]{:S(2)}) collective-permute-start(bf16[9,384,128]{2,1,0:T(8,128)(2,1)S(1)} %get-tuple-element.32), channel_id=1, source_target_pairs={{0,1},{1,0},{2,3},{3,2},{4,5},{5,4},{6,7},{7,6},{8,9},{9,8},{10,11... | collective-permute-start | bytes 2654216 | tf_op jit(solution)/shard_map/ppermute | solution.py:298
  44.7 1.0 copy-start
  45.6 1.5 %collective-permute-start.4 = (bf16[9,96,128]{2,1,0:T(8,128)(2,1)S(1)}, bf16[9,96,128]{2,1,0:T(8,128)(2,1)S(1)}, u32[]{:S(2)}, u32[]{:S(2)}) collective-permute-start(bf16[9,96,128]{2,1,0:T(8,128)(2,1)S(1)} %get-tuple-element.30), channel_id=1, source_target_pairs={{0,1},{1,0},{2,3},{3,2},{4,5},{5,4},{6,7},{7,6},{8,9},{9,8},{10,11... | collective-permute-start | bytes 663560 | tf_op jit(solution)/shard_map/ppermute | solution.py:298
  48.4 25.1 %all-to-all-start = ((bf16[16,272,128]{2,1,0:T(8,128)(2,1)}), bf16[16,272,128]{2,1,0:T(8,128)(2,1)}, u32[]{:S(2)}, u32[]{:S(2)}) async-start(bf16[16,272,128]{2,1,0:T(8,128)(2,1)} %bitcast.11), calls=%async_computation | async-start | bytes 2228224 | tf_op jit(solution)/shard_map/all_to_all | solution.py:302
  55.2 1.3 copy-start.1
  59.1 4.7 %collective-permute-start.6 = (bf16[512,128]{1,0:T(8,128)(2,1)S(1)}, bf16[512,128]{1,0:T(8,128)(2,1)S(1)}, u32[]{:S(2)}, u32[]{:S(2)}) collective-permute-start(bf16[512,128]{1,0:T(8,128)(2,1)S(1)} %get-tuple-element.33), channel_id=1, source_target_pairs={{0,4},{4,8},{8,12},{12,16},{16,20},{20,24},{24,28},{28,32},{32,36}... | collective-permute-start | bytes 393224 | tf_op jit(solution)/shard_map/ppermute | solution.py:319
  61.4 6.3 %collective-permute-start.7 = (bf16[512,128]{1,0:T(8,128)(2,1)S(1)}, bf16[512,128]{1,0:T(8,128)(2,1)S(1)}, u32[]{:S(2)}, u32[]{:S(2)}) collective-permute-start(bf16[512,128]{1,0:T(8,128)(2,1)S(1)} %get-tuple-element.34), channel_id=1, source_target_pairs={{4,0},{8,4},{12,8},{16,12},{20,16},{24,20},{28,24},{32,28},{36,32}... | collective-permute-start | bytes 393224 | tf_op jit(solution)/shard_map/ppermute | solution.py:319
  119.1 7.6 %collective-permute-start.8 = (bf16[4352,128]{1,0:T(8,128)(2,1)S(1)}, bf16[4352,128]{1,0:T(8,128)(2,1)S(1)}, u32[]{:S(2)}, u32[]{:S(2)}) collective-permute-start(bf16[4352,128]{1,0:T(8,128)(2,1)S(1)} %bitcast.32), channel_id=1, source_target_pairs={{0,1},{1,0},{2,3},{3,2},{4,5},{5,4},{6,7},{7,6},{8,9},{9,8},{10,11... | collective-permute-start | bytes 3342344 | tf_op jit(solution)/shard_map/ppermute | solution.py:298

commit v3 on v2

--- a/solution.py
+++ b/solution.py
@@ -7,7 +7,7 @@
 
 BF16 = jnp.bfloat16
 F32 = jnp.float32
-ROOM = 50 * 1024 * 1024
+ROOM = 16 * 1024 * 1024
 SCALAR = pl.BlockSpec(memory_space=pltpu.SMEM)
 WHOLE = pl.BlockSpec(memory_space=pltpu.VMEM)
 
@@ -263,22 +263,26 @@
 
 
 def unpack_kernel(core_ref, mine_ref, away_ref, sum_a_ref, sum_b_ref):
-    core = core_ref[0]
-    for tap in range(9):
-        rows = slice(96 * tap, 96 * tap + 96)
-        mine, away = mine_ref[rows].astype(F32), away_ref[rows].astype(F32)
-        sum_a_ref[tap, 0] = jnp.where(core == 0, mine, away)
-        sum_a_ref[tap, 1] = jnp.where(core == 0, away, mine)
-        rows = slice(864 + 384 * tap, 1248 + 384 * tap)
-        mine, away = mine_ref[rows].astype(F32), away_ref[rows].astype(F32)
-        sum_b_ref[tap, :, 0:128] = jnp.where(core == 0, mine, away)
-        sum_b_ref[tap, :, 128:256] = jnp.where(core == 0, away, mine)
+    core, tap = core_ref[0], pl.program_id(0)
+    rows = pl.ds(pl.multiple_of(96 * tap, 32), 96)
+    mine, away = mine_ref[rows].astype(F32), away_ref[rows].astype(F32)
+    sum_a_ref[0, 0] = jnp.where(core == 0, mine, away)
+    sum_a_ref[0, 1] = jnp.where(core == 0, away, mine)
+    rows = pl.ds(pl.multiple_of(864 + 384 * tap, 32), 384)
+    mine, away = mine_ref[rows].astype(F32), away_ref[rows].astype(F32)
+    sum_b_ref[0, :, 0:128] = jnp.where(core == 0, mine, away)
+    sum_b_ref[0, :, 128:256] = jnp.where(core == 0, away, mine)
 
 
 def unpack(core, mine, away):
     return pl.pallas_call(
         unpack_kernel,
-        in_specs=[SCALAR] + [WHOLE] * 2,
+        grid=(9,),
+        in_specs=[SCALAR, WHOLE, WHOLE],
+        out_specs=(
+            pl.BlockSpec((1, 2, 96, 128), lambda tap: (tap, 0, 0, 0)),
+            pl.BlockSpec((1, 384, 256), lambda tap: (tap, 0, 0)),
+        ),
         out_shape=(
             jax.ShapeDtypeStruct((9, 2, 96, 128), F32),
             jax.ShapeDtypeStruct((9, 384, 256), F32),
@@ -306,10 +310,12 @@
     return jnp.sum(blocks.astype(F32), axis=0).astype(BF16)
 
 
-def reduce_over_chips(blocks):
-    part = total_of(blocks)
-    part = total_of(exchange(jnp.broadcast_to(part, (8, 272, 128)), ALONG))
-    return exchange(jnp.broadcast_to(part, (16, 272, 128)), ACROSS).reshape(4352, 128)
+def reduce_over_chips(rows, beside):
+    part = total_of(exchange(rows.reshape(16, 272, 128), ACROSS))
+    blocks = exchange(jnp.broadcast_to(part, (8, 272, 128)), ALONG)
+    blocks, beside = lax.optimization_barrier((blocks, beside))
+    part = jnp.broadcast_to(total_of(blocks), (16, 272, 128))
+    return exchange(part, ACROSS).reshape(4352, 128), beside
 
 
 def neighbours(to_left, to_right):
@@ -339,9 +345,7 @@
     inner, to_left, to_right = back_a(grad_pre, pair_weight)
     from_left, from_right = neighbours(to_left, to_right)
     rows = merge(keep_a, other_a, keep_b, other_b)
-    blocks = exchange(rows.reshape(16, 272, 128), ACROSS)
-    blocks, from_left, from_right = lax.optimization_barrier((blocks, from_left, from_right))
-    mine = reduce_over_chips(blocks)
+    mine, (from_left, from_right) = reduce_over_chips(rows, (from_left, from_right))
     away = other_core(mine)
     first = (inner[:1].astype(F32) + from_left.astype(F32)).astype(BF16)
     last = (inner[3:].astype(F32) + from_right.astype(F32)).astype(BF16)

time: 130 us -> 132 us (1.015)
  local copies, waits for them, and re-layouts: 6.1 us -> 12.8 us
  waiting for transfers between devices: 29.7 us -> 25.2 us
  starting transfers between devices: 26 us -> 30 us
  blocking collectives: 43.9 us -> 42.1 us
    all_to_all x1, waiting for transfers between devices: 5.77 us -> 0.01 us  [exchange(): lax.all_to_all(blocks, AXES, 0, 0, axis_index_groups=groups, tiled=True)]
    all_to_all x1, starting transfers between devices: 6.81 us -> 10.3 us  [exchange(): lax.all_to_all(blocks, AXES, 0, 0, axis_index_groups=groups, tiled=True)]
    unnamed x11 -> x25, local copies, waits for them, and re-layouts: 2.27 us -> 5.11 us
    ppermute x3, waiting for transfers between devices: 2.67 us -> 4.66 us  [neighbours(): lax.ppermute(to_right, 'slab', up)]
    all_to_all x2, blocking collectives: 43.9 us -> 42.1 us  [exchange(): lax.all_to_all(blocks, AXES, 0, 0, axis_index_groups=groups, tiled=True)]
    pallas_call x1, Pallas kernels: 2.44 us -> 3.95 us  [unpack(): pl.pallas_call(unpack_kernel, grid=(9,), in_specs=[SCALAR, WHOLE, WHOLE],...]
    slice x2, local copies, waits for them, and re-layouts: 0.01 us -> 1.48 us  [shards(): side[512:576]]
    pallas_call x1, Pallas kernels: 4.22 us -> 2.79 us  [kernel_a(): pl.pallas_call(kernel_a_kernel, in_specs=[SCALAR] + [WHOLE] * 3, out_shap...]
  transfers between devices with their start and end apart: 10 -> 10, of which waited for: 9 -> 7; matrix products, arithmetic and copies ran while one was open for 2% -> 4% of each run, Pallas kernels for 5% -> 4%
where the time goes in v3:
time: 132 us; the launch traced here: 131 us
  blocking collectives  42.1 us (32%)
  starting transfers between devices  30 us (23%)
  waiting for transfers between devices  25.2 us (19%)
  Pallas kernels  19.9 us (15%)
  local copies, waits for them, and re-layouts  12.8 us (10%)
    all_to_all x2, blocking collectives, exchange(): lax.all_to_all(blocks, AXES, 0, 0, axis_index_groups=groups, tiled=True)  42.1 us
    ppermute x3, waiting for transfers between devices, neighbours(): lax.ppermute(to_left, 'slab', down)  18.3 us
    all_to_all x1, starting transfers between devices, exchange(): lax.all_to_all(blocks, AXES, 0, 0, axis_index_groups=groups, tiled=True)  10.3 us
    ppermute x3, starting transfers between devices, neighbours(): lax.ppermute(to_right, 'slab', up)  9.93 us
    pallas_call x1, Pallas kernels, block_b(): pl.pallas_call(block_b_kernel, in_specs=[SCALAR] + [WHOLE] * 5, out_shape...  6.24 us
    ppermute x3, starting transfers between devices, other_core(): return lax.ppermute(value, AXES, CORES)  5.82 us
    unnamed x25, local copies, waits for them, and re-layouts  5.11 us
    ppermute x3, waiting for transfers between devices, neighbours(): lax.ppermute(to_right, 'slab', up)  4.66 us
  transfers between devices with their start and end apart: 10, of which 7 were waited for; matrix products, arithmetic and copies ran while one was open for 4% of the time, Pallas kernels for 4%

profile of v3, /device:TPU:1, one launch (start us, length us, event | category | flops | bytes accessed | tf_op | source)
XLA Modules:
  0.0 131.5 jit_solution(9646723328680739852)
XLA Ops:
  0.7 1.2 fusion.2
  2.2 4.4 %collective-permute-start = (bf16[640,128]{1,0:T(8,128)(2,1)S(1)}, bf16[640,128]{1,0:T(8,128)(2,1)S(1)}, u32[]{:S(2)}, u32[]{:S(2)}) collective-permute-start(bf16[640,128]{1,0:T(8,128)(2,1)S(1)} %get-tuple-element.52), channel_id=1, source_target_pairs={{0,4},{4,8},{8,12},{12,16},{16,20},{20,24},{24,28},{28,32},{32,36}... | collective-permute-start | bytes 491528 | tf_op jit(solution)/shard_map/ppermute | solution.py:325
  6.6 1.3 collective-permute-start.1
  8.6 0.8 collective-permute-done
  9.4 8.0 %collective-permute-done.1 = bf16[640,128]{1,0:T(8,128)(2,1)S(1)} collective-permute-done((bf16[640,128]{1,0:T(8,128)(2,1)S(1)}, bf16[640,128]{1,0:T(8,128)(2,1)S(1)}, u32[]{:S(2)}, u32[]{:S(2)}) %collective-permute-start.1) | collective-permute-done | bytes 163872 | tf_op jit(solution)/shard_map/ppermute | solution.py:325
  18.1 4.0 %shard_map.75 = (bf16[6,544,256]{2,1,0:T(8,128)(2,1)S(1)}, bf16[4,512,256]{2,1,0:T(8,128)(2,1)S(1)}, bf16[2,256,128]{2,1,0:T(8,128)(2,1)}) custom-call(bf16[512,128]{1,0:T(8,128)(2,1)S(1)} %slice.71.left_ref, bf16[4,512,128]{2,1,0:T(8,128)(2,1)S(1)} %reshape.51.cells_ref, bf16[512,128]{1,0:T(8,128)(2,1)S(1)} %slice.72.right_ref, ...), custom_call_target="tpu_custom_call" | custom-call | flops 2415919104 | bytes 6000000 | tf_op jit(solution)/shard_map/pallas_call | solution.py:77
  22.2 1.2 copy-done.1
  23.4 1.0 copy-done.5
  24.3 2.2 %collective-permute-start.2 = (bf16[2,256,128]{2,1,0:T(8,128)(2,1)}, bf16[2,256,128]{2,1,0:T(8,128)(2,1)S(1)}, u32[]{:S(2)}, u32[]{:S(2)}) collective-permute-start(bf16[2,256,128]{2,1,0:T(8,128)(2,1)} %get-tuple-element.22.cells_ref), channel_id=1, source_target_pairs={{0,4},{4,8},{8,12},{12,16},{16,20},{20,24},{24,28},{28,32},{32,36}... | collective-permute-start | bytes 393224 | tf_op jit(solution)/shard_map/ppermute | solution.py:325
  26.5 1.3 collective-permute-start.3
  29.3 0.8 broadcast_in_dim.28
  30.1 1.0 reshape.54.cot_ref
  31.1 5.0 %collective-permute-done.3.right_ref = bf16[2,256,128]{2,1,0:T(8,128)(2,1)S(1)} collective-permute-done((bf16[2,256,128]{2,1,0:T(8,128)(2,1)}, bf16[2,256,128]{2,1,0:T(8,128)(2,1)S(1)}, u32[]{:S(2)}, u32[]{:S(2)}) %collective-permute-start.3) | collective-permute-done | bytes 131104 | tf_op jit(solution)/shard_map/ppermute | solution.py:325
  36.2 6.2 %shard_map.76 = (bf16[64,256]{1,0:T(8,128)(2,1)}, bf16[9,384,128]{2,1,0:T(8,128)(2,1)S(1)}, bf16[9,384,128]{2,1,0:T(8,128)(2,1)S(1)}, bf16[2,256,128]{2,1,0:T(8,128)(2,1)S(1)}) custom-call(s32[1]{0:T(128)} %bitcast.core_ref, bf16[2,256,128]{2,1,0:T(8,128)(2,1)S(1)} %collective-permute-done.2.left_ref, bf16[2,256,128]{2,1,0:T(8,128)(2,1)} %get-tuple-element.22.cells_ref, ...), custom_call_target="tpu_custom_call" | custom-call | flops 3623878656 | bytes 5000000 | tf_op jit(solution)/shard_map/pallas_call | solution.py:149
  42.4 1.3 collective-permute-start.5
  43.7 2.8 %shard_map.77 = (bf16[4,544,256]{2,1,0:T(8,128)(2,1)S(1)}, bf16[9,96,128]{2,1,0:T(8,128)(2,1)S(1)}, bf16[9,96,128]{2,1,0:T(8,128)(2,1)S(1)}) custom-call(s32[1]{0:T(128)} %bitcast.core_ref, bf16[2,256,128]{2,1,0:T(8,128)(2,1)S(1)} %get-tuple-element.24.grad_ref, bf16[4,512,256]{2,1,0:T(8,128)(2,1)S(1)} %copy-done.6, bf16[6,544,256]{2,1,0:T(8,128)(2,1)S(1)} %copy-done.2), custom_call_target="tpu_custom_call" | custom-call | flops 2415919104 | bytes 6000000 | tf_op jit(solution)/shard_map/pallas_call | solution.py:192
  46.5 1.0 copy-done.3
  47.5 1.4 %collective-permute-done.4.other_a_ref = bf16[9,96,128]{2,1,0:T(8,128)(2,1)S(1)} collective-permute-done((bf16[9,96,128]{2,1,0:T(8,128)(2,1)S(1)}, bf16[9,96,128]{2,1,0:T(8,128)(2,1)S(1)}, u32[]{:S(2)}, u32[]{:S(2)}) %collective-permute-start.4) | collective-permute-done | bytes 221216 | tf_op jit(solution)/shard_map/ppermute | solution.py:302
  49.2 23.9 %all_to_all.15 = bf16[16,272,128]{2,1,0:T(8,128)(2,1)S(1)} all-to-all(bf16[16,272,128]{2,1,0:T(8,128)(2,1)S(1)} %bitcast.34), channel_id=1, replica_groups={{0,16,32,48,64,80,96,112,128,144,160,176,192,208,224,240},{1,17,33,49,6..., dimensions={0} | all-to-all | bytes 2228224 | tf_op jit(solution)/shard_map/all_to_all | solution.py:306
  73.2 0.9 broadcast_in_dim.29
  74.1 10.3 %all-to-all-start.1 = ((bf16[8,272,128]{2,1,0:T(8,128)(2,1)}), bf16[8,272,128]{2,1,0:T(8,128)(2,1)S(1)}, u32[]{:S(2)}, u32[]{:S(2)}) async-start(bf16[8,272,128]{2,1,0:T(8,128)(2,1)} %broadcast_in_dim.29), calls=%async_computation.1 | async-start | bytes 1114112 | tf_op jit(solution)/shard_map/all_to_all | solution.py:306
  84.5 1.2 copy-done.4
  85.7 2.6 %shard_map.78 = (bf16[4,512,128]{2,1,0:T(8,128)(2,1)S(1)}, bf16[512,128]{1,0:T(8,128)(2,1)S(1)}, bf16[512,128]{1,0:T(8,128)(2,1)S(1)}) custom-call(bf16[4,544,256]{2,1,0:T(8,128)(2,1)S(1)} %copy-done.4, bf16[9,256,256]{2,1,0:T(8,128)(2,1)S(1)} %maximum_maximum_fusion.weight_ref), custom_call_target="tpu_custom_call" | custom-call | flops 2415919104 | bytes 4000000 | tf_op jit(solution)/shard_map/pallas_call | solution.py:227
  88.4 3.4 %collective-permute-start.6 = (bf16[512,128]{1,0:T(8,128)(2,1)S(1)}, bf16[512,128]{1,0:T(8,128)(2,1)S(1)}, u32[]{:S(2)}, u32[]{:S(2)}) collective-permute-start(bf16[512,128]{1,0:T(8,128)(2,1)S(1)} %get-tuple-element.33), channel_id=1, source_target_pairs={{0,4},{4,8},{8,12},{12,16},{16,20},{20,24},{24,28},{28,32},{32,36}... | collective-permute-start | bytes 393224 | tf_op jit(solution)/shard_map/ppermute | solution.py:325
  91.7 1.3 collective-permute-start.7
  93.0 3.9 %collective-permute-done.6 = bf16[512,128]{1,0:T(8,128)(2,1)S(1)} collective-permute-done((bf16[512,128]{1,0:T(8,128)(2,1)S(1)}, bf16[512,128]{1,0:T(8,128)(2,1)S(1)}, u32[]{:S(2)}, u32[]{:S(2)}) %collective-permute-start.6) | collective-permute-done | bytes 131104 | tf_op jit(solution)/shard_map/ppermute | solution.py:325
  96.9 5.2 %collective-permute-done.7 = bf16[512,128]{1,0:T(8,128)(2,1)S(1)} collective-permute-done((bf16[512,128]{1,0:T(8,128)(2,1)S(1)}, bf16[512,128]{1,0:T(8,128)(2,1)S(1)}, u32[]{:S(2)}, u32[]{:S(2)}) %collective-permute-start.7) | collective-permute-done | bytes 131104 | tf_op jit(solution)/shard_map/ppermute | solution.py:325
  102.4 18.2 %all_to_all.16 = bf16[16,272,128]{2,1,0:T(8,128)(2,1)S(1)} all-to-all(bf16[16,272,128]{2,1,0:T(8,128)(2,1)S(1)} %broadcast_in_dim.34), channel_id=1, replica_groups={{0,16,32,48,64,80,96,112,128,144,160,176,192,208,224,240},{1,17,33,49,6..., dimensions={0} | all-to-all | bytes 2228224 | tf_op jit(solution)/shard_map/all_to_all | solution.py:306
  120.6 4.5 %collective-permute-start.8 = (bf16[4352,128]{1,0:T(8,128)(2,1)S(1)}, bf16[4352,128]{1,0:T(8,128)(2,1)S(1)}, u32[]{:S(2)}, u32[]{:S(2)}) collective-permute-start(bf16[4352,128]{1,0:T(8,128)(2,1)S(1)} %bitcast.32), channel_id=1, source_target_pairs={{0,1},{1,0},{2,3},{3,2},{4,5},{5,4},{6,7},{7,6},{8,9},{9,8},{10,11... | collective-permute-start | bytes 3342344 | tf_op jit(solution)/shard_map/ppermute | solution.py:302
  125.3 1.4 %reshape.57 = bf16[1,4,32,32,64]{4,3,2,1,0:T(8,128)(2,1)} reshape(bf16[4,512,128]{2,1,0:T(8,128)(2,1)S(1)} %pad_maximum_fusion) | data formatting | bytes 1048576 | tf_op jit(solution)/shard_map/reshape | solution.py:356
  126.7 0.8 collective-permute-done.8.away_ref
  127.5 3.9 %shard_map.80 = (f32[9,2,96,128]{3,2,1,0:T(8,128)}, f32[9,384,256]{2,1,0:T(8,128)}) custom-call(s32[1]{0:T(128)} %bitcast.core_ref, bf16[4352,128]{1,0:T(8,128)(2,1)S(1)} %bitcast.33, bf16[4352,128]{1,0:T(8,128)(2,1)S(1)} %collective-permute-done.8.away_ref), custom_call_target="tpu_custom_call" | custom-call | bytes 7000000 | tf_op jit(solution)/shard_map/pallas_call | solution.py:278
  (46 shorter events, 4.1 us)
Async XLA Ops:
  0.6 7.3 %copy-start.7 = (bf16[1,4,32,32,64]{4,3,2,1,0:T(8,128)(2,1)S(1)}, bf16[1,4,32,32,64]{4,3,2,1,0:T(8,128)(2,1)}, u32[]{:S(2)}) copy-start(bf16[1,4,32,32,64]{4,3,2,1,0:T(8,128)(2,1)} %param.4) | copy-start | bytes 1572868
  0.6 1.5 %copy-start.11 = (bf16[1,1,8,8,256]{4,3,2,1,0:T(8,128)(2,1)S(1)}, bf16[1,1,8,8,256]{4,3,2,1,0:T(8,128)(2,1)}, u32[]{:S(2)}) copy-start(bf16[1,1,8,8,256]{4,3,2,1,0:T(8,128)(2,1)} %param.7) | copy-start | bytes 98308
  1.8 6.6 %copy-start.8 = (bf16[3,3,3,64,128]{4,3,2,1,0:T(8,128)(2,1)S(1)}, bf16[3,3,3,64,128]{4,3,2,1,0:T(8,128)(2,1)}, u32[]{:S(2)}) copy-start(bf16[3,3,3,64,128]{4,3,2,1,0:T(8,128)(2,1)} %param.5) | copy-start | bytes 1327108
  2.2 7.2 %collective-permute-start = (bf16[640,128]{1,0:T(8,128)(2,1)S(1)}, bf16[640,128]{1,0:T(8,128)(2,1)S(1)}, u32[]{:S(2)}, u32[]{:S(2)}) collective-permute-start(bf16[640,128]{1,0:T(8,128)(2,1)S(1)} %get-tuple-element.52), channel_id=1, source_target_pairs={{0,4},{4,8},{8,12},{12,16},{16,20},{20,24},{24,28},{28,32},{32,36}... | collective-permute-start | bytes 491528 | tf_op jit(solution)/shard_map/ppermute | solution.py:325
  6.6 10.9 %collective-permute-start.1 = (bf16[640,128]{1,0:T(8,128)(2,1)S(1)}, bf16[640,128]{1,0:T(8,128)(2,1)S(1)}, u32[]{:S(2)}, u32[]{:S(2)}) collective-permute-start(bf16[640,128]{1,0:T(8,128)(2,1)S(1)} %get-tuple-element.51), channel_id=1, source_target_pairs={{4,0},{8,4},{12,8},{16,12},{20,16},{24,20},{28,24},{32,28},{36,32}... | collective-permute-start | bytes 491528 | tf_op jit(solution)/shard_map/ppermute | solution.py:325
  9.4 8.0 %copy-start.9 = (bf16[640,128]{1,0:T(8,128)(2,1)}, bf16[640,128]{1,0:T(8,128)(2,1)S(1)}, u32[]{:S(2)}) copy-start(bf16[640,128]{1,0:T(8,128)(2,1)S(1)} %collective-permute-done) | copy-start | bytes 491524
  17.4 0.7 copy-start.10
  18.1 18.0 %copy-start = (bf16[3,3,3,128,256]{4,3,2,1,0:T(8,128)(2,1)S(1)}, bf16[3,3,3,128,256]{4,3,2,1,0:T(8,128)(2,1)}, u32[]{:S(2)}) copy-start(bf16[3,3,3,128,256]{4,3,2,1,0:T(8,128)(2,1)} %param.6) | copy-start | bytes 5308420
  22.2 1.2 copy-start.1
  23.4 1.0 copy-start.5
  24.3 6.8 %collective-permute-start.2 = (bf16[2,256,128]{2,1,0:T(8,128)(2,1)}, bf16[2,256,128]{2,1,0:T(8,128)(2,1)S(1)}, u32[]{:S(2)}, u32[]{:S(2)}) collective-permute-start(bf16[2,256,128]{2,1,0:T(8,128)(2,1)} %get-tuple-element.22.cells_ref), channel_id=1, source_target_pairs={{0,4},{4,8},{8,12},{12,16},{16,20},{20,24},{24,28},{28,32},{32,36}... | collective-permute-start | bytes 393224 | tf_op jit(solution)/shard_map/ppermute | solution.py:325
  26.5 9.6 %collective-permute-start.3 = (bf16[2,256,128]{2,1,0:T(8,128)(2,1)}, bf16[2,256,128]{2,1,0:T(8,128)(2,1)S(1)}, u32[]{:S(2)}, u32[]{:S(2)}) collective-permute-start(bf16[2,256,128]{2,1,0:T(8,128)(2,1)} %get-tuple-element.22.cells_ref), channel_id=1, source_target_pairs={{4,0},{8,4},{12,8},{16,12},{20,16},{24,20},{28,24},{32,28},{36,32}... | collective-permute-start | bytes 393224 | tf_op jit(solution)/shard_map/ppermute | solution.py:325
  36.2 7.5 %copy-start.2 = (bf16[6,544,256]{2,1,0:T(8,128)(2,1)S(1)}, bf16[6,544,256]{2,1,0:T(8,128)(2,1)}, u32[]{:S(2)}) copy-start(bf16[6,544,256]{2,1,0:T(8,128)(2,1)} %copy-done.1) | copy-start | bytes 5013508
  36.2 7.5 %copy-start.6 = (bf16[4,512,256]{2,1,0:T(8,128)(2,1)S(1)}, bf16[4,512,256]{2,1,0:T(8,128)(2,1)}, u32[]{:S(2)}) copy-start(bf16[4,512,256]{2,1,0:T(8,128)(2,1)} %copy-done.5) | copy-start | bytes 3145732
  42.4 6.6 %collective-permute-start.5 = (bf16[9,384,128]{2,1,0:T(8,128)(2,1)S(1)}, bf16[9,384,128]{2,1,0:T(8,128)(2,1)S(1)}, u32[]{:S(2)}, u32[]{:S(2)}) collective-permute-start(bf16[9,384,128]{2,1,0:T(8,128)(2,1)S(1)} %get-tuple-element.32), channel_id=1, source_target_pairs={{0,1},{1,0},{2,3},{3,2},{4,5},{5,4},{6,7},{7,6},{8,9},{9,8},{10,11... | collective-permute-start | bytes 2654216 | tf_op jit(solution)/shard_map/ppermute | solution.py:302
  46.5 1.0 copy-start.3
  47.5 1.5 %collective-permute-start.4 = (bf16[9,96,128]{2,1,0:T(8,128)(2,1)S(1)}, bf16[9,96,128]{2,1,0:T(8,128)(2,1)S(1)}, u32[]{:S(2)}, u32[]{:S(2)}) collective-permute-start(bf16[9,96,128]{2,1,0:T(8,128)(2,1)S(1)} %get-tuple-element.30), channel_id=1, source_target_pairs={{0,1},{1,0},{2,3},{3,2},{4,5},{5,4},{6,7},{7,6},{8,9},{9,8},{10,11... | collective-permute-start | bytes 663560 | tf_op jit(solution)/shard_map/ppermute | solution.py:302
  74.1 28.0 %all-to-all-start.1 = ((bf16[8,272,128]{2,1,0:T(8,128)(2,1)}), bf16[8,272,128]{2,1,0:T(8,128)(2,1)S(1)}, u32[]{:S(2)}, u32[]{:S(2)}) async-start(bf16[8,272,128]{2,1,0:T(8,128)(2,1)} %broadcast_in_dim.29), calls=%async_computation.1 | async-start | bytes 1114112 | tf_op jit(solution)/shard_map/all_to_all | solution.py:306
  84.5 1.2 copy-start.4
  88.4 8.5 %collective-permute-start.6 = (bf16[512,128]{1,0:T(8,128)(2,1)S(1)}, bf16[512,128]{1,0:T(8,128)(2,1)S(1)}, u32[]{:S(2)}, u32[]{:S(2)}) collective-permute-start(bf16[512,128]{1,0:T(8,128)(2,1)S(1)} %get-tuple-element.33), channel_id=1, source_target_pairs={{0,4},{4,8},{8,12},{12,16},{16,20},{20,24},{24,28},{28,32},{32,36}... | collective-permute-start | bytes 393224 | tf_op jit(solution)/shard_map/ppermute | solution.py:325
  91.7 10.4 %collective-permute-start.7 = (bf16[512,128]{1,0:T(8,128)(2,1)S(1)}, bf16[512,128]{1,0:T(8,128)(2,1)S(1)}, u32[]{:S(2)}, u32[]{:S(2)}) collective-permute-start(bf16[512,128]{1,0:T(8,128)(2,1)S(1)} %get-tuple-element.34), channel_id=1, source_target_pairs={{4,0},{8,4},{12,8},{16,12},{20,16},{24,20},{28,24},{32,28},{36,32}... | collective-permute-start | bytes 393224 | tf_op jit(solution)/shard_map/ppermute | solution.py:325
  120.6 6.9 %collective-permute-start.8 = (bf16[4352,128]{1,0:T(8,128)(2,1)S(1)}, bf16[4352,128]{1,0:T(8,128)(2,1)S(1)}, u32[]{:S(2)}, u32[]{:S(2)}) collective-permute-start(bf16[4352,128]{1,0:T(8,128)(2,1)S(1)} %bitcast.32), channel_id=1, source_target_pairs={{0,1},{1,0},{2,3},{3,2},{4,5},{5,4},{6,7},{7,6},{8,9},{9,8},{10,11... | collective-permute-start | bytes 3342344 | tf_op jit(solution)/shard_map/ppermute | solution.py:302

commit v4 on v2

--- a/solution.py
+++ b/solution.py
@@ -7,7 +7,8 @@
 
 BF16 = jnp.bfloat16
 F32 = jnp.float32
-ROOM = 50 * 1024 * 1024
+LARGE_ROOM = 50 * 1024 * 1024
+ROOM = 16 * 1024 * 1024
 SCALAR = pl.BlockSpec(memory_space=pltpu.SMEM)
 WHOLE = pl.BlockSpec(memory_space=pltpu.VMEM)
 
@@ -81,7 +82,7 @@
             jax.ShapeDtypeStruct((4, 512, 256), BF16),
             jax.ShapeDtypeStruct((2, 256, 128), BF16),
         ),
-        compiler_params=pltpu.CompilerParams(vmem_limit_bytes=ROOM),
+        compiler_params=pltpu.CompilerParams(vmem_limit_bytes=LARGE_ROOM),
         cost_estimate=pl.CostEstimate(flops=2 * 2048 * 2304 * 256, bytes_accessed=6 * 10**6, transcendentals=10**6),
     )(left, cells, right, weight)
 

time: 130 us -> 131 us (level)
  local copies, waits for them, and re-layouts: 6.1 us -> 10.8 us
  waiting for transfers between devices: 29.7 us -> 26.8 us
    ppermute x3, waiting for transfers between devices: 19 us -> 16.9 us  [neighbours(): lax.ppermute(to_left, 'slab', down)]
    unnamed x11 -> x23, local copies, waits for them, and re-layouts: 2.27 us -> 3.92 us
    slice x2, local copies, waits for them, and re-layouts: 0.01 us -> 1.48 us  [shards(): side[512:576]]
    pallas_call x1, Pallas kernels: 4.22 us -> 2.79 us  [kernel_a(): pl.pallas_call(kernel_a_kernel, in_specs=[SCALAR] + [WHOLE] * 3, out_shap...]
  transfers between devices with their start and end apart: 10 -> 10, of which waited for: 9 -> 8; matrix products, arithmetic and copies ran while one was open for 2% -> 4% of each run, Pallas kernels for 5% -> 4%
where the time goes in v4:
time: 131 us; the launch traced here: 130 us
  blocking collectives  43.9 us (34%)
  waiting for transfers between devices  26.8 us (20%)
  starting transfers between devices  26.1 us (20%)
  Pallas kernels  19.4 us (15%)
  local copies, waits for them, and re-layouts  10.8 us (8%)
  other arithmetic  1.78 us (1%)
    all_to_all x2, blocking collectives, exchange(): lax.all_to_all(blocks, AXES, 0, 0, axis_index_groups=groups, tiled=True)  43.9 us
    ppermute x3, waiting for transfers between devices, neighbours(): lax.ppermute(to_left, 'slab', down)  16.9 us
    ppermute x3, starting transfers between devices, neighbours(): lax.ppermute(to_right, 'slab', up)  8.89 us
    all_to_all x1, starting transfers between devices, exchange(): lax.all_to_all(blocks, AXES, 0, 0, axis_index_groups=groups, tiled=True)  6.8 us
    ppermute x3, starting transfers between devices, other_core(): return lax.ppermute(value, AXES, CORES)  6.57 us
    pallas_call x1, Pallas kernels, block_b(): pl.pallas_call(block_b_kernel, in_specs=[SCALAR] + [WHOLE] * 5, out_shape...  6.25 us
    all_to_all x1, waiting for transfers between devices, exchange(): lax.all_to_all(blocks, AXES, 0, 0, axis_index_groups=groups, tiled=True)  5.74 us
    pallas_call x1, Pallas kernels, forward_a(): pl.pallas_call(forward_a_kernel, out_shape=(jax.ShapeDtypeStruct((6, 544,...  4.01 us
  transfers between devices with their start and end apart: 10, of which 8 were waited for; matrix products, arithmetic and copies ran while one was open for 4% of the time, Pallas kernels for 4%

profile of v4, /device:TPU:1, one launch (start us, length us, event | category | flops | bytes accessed | tf_op | source)
XLA Modules:
  0.0 129.8 jit_solution(11377573652019418710)
XLA Ops:
  0.7 1.2 fusion.2
  2.2 4.4 %collective-permute-start = (bf16[640,128]{1,0:T(8,128)(2,1)S(1)}, bf16[640,128]{1,0:T(8,128)(2,1)S(1)}, u32[]{:S(2)}, u32[]{:S(2)}) collective-permute-start(bf16[640,128]{1,0:T(8,128)(2,1)S(1)} %get-tuple-element.52), channel_id=1, source_target_pairs={{0,4},{4,8},{8,12},{12,16},{16,20},{20,24},{24,28},{28,32},{32,36}... | collective-permute-start | bytes 491528 | tf_op jit(solution)/shard_map/ppermute | solution.py:320
  6.6 1.3 collective-permute-start.1
  8.6 0.8 collective-permute-done
  9.4 8.0 %collective-permute-done.1 = bf16[640,128]{1,0:T(8,128)(2,1)S(1)} collective-permute-done((bf16[640,128]{1,0:T(8,128)(2,1)S(1)}, bf16[640,128]{1,0:T(8,128)(2,1)S(1)}, u32[]{:S(2)}, u32[]{:S(2)}) %collective-permute-start.1) | collective-permute-done | bytes 163872 | tf_op jit(solution)/shard_map/ppermute | solution.py:320
  18.1 4.0 %shard_map.75 = (bf16[6,544,256]{2,1,0:T(8,128)(2,1)}, bf16[4,512,256]{2,1,0:T(8,128)(2,1)S(1)}, bf16[2,256,128]{2,1,0:T(8,128)(2,1)}) custom-call(bf16[512,128]{1,0:T(8,128)(2,1)S(1)} %slice.71.left_ref, bf16[4,512,128]{2,1,0:T(8,128)(2,1)S(1)} %reshape.51.cells_ref, bf16[512,128]{1,0:T(8,128)(2,1)S(1)} %slice.72.right_ref, ...), custom_call_target="tpu_custom_call" | custom-call | flops 2415919104 | bytes 6000000 | tf_op jit(solution)/shard_map/pallas_call | solution.py:78
  22.1 1.0 copy-done.4
  23.1 2.2 %collective-permute-start.2 = (bf16[2,256,128]{2,1,0:T(8,128)(2,1)}, bf16[2,256,128]{2,1,0:T(8,128)(2,1)S(1)}, u32[]{:S(2)}, u32[]{:S(2)}) collective-permute-start(bf16[2,256,128]{2,1,0:T(8,128)(2,1)} %get-tuple-element.22.cells_ref), channel_id=1, source_target_pairs={{0,4},{4,8},{8,12},{12,16},{16,20},{20,24},{24,28},{28,32},{32,36}... | collective-permute-start | bytes 393224 | tf_op jit(solution)/shard_map/ppermute | solution.py:320
  25.3 1.3 collective-permute-start.3
  28.9 1.0 reshape.54.cot_ref
  29.9 5.0 %collective-permute-done.3.right_ref = bf16[2,256,128]{2,1,0:T(8,128)(2,1)S(1)} collective-permute-done((bf16[2,256,128]{2,1,0:T(8,128)(2,1)}, bf16[2,256,128]{2,1,0:T(8,128)(2,1)S(1)}, u32[]{:S(2)}, u32[]{:S(2)}) %collective-permute-start.3) | collective-permute-done | bytes 131104 | tf_op jit(solution)/shard_map/ppermute | solution.py:320
  34.9 6.2 %shard_map.76 = (bf16[64,256]{1,0:T(8,128)(2,1)}, bf16[9,384,128]{2,1,0:T(8,128)(2,1)S(1)}, bf16[9,384,128]{2,1,0:T(8,128)(2,1)S(1)}, bf16[2,256,128]{2,1,0:T(8,128)(2,1)S(1)}) custom-call(s32[1]{0:T(128)} %bitcast.core_ref, bf16[2,256,128]{2,1,0:T(8,128)(2,1)S(1)} %collective-permute-done.2.left_ref, bf16[2,256,128]{2,1,0:T(8,128)(2,1)} %get-tuple-element.22.cells_ref, ...), custom_call_target="tpu_custom_call" | custom-call | flops 3623878656 | bytes 5000000 | tf_op jit(solution)/shard_map/pallas_call | solution.py:150
  41.2 1.3 collective-permute-start.5
  42.5 2.8 %shard_map.77 = (bf16[4,544,256]{2,1,0:T(8,128)(2,1)S(1)}, bf16[9,96,128]{2,1,0:T(8,128)(2,1)S(1)}, bf16[9,96,128]{2,1,0:T(8,128)(2,1)S(1)}) custom-call(s32[1]{0:T(128)} %bitcast.core_ref, bf16[2,256,128]{2,1,0:T(8,128)(2,1)S(1)} %get-tuple-element.24.grad_ref, bf16[4,512,256]{2,1,0:T(8,128)(2,1)S(1)} %copy-done.5, bf16[6,544,256]{2,1,0:T(8,128)(2,1)S(1)} %copy-done.1), custom_call_target="tpu_custom_call" | custom-call | flops 2415919104 | bytes 6000000 | tf_op jit(solution)/shard_map/pallas_call | solution.py:193
  45.3 1.0 copy-done.2
  46.3 1.4 %collective-permute-done.4.other_a_ref = bf16[9,96,128]{2,1,0:T(8,128)(2,1)S(1)} collective-permute-done((bf16[9,96,128]{2,1,0:T(8,128)(2,1)S(1)}, bf16[9,96,128]{2,1,0:T(8,128)(2,1)S(1)}, u32[]{:S(2)}, u32[]{:S(2)}) %collective-permute-start.4) | collective-permute-done | bytes 221216 | tf_op jit(solution)/shard_map/ppermute | solution.py:299
  47.7 1.2 shard_map.79
  49.0 6.8 %all-to-all-start = ((bf16[16,272,128]{2,1,0:T(8,128)(2,1)}), bf16[16,272,128]{2,1,0:T(8,128)(2,1)}, u32[]{:S(2)}, u32[]{:S(2)}) async-start(bf16[16,272,128]{2,1,0:T(8,128)(2,1)} %bitcast.11), calls=%async_computation | async-start | bytes 2228224 | tf_op jit(solution)/shard_map/all_to_all | solution.py:303
  55.8 1.2 copy-done.3
  57.1 2.6 %shard_map.78 = (bf16[4,512,128]{2,1,0:T(8,128)(2,1)S(1)}, bf16[512,128]{1,0:T(8,128)(2,1)S(1)}, bf16[512,128]{1,0:T(8,128)(2,1)S(1)}) custom-call(bf16[4,544,256]{2,1,0:T(8,128)(2,1)S(1)} %copy-done.3, bf16[9,256,256]{2,1,0:T(8,128)(2,1)S(1)} %maximum_maximum_fusion.weight_ref), custom_call_target="tpu_custom_call" | custom-call | flops 2415919104 | bytes 4000000 | tf_op jit(solution)/shard_map/pallas_call | solution.py:228
  59.7 2.3 %collective-permute-start.6 = (bf16[512,128]{1,0:T(8,128)(2,1)S(1)}, bf16[512,128]{1,0:T(8,128)(2,1)S(1)}, u32[]{:S(2)}, u32[]{:S(2)}) collective-permute-start(bf16[512,128]{1,0:T(8,128)(2,1)S(1)} %get-tuple-element.33), channel_id=1, source_target_pairs={{0,4},{4,8},{8,12},{12,16},{16,20},{20,24},{24,28},{28,32},{32,36}... | collective-permute-start | bytes 393224 | tf_op jit(solution)/shard_map/ppermute | solution.py:320
  62.0 1.3 collective-permute-start.7
  63.3 1.1 collective-permute-done.6
  64.4 3.9 %collective-permute-done.7 = bf16[512,128]{1,0:T(8,128)(2,1)S(1)} collective-permute-done((bf16[512,128]{1,0:T(8,128)(2,1)S(1)}, bf16[512,128]{1,0:T(8,128)(2,1)S(1)}, u32[]{:S(2)}, u32[]{:S(2)}) %collective-permute-start.7) | collective-permute-done | bytes 131104 | tf_op jit(solution)/shard_map/ppermute | solution.py:320
  68.3 5.7 %all-to-all-done = bf16[16,272,128]{2,1,0:T(8,128)(2,1)} async-done(((bf16[16,272,128]{2,1,0:T(8,128)(2,1)}), bf16[16,272,128]{2,1,0:T(8,128)(2,1)}, u32[]{:S(2)}, u32[]{:S(2)}) %all-to-all-start) | async-done | bytes 1114144 | tf_op jit(solution)/shard_map/all_to_all | solution.py:303
  74.1 1.4 %reduce_sum.24 = bf16[272,128]{1,0:T(8,128)(2,1)S(1)} reduce(bf16[16,272,128]{2,1,0:T(8,128)(2,1)} %all-to-all-done, bf16[]{:T(256)} %constant.21.clone.1), dimensions={0}, to_apply=%region_0.1 | reduce | flops 522240 | bytes 1183746 | tf_op jit(solution)/shard_map/reduce_sum | solution.py:307
  75.6 23.6 %all_to_all.15 = bf16[8,272,128]{2,1,0:T(8,128)(2,1)S(1)} all-to-all(bf16[8,272,128]{2,1,0:T(8,128)(2,1)S(1)} %broadcast_in_dim.33), channel_id=1, replica_groups={{0,4,8,12,2,6,10,14},{1,5,9,13,3,7,11,15},{16,20,24,28,18,22,26,30},{17..., dimensions={0} | all-to-all | bytes 1114112 | tf_op jit(solution)/shard_map/all_to_all | solution.py:303
  99.4 20.3 %all_to_all.16 = bf16[16,272,128]{2,1,0:T(8,128)(2,1)S(1)} all-to-all(bf16[16,272,128]{2,1,0:T(8,128)(2,1)S(1)} %broadcast_in_dim.34), channel_id=1, replica_groups={{0,16,32,48,64,80,96,112,128,144,160,176,192,208,224,240},{1,17,33,49,6..., dimensions={0} | all-to-all | bytes 2228224 | tf_op jit(solution)/shard_map/all_to_all | solution.py:303
  119.7 5.3 %collective-permute-start.8 = (bf16[4352,128]{1,0:T(8,128)(2,1)S(1)}, bf16[4352,128]{1,0:T(8,128)(2,1)S(1)}, u32[]{:S(2)}, u32[]{:S(2)}) collective-permute-start(bf16[4352,128]{1,0:T(8,128)(2,1)S(1)} %bitcast.32), channel_id=1, source_target_pairs={{0,1},{1,0},{2,3},{3,2},{4,5},{5,4},{6,7},{7,6},{8,9},{9,8},{10,11... | collective-permute-start | bytes 3342344 | tf_op jit(solution)/shard_map/ppermute | solution.py:299
  125.2 1.4 %reshape.57 = bf16[1,4,32,32,64]{4,3,2,1,0:T(8,128)(2,1)} reshape(bf16[4,512,128]{2,1,0:T(8,128)(2,1)S(1)} %pad_maximum_fusion) | data formatting | bytes 1048576 | tf_op jit(solution)/shard_map/reshape | solution.py:353
  126.5 0.8 collective-permute-done.8.away_ref
  127.4 2.4 %shard_map.80 = (f32[9,2,96,128]{3,2,1,0:T(8,128)}, f32[9,384,256]{2,1,0:T(8,128)}) custom-call(s32[1]{0:T(128)} %bitcast.core_ref, bf16[4352,128]{1,0:T(8,128)(2,1)S(1)} %bitcast.33, bf16[4352,128]{1,0:T(8,128)(2,1)S(1)} %collective-permute-done.8.away_ref), custom_call_target="tpu_custom_call" | custom-call | bytes 7000000 | tf_op jit(solution)/shard_map/pallas_call | solution.py:280
  (44 shorter events, 4.5 us)
Async XLA Ops:
  0.6 7.3 %copy-start.6 = (bf16[1,4,32,32,64]{4,3,2,1,0:T(8,128)(2,1)S(1)}, bf16[1,4,32,32,64]{4,3,2,1,0:T(8,128)(2,1)}, u32[]{:S(2)}) copy-start(bf16[1,4,32,32,64]{4,3,2,1,0:T(8,128)(2,1)} %param.4) | copy-start | bytes 1572868
  0.6 1.5 %copy-start.10 = (bf16[1,1,8,8,256]{4,3,2,1,0:T(8,128)(2,1)S(1)}, bf16[1,1,8,8,256]{4,3,2,1,0:T(8,128)(2,1)}, u32[]{:S(2)}) copy-start(bf16[1,1,8,8,256]{4,3,2,1,0:T(8,128)(2,1)} %param.7) | copy-start | bytes 98308
  1.8 6.6 %copy-start.7 = (bf16[3,3,3,64,128]{4,3,2,1,0:T(8,128)(2,1)S(1)}, bf16[3,3,3,64,128]{4,3,2,1,0:T(8,128)(2,1)}, u32[]{:S(2)}) copy-start(bf16[3,3,3,64,128]{4,3,2,1,0:T(8,128)(2,1)} %param.5) | copy-start | bytes 1327108
  2.2 7.2 %collective-permute-start = (bf16[640,128]{1,0:T(8,128)(2,1)S(1)}, bf16[640,128]{1,0:T(8,128)(2,1)S(1)}, u32[]{:S(2)}, u32[]{:S(2)}) collective-permute-start(bf16[640,128]{1,0:T(8,128)(2,1)S(1)} %get-tuple-element.52), channel_id=1, source_target_pairs={{0,4},{4,8},{8,12},{12,16},{16,20},{20,24},{24,28},{28,32},{32,36}... | collective-permute-start | bytes 491528 | tf_op jit(solution)/shard_map/ppermute | solution.py:320
  6.6 10.9 %collective-permute-start.1 = (bf16[640,128]{1,0:T(8,128)(2,1)S(1)}, bf16[640,128]{1,0:T(8,128)(2,1)S(1)}, u32[]{:S(2)}, u32[]{:S(2)}) collective-permute-start(bf16[640,128]{1,0:T(8,128)(2,1)S(1)} %get-tuple-element.51), channel_id=1, source_target_pairs={{4,0},{8,4},{12,8},{16,12},{20,16},{24,20},{28,24},{32,28},{36,32}... | collective-permute-start | bytes 491528 | tf_op jit(solution)/shard_map/ppermute | solution.py:320
  9.4 8.0 %copy-start.8 = (bf16[640,128]{1,0:T(8,128)(2,1)}, bf16[640,128]{1,0:T(8,128)(2,1)S(1)}, u32[]{:S(2)}) copy-start(bf16[640,128]{1,0:T(8,128)(2,1)S(1)} %collective-permute-done) | copy-start | bytes 491524
  17.4 0.7 copy-start.9
  18.1 16.8 %copy-start = (bf16[3,3,3,128,256]{4,3,2,1,0:T(8,128)(2,1)S(1)}, bf16[3,3,3,128,256]{4,3,2,1,0:T(8,128)(2,1)}, u32[]{:S(2)}) copy-start(bf16[3,3,3,128,256]{4,3,2,1,0:T(8,128)(2,1)} %param.6) | copy-start | bytes 5308420
  22.1 1.0 copy-start.4
  23.1 6.8 %collective-permute-start.2 = (bf16[2,256,128]{2,1,0:T(8,128)(2,1)}, bf16[2,256,128]{2,1,0:T(8,128)(2,1)S(1)}, u32[]{:S(2)}, u32[]{:S(2)}) collective-permute-start(bf16[2,256,128]{2,1,0:T(8,128)(2,1)} %get-tuple-element.22.cells_ref), channel_id=1, source_target_pairs={{0,4},{4,8},{8,12},{12,16},{16,20},{20,24},{24,28},{28,32},{32,36}... | collective-permute-start | bytes 393224 | tf_op jit(solution)/shard_map/ppermute | solution.py:320
  25.3 9.6 %collective-permute-start.3 = (bf16[2,256,128]{2,1,0:T(8,128)(2,1)}, bf16[2,256,128]{2,1,0:T(8,128)(2,1)S(1)}, u32[]{:S(2)}, u32[]{:S(2)}) collective-permute-start(bf16[2,256,128]{2,1,0:T(8,128)(2,1)} %get-tuple-element.22.cells_ref), channel_id=1, source_target_pairs={{4,0},{8,4},{12,8},{16,12},{20,16},{24,20},{28,24},{32,28},{36,32}... | collective-permute-start | bytes 393224 | tf_op jit(solution)/shard_map/ppermute | solution.py:320
  34.9 7.5 %copy-start.1 = (bf16[6,544,256]{2,1,0:T(8,128)(2,1)S(1)}, bf16[6,544,256]{2,1,0:T(8,128)(2,1)}, u32[]{:S(2)}) copy-start(bf16[6,544,256]{2,1,0:T(8,128)(2,1)} %get-tuple-element.26.window_ref) | copy-start | bytes 5013508
  34.9 7.5 %copy-start.5 = (bf16[4,512,256]{2,1,0:T(8,128)(2,1)S(1)}, bf16[4,512,256]{2,1,0:T(8,128)(2,1)}, u32[]{:S(2)}) copy-start(bf16[4,512,256]{2,1,0:T(8,128)(2,1)} %copy-done.4) | copy-start | bytes 3145732
  41.2 6.5 %collective-permute-start.5 = (bf16[9,384,128]{2,1,0:T(8,128)(2,1)S(1)}, bf16[9,384,128]{2,1,0:T(8,128)(2,1)S(1)}, u32[]{:S(2)}, u32[]{:S(2)}) collective-permute-start(bf16[9,384,128]{2,1,0:T(8,128)(2,1)S(1)} %get-tuple-element.32), channel_id=1, source_target_pairs={{0,1},{1,0},{2,3},{3,2},{4,5},{5,4},{6,7},{7,6},{8,9},{9,8},{10,11... | collective-permute-start | bytes 2654216 | tf_op jit(solution)/shard_map/ppermute | solution.py:299
  45.3 1.0 copy-start.2
  46.3 1.5 %collective-permute-start.4 = (bf16[9,96,128]{2,1,0:T(8,128)(2,1)S(1)}, bf16[9,96,128]{2,1,0:T(8,128)(2,1)S(1)}, u32[]{:S(2)}, u32[]{:S(2)}) collective-permute-start(bf16[9,96,128]{2,1,0:T(8,128)(2,1)S(1)} %get-tuple-element.30), channel_id=1, source_target_pairs={{0,1},{1,0},{2,3},{3,2},{4,5},{5,4},{6,7},{7,6},{8,9},{9,8},{10,11... | collective-permute-start | bytes 663560 | tf_op jit(solution)/shard_map/ppermute | solution.py:299
  49.0 25.1 %all-to-all-start = ((bf16[16,272,128]{2,1,0:T(8,128)(2,1)}), bf16[16,272,128]{2,1,0:T(8,128)(2,1)}, u32[]{:S(2)}, u32[]{:S(2)}) async-start(bf16[16,272,128]{2,1,0:T(8,128)(2,1)} %bitcast.11), calls=%async_computation | async-start | bytes 2228224 | tf_op jit(solution)/shard_map/all_to_all | solution.py:303
  55.8 1.3 copy-start.3
  59.7 4.7 %collective-permute-start.6 = (bf16[512,128]{1,0:T(8,128)(2,1)S(1)}, bf16[512,128]{1,0:T(8,128)(2,1)S(1)}, u32[]{:S(2)}, u32[]{:S(2)}) collective-permute-start(bf16[512,128]{1,0:T(8,128)(2,1)S(1)} %get-tuple-element.33), channel_id=1, source_target_pairs={{0,4},{4,8},{8,12},{12,16},{16,20},{20,24},{24,28},{28,32},{32,36}... | collective-permute-start | bytes 393224 | tf_op jit(solution)/shard_map/ppermute | solution.py:320
  62.0 6.3 %collective-permute-start.7 = (bf16[512,128]{1,0:T(8,128)(2,1)S(1)}, bf16[512,128]{1,0:T(8,128)(2,1)S(1)}, u32[]{:S(2)}, u32[]{:S(2)}) collective-permute-start(bf16[512,128]{1,0:T(8,128)(2,1)S(1)} %get-tuple-element.34), channel_id=1, source_target_pairs={{4,0},{8,4},{12,8},{16,12},{20,16},{24,20},{28,24},{32,28},{36,32}... | collective-permute-start | bytes 393224 | tf_op jit(solution)/shard_map/ppermute | solution.py:320
  119.7 7.7 %collective-permute-start.8 = (bf16[4352,128]{1,0:T(8,128)(2,1)S(1)}, bf16[4352,128]{1,0:T(8,128)(2,1)S(1)}, u32[]{:S(2)}, u32[]{:S(2)}) collective-permute-start(bf16[4352,128]{1,0:T(8,128)(2,1)S(1)} %bitcast.32), channel_id=1, source_target_pairs={{0,1},{1,0},{2,3},{3,2},{4,5},{5,4},{6,7},{7,6},{8,9},{9,8},{10,11... | collective-permute-start | bytes 3342344 | tf_op jit(solution)/shard_map/ppermute | solution.py:299

commit v5 on v2

--- a/solution.py
+++ b/solution.py
@@ -10,6 +10,7 @@
 ROOM = 50 * 1024 * 1024
 SCALAR = pl.BlockSpec(memory_space=pltpu.SMEM)
 WHOLE = pl.BlockSpec(memory_space=pltpu.VMEM)
+APART = pl.BlockSpec(memory_space=pltpu.HBM)
 
 
 def nt_dot(lhs, rhs):
@@ -39,51 +40,82 @@
     return lax.broadcasted_iota(jnp.int32, shape, 1) < 64
 
 
-def forward_a_kernel(left_ref, cells_ref, right_ref, weight_ref, window_ref, slope_ref, pooled_ref):
+def pack_pairs(pairs, window_ref, layer):
     edge = jnp.zeros((16, 256), BF16)
-    for layer in range(6):
-        if layer == 0:
-            pairs = left_ref[...]
-        elif layer == 5:
-            pairs = right_ref[...]
+    wide = pairs.astype(F32)
+    outer = jnp.where(low_lanes(wide.shape), next_rows(wide, 16), previous_rows(wide, 16))
+    window_ref[layer, 0:16, :] = edge
+    window_ref[layer, 528:544, :] = edge
+    window_ref[layer, 16:528, 0:128] = pairs
+    window_ref[layer, 16:528, 128:256] = outer.astype(BF16)
+
+
+def layer_terms(window_ref, source, weight_ref, shift_x, total):
+    for shift_y in range(3):
+        view = window_ref[source, 16 * shift_y : 16 * shift_y + 512, :]
+        term = nn_dot(view, weight_ref[3 * shift_x + shift_y])
+        total = term if total is None else total + term
+    return total
+
+
+def slope_and_pool(total):
+    sigma = 1.0 / (1.0 + jnp.exp(-total))
+    blocks = (total * sigma).reshape(16, 2, 16, 256)
+    blocks = blocks[:, 0] + blocks[:, 1]
+    slope = sigma * (1.0 + total * (1.0 - sigma))
+    return slope.astype(BF16), (blocks[:, :, :128] + blocks[:, :, 128:]).reshape(256, 128)
+
+
+def forward_inner_kernel(cells_ref, weight_ref, window_ref, partial_ref, slope_ref, pool_ref):
+    for layer in range(4):
+        pack_pairs(cells_ref[layer], window_ref, layer)
+    for layer in range(4):
+        total = None
+        for shift_x in range(3):
+            source = layer + shift_x - 1
+            if 0 <= source < 4:
+                total = layer_terms(window_ref, source, weight_ref, shift_x, total)
+        if layer in (0, 3):
+            partial_ref[layer // 3] = total
         else:
-            pairs = cells_ref[layer - 1]
-        wide = pairs.astype(F32)
-        outer = jnp.where(low_lanes(wide.shape), next_rows(wide, 16), previous_rows(wide, 16))
-        window_ref[layer, 0:16, :] = edge
-        window_ref[layer, 528:544, :] = edge
-        window_ref[layer, 16:528, 0:128] = pairs
-        window_ref[layer, 16:528, 128:256] = outer.astype(BF16)
-    for half in range(2):
-        total = None
-        for tap in range(9):
-            shift_x, shift_y = tap // 3, tap % 3
-            first = 2 * half + shift_x
-            window = window_ref[first : first + 2, 16 * shift_y : 16 * shift_y + 512, :]
-            term = nn_dot(window.reshape(1024, 256), weight_ref[tap])
-            total = term if total is None else total + term
-        sigma = 1.0 / (1.0 + jnp.exp(-total))
-        active = total * sigma
-        slope = sigma * (1.0 + total * (1.0 - sigma))
-        slope_ref[2 * half : 2 * half + 2] = slope.astype(BF16).reshape(2, 512, 256)
-        blocks = active.reshape(2, 16, 2, 16, 256)
-        blocks = (blocks[0] + blocks[1])
-        blocks = blocks[:, 0] + blocks[:, 1]
-        pooled = (blocks[:, :, :128] + blocks[:, :, 128:]) * 0.125
-        pooled_ref[half] = pooled.astype(BF16).reshape(256, 128)
-
-
-def forward_a(left, cells, right, weight):
-    return pl.pallas_call(
-        forward_a_kernel,
-        out_shape=(
-            jax.ShapeDtypeStruct((6, 544, 256), BF16),
-            jax.ShapeDtypeStruct((4, 512, 256), BF16),
+            slope_ref[layer - 1], pool_ref[layer - 1] = slope_and_pool(total)
+
+
+def forward_inner(cells, weight):
+    return pl.pallas_call(
+        forward_inner_kernel,
+        out_shape=(
+            jax.ShapeDtypeStruct((4, 544, 256), BF16),
+            jax.ShapeDtypeStruct((2, 512, 256), F32),
+            jax.ShapeDtypeStruct((2, 512, 256), BF16),
+            jax.ShapeDtypeStruct((2, 256, 128), F32),
+        ),
+        compiler_params=pltpu.CompilerParams(vmem_limit_bytes=ROOM),
+        cost_estimate=pl.CostEstimate(flops=2 * 2048 * 2304 * 256, bytes_accessed=6 * 10**6, transcendentals=10**6),
+    )(cells, weight)
+
+
+def forward_outer_kernel(left_ref, right_ref, weight_ref, partial_ref, pool_ref, window_ref, slope_ref, pooled_ref):
+    pack_pairs(left_ref[...], window_ref, 0)
+    pack_pairs(right_ref[...], window_ref, 1)
+    for side in range(2):
+        total = layer_terms(window_ref, side, weight_ref, 2 * side, partial_ref[side])
+        slope, pool = slope_and_pool(total)
+        slope_ref[side] = slope
+        pooled_ref[side] = ((pool + pool_ref[side]) * 0.125).astype(BF16)
+
+
+def forward_outer(left, right, weight, partial, pool):
+    return pl.pallas_call(
+        forward_outer_kernel,
+        out_shape=(
+            jax.ShapeDtypeStruct((2, 544, 256), BF16),
+            jax.ShapeDtypeStruct((2, 512, 256), BF16),
             jax.ShapeDtypeStruct((2, 256, 128), BF16),
         ),
         compiler_params=pltpu.CompilerParams(vmem_limit_bytes=ROOM),
-        cost_estimate=pl.CostEstimate(flops=2 * 2048 * 2304 * 256, bytes_accessed=6 * 10**6, transcendentals=10**6),
-    )(left, cells, right, weight)
+        cost_estimate=pl.CostEstimate(flops=10**9, bytes_accessed=5 * 10**6, transcendentals=10**6),
+    )(left, right, weight, partial, pool)
 
 
 def block_b_kernel(core_ref, left_ref, cells_ref, right_ref, weight_ref, cot_ref, features_ref, keep_ref, send_ref, grad_ref, window, grads, column):
@@ -165,33 +197,44 @@
     )(core, left, cells, right, weight, cot)
 
 
-def kernel_a_kernel(core_ref, grad_ref, slope_ref, window_ref, pre_ref, keep_ref, send_ref):
+def kernel_a_kernel(core_ref, grad_ref, slope_ref, ends_ref, window_ref, sides_ref, pre_out, keep_ref, send_ref, pre_ref, sem):
     core = core_ref[0]
     edge = jnp.zeros((16, 256), BF16)
     for layer in range(4):
         spread = grad_ref[layer // 2].astype(F32).reshape(16, 1, 16, 128) * 0.125
         spread = jnp.broadcast_to(spread, (16, 2, 16, 128)).reshape(512, 128)
-        slope = slope_ref[layer].astype(F32)
+        slope = (ends_ref[layer // 3] if layer in (0, 3) else slope_ref[layer - 1]).astype(F32)
         pre_ref[layer, 0:16, :] = edge
         pre_ref[layer, 528:544, :] = edge
         pre_ref[layer, 16:528, 0:128] = (spread * slope[:, 0:128]).astype(BF16)
         pre_ref[layer, 16:528, 128:256] = (spread * slope[:, 128:256]).astype(BF16)
+    store = pltpu.make_async_copy(pre_ref, pre_out, sem)
+    store.start()
     grads = pre_ref[:, 16:528, :].reshape(2048, 256)
     for tap in range(9):
         shift_x, shift_y = tap // 3, tap % 3
-        view = window_ref[shift_x : shift_x + 4, 16 * shift_y : 16 * shift_y + 512, :].reshape(2048, 256)
-        terms = tn_dot(view, grads) * 0.25
+        rows = slice(16 * shift_y, 16 * shift_y + 512)
+        if shift_x == 0:
+            terms = tn_dot(window_ref[0:3, rows].reshape(1536, 256), grads[512:]) + tn_dot(sides_ref[0, rows], grads[:512])
+        elif shift_x == 1:
+            terms = tn_dot(window_ref[:, rows].reshape(2048, 256), grads)
+        else:
+            terms = tn_dot(window_ref[1:4, rows].reshape(1536, 256), grads[:1536]) + tn_dot(sides_ref[1, rows], grads[1536:])
+        terms = terms * 0.25
         even, odd = terms[:, :128], terms[:, 128:]
         first = jnp.concatenate([even[192:256] + odd[0:64], even[0:32] + odd[64:96]]).astype(BF16)
         second = (even[32:128] + odd[96:192]).astype(BF16)
         keep_ref[tap] = jnp.where(core == 0, first, second)
         send_ref[tap] = jnp.where(core == 0, second, first)
-
-
-def kernel_a(core, grad, slope, window):
+    store.wait()
+
+
+def kernel_a(core, grad, slope, ends, window, sides):
     return pl.pallas_call(
         kernel_a_kernel,
-        in_specs=[SCALAR] + [WHOLE] * 3,
+        in_specs=[SCALAR] + [WHOLE] * 5,
+        out_specs=(APART, WHOLE, WHOLE),
+        scratch_shapes=[pltpu.VMEM((4, 544, 256), BF16), pltpu.SemaphoreType.DMA],
         out_shape=(
             jax.ShapeDtypeStruct((4, 544, 256), BF16),
             jax.ShapeDtypeStruct((9, 96, 128), BF16),
@@ -199,7 +242,7 @@
         ),
         compiler_params=pltpu.CompilerParams(vmem_limit_bytes=ROOM),
         cost_estimate=pl.CostEstimate(flops=2 * 2048 * 2304 * 256, bytes_accessed=6 * 10**6, transcendentals=0),
-    )(core, grad, slope, window)
+    )(core, grad, slope, ends, window, sides)
 
 
 def back_a_kernel(grads_ref, weight_ref, inner_ref, to_left_ref, to_right_ref):
@@ -327,14 +370,15 @@
     cot = cotangent.reshape(64, 256)
     cot_rows = [cot[:, :128], cot[:, 128:]]
     left, right = neighbours(jnp.concatenate([cells[0]] + cot_rows), jnp.concatenate([cells[3]] + cot_rows))
-    window, slope_a, pooled = forward_a(left[:512], cells, right[:512], pair_weight)
+    window, partial, slope_a, pool = forward_inner(cells, pair_weight)
+    sides, ends, pooled = forward_outer(left[:512], right[:512], pair_weight, partial, pool)
     pooled_left, pooled_right = neighbours(pooled, pooled)
     cots = [jnp.concatenate([side[512:576], side[576:640]], axis=1) for side in (left, right)]
     cots = jnp.stack([cots[0], cot, cots[1]])
     cots = jnp.broadcast_to(cots[:, :, None, :], (3, 64, 2, 256)).reshape(3, 128, 256)
     features, keep_b, send_b, grad_pooled = block_b(core, pooled_left, pooled, pooled_right, taps_b, cots)
     other_b = other_core(send_b)
-    grad_pre, keep_a, send_a = kernel_a(core, grad_pooled, slope_a, window)
+    grad_pre, keep_a, send_a = kernel_a(core, grad_pooled, slope_a, ends, window, sides)
     other_a = other_core(send_a)
     inner, to_left, to_right = back_a(grad_pre, pair_weight)
     from_left, from_right = neighbours(to_left, to_right)

time: 130 us -> 129 us (level)
  waiting for transfers between devices: 29.7 us -> 21.2 us
  blocking collectives: 43.9 us -> 46.4 us
  starting transfers between devices: 26 us -> 27.8 us
  local copies, waits for them, and re-layouts: 6.1 us -> 7.7 us
    ppermute x3, waiting for transfers between devices: 19 us -> 14.2 us  [neighbours(): lax.ppermute(to_left, 'slab', down)]
    all_to_all x2, blocking collectives: 43.9 us -> 46.4 us  [exchange(): lax.all_to_all(blocks, AXES, 0, 0, axis_index_groups=groups, tiled=True)]
    all_to_all x1, waiting for transfers between devices: 5.77 us -> 3.54 us  [exchange(): lax.all_to_all(blocks, AXES, 0, 0, axis_index_groups=groups, tiled=True)]
    ppermute x3, waiting for transfers between devices: 2.67 us -> 1.12 us  [neighbours(): lax.ppermute(to_right, 'slab', up)]
    pallas_call x2 -> x3, Pallas kernels: 7.64 us -> 8.96 us  [the longest x1 4.34 us: kernel_a(): pl.pallas_call(kernel_a_kernel, in_specs=[SCALAR] + [WHOLE] * 5, out_spec...]
  transfers between devices with their start and end apart: 10 -> 10, of which waited for: 9 -> 7; matrix products, arithmetic and copies ran while one was open for 2% -> 4% of each run, Pallas kernels for 5% -> 8%
where the time goes in v5:
time: 129 us
  blocking collectives  46.4 us (36%)
  starting transfers between devices  27.8 us (22%)
  Pallas kernels  21.9 us (17%)
  waiting for transfers between devices  21.2 us (16%)
  local copies, waits for them, and re-layouts  7.7 us (6%)
  other arithmetic  2.8 us (2%)
    all_to_all x2, blocking collectives, exchange(): lax.all_to_all(blocks, AXES, 0, 0, axis_index_groups=groups, tiled=True)  46.4 us
    ppermute x3, waiting for transfers between devices, neighbours(): lax.ppermute(to_left, 'slab', down)  14.2 us
    ppermute x3, starting transfers between devices, neighbours(): lax.ppermute(to_right, 'slab', up)  10.1 us
    all_to_all x1, starting transfers between devices, exchange(): lax.all_to_all(blocks, AXES, 0, 0, axis_index_groups=groups, tiled=True)  7.19 us
    ppermute x3, starting transfers between devices, other_core(): return lax.ppermute(value, AXES, CORES)  6.69 us
    pallas_call x1, Pallas kernels, block_b(): pl.pallas_call(block_b_kernel, in_specs=[SCALAR] + [WHOLE] * 5, out_shape...  6.66 us
    pallas_call x1, Pallas kernels, kernel_a(): pl.pallas_call(kernel_a_kernel, in_specs=[SCALAR] + [WHOLE] * 5, out_spec...  4.34 us
    ppermute x3, starting transfers between devices, neighbours(): lax.ppermute(to_left, 'slab', down)  3.88 us
  transfers between devices with their start and end apart: 10, of which 7 were waited for; matrix products, arithmetic and copies ran while one was open for 4% of the time, Pallas kernels for 8%

profile of v5, /device:TPU:1, one launch (start us, length us, event | category | flops | bytes accessed | tf_op | source)
XLA Modules:
  0.0 128.8 jit_solution(491074398045904286)
XLA Ops:
  0.7 1.2 fusion.2
  2.2 4.4 %collective-permute-start = (bf16[640,128]{1,0:T(8,128)(2,1)S(1)}, bf16[640,128]{1,0:T(8,128)(2,1)S(1)}, u32[]{:S(2)}, u32[]{:S(2)}) collective-permute-start(bf16[640,128]{1,0:T(8,128)(2,1)S(1)} %get-tuple-element.60), channel_id=1, source_target_pairs={{0,4},{4,8},{8,12},{12,16},{16,20},{20,24},{24,28},{28,32},{32,36}... | collective-permute-start | bytes 491528 | tf_op jit(solution)/shard_map/ppermute | solution.py:362
  6.6 1.3 %collective-permute-start.1 = (bf16[640,128]{1,0:T(8,128)(2,1)S(1)}, bf16[640,128]{1,0:T(8,128)(2,1)S(1)}, u32[]{:S(2)}, u32[]{:S(2)}) collective-permute-start(bf16[640,128]{1,0:T(8,128)(2,1)S(1)} %get-tuple-element.59), channel_id=1, source_target_pairs={{4,0},{8,4},{12,8},{16,12},{20,16},{24,20},{28,24},{32,28},{36,32}... | collective-permute-start | bytes 491528 | tf_op jit(solution)/shard_map/ppermute | solution.py:362
  8.5 1.1 maximum_maximum_fusion.weight_ref
  9.6 3.7 %shard_map.75 = (bf16[4,544,256]{2,1,0:T(8,128)(2,1)S(1)}, f32[2,512,256]{2,1,0:T(8,128)S(1)}, bf16[2,512,256]{2,1,0:T(8,128)(2,1)S(1)}, f32[2,256,128]{2,1,0:T(8,128)S(1)}) custom-call(bf16[4,512,128]{2,1,0:T(8,128)(2,1)S(1)} %reshape.52.cells_ref, bf16[9,256,256]{2,1,0:T(8,128)(2,1)} %maximum_maximum_fusion.weight_ref), custom_call_target="tpu_custom_call" | custom-call | flops 2415919104 | bytes 6000000 | tf_op jit(solution)/shard_map/pallas_call | solution.py:85
  13.4 4.1 %collective-permute-done.1 = bf16[640,128]{1,0:T(8,128)(2,1)S(1)} collective-permute-done((bf16[640,128]{1,0:T(8,128)(2,1)S(1)}, bf16[640,128]{1,0:T(8,128)(2,1)S(1)}, u32[]{:S(2)}, u32[]{:S(2)}) %collective-permute-start.1) | collective-permute-done | bytes 163872 | tf_op jit(solution)/shard_map/ppermute | solution.py:362
  17.5 1.0 shard_map.76
  18.4 2.2 %collective-permute-start.2 = (bf16[2,256,128]{2,1,0:T(8,128)(2,1)S(1)}, bf16[2,256,128]{2,1,0:T(8,128)(2,1)S(1)}, u32[]{:S(2)}, u32[]{:S(2)}) collective-permute-start(bf16[2,256,128]{2,1,0:T(8,128)(2,1)S(1)} %get-tuple-element.28.cells_ref), channel_id=1, source_target_pairs={{0,4},{4,8},{8,12},{12,16},{16,20},{20,24},{24,28},{28,32},{32,36}... | collective-permute-start | bytes 393224 | tf_op jit(solution)/shard_map/ppermute | solution.py:362
  20.6 1.3 %collective-permute-start.3 = (bf16[2,256,128]{2,1,0:T(8,128)(2,1)S(1)}, bf16[2,256,128]{2,1,0:T(8,128)(2,1)S(1)}, u32[]{:S(2)}, u32[]{:S(2)}) collective-permute-start(bf16[2,256,128]{2,1,0:T(8,128)(2,1)S(1)} %get-tuple-element.28.cells_ref), channel_id=1, source_target_pairs={{4,0},{8,4},{12,8},{16,12},{20,16},{24,20},{28,24},{32,28},{36,32}... | collective-permute-start | bytes 393224 | tf_op jit(solution)/shard_map/ppermute | solution.py:362
  22.8 1.0 reshape.54.cot_ref
  23.8 6.3 %collective-permute-done.3.right_ref = bf16[2,256,128]{2,1,0:T(8,128)(2,1)S(1)} collective-permute-done((bf16[2,256,128]{2,1,0:T(8,128)(2,1)S(1)}, bf16[2,256,128]{2,1,0:T(8,128)(2,1)S(1)}, u32[]{:S(2)}, u32[]{:S(2)}) %collective-permute-start.3) | collective-permute-done | bytes 131104 | tf_op jit(solution)/shard_map/ppermute | solution.py:362
  30.1 6.7 %shard_map.77 = (bf16[64,256]{1,0:T(8,128)(2,1)}, bf16[9,384,128]{2,1,0:T(8,128)(2,1)S(1)}, bf16[9,384,128]{2,1,0:T(8,128)(2,1)S(1)}, bf16[2,256,128]{2,1,0:T(8,128)(2,1)S(1)}) custom-call(s32[1]{0:T(128)} %bitcast.core_ref, bf16[2,256,128]{2,1,0:T(8,128)(2,1)S(1)} %collective-permute-done.2.left_ref, bf16[2,256,128]{2,1,0:T(8,128)(2,1)S(1)} %get-tuple-element.28.cells_ref, ...), custom_call_target="tpu_custom_call" | custom-call | flops 3623878656 | bytes 5000000 | tf_op jit(solution)/shard_map/pallas_call | solution.py:181
  36.7 1.5 %collective-permute-start.5 = (bf16[9,384,128]{2,1,0:T(8,128)(2,1)S(1)}, bf16[9,384,128]{2,1,0:T(8,128)(2,1)S(1)}, u32[]{:S(2)}, u32[]{:S(2)}) collective-permute-start(bf16[9,384,128]{2,1,0:T(8,128)(2,1)S(1)} %get-tuple-element.40), channel_id=1, source_target_pairs={{0,1},{1,0},{2,3},{3,2},{4,5},{5,4},{6,7},{7,6},{8,9},{9,8},{10,11... | collective-permute-start | bytes 2654216 | tf_op jit(solution)/shard_map/ppermute | solution.py:341
  38.2 4.3 %shard_map.78 = (bf16[4,544,256]{2,1,0:T(8,128)(2,1)S(1)}, bf16[9,96,128]{2,1,0:T(8,128)(2,1)S(1)}, bf16[9,96,128]{2,1,0:T(8,128)(2,1)S(1)}) custom-call(s32[1]{0:T(128)} %bitcast.core_ref, bf16[2,256,128]{2,1,0:T(8,128)(2,1)S(1)} %get-tuple-element.30.grad_ref, bf16[2,512,256]{2,1,0:T(8,128)(2,1)S(1)} %get-tuple-element.31.slope_ref, ...), custom_call_target="tpu_custom_call" | custom-call | flops 2415919104 | bytes 6000000 | tf_op jit(solution)/shard_map/pallas_call | solution.py:233
  42.5 1.0 copy-done.2
  43.5 1.5 %collective-permute-done.4.other_a_ref = bf16[9,96,128]{2,1,0:T(8,128)(2,1)S(1)} collective-permute-done((bf16[9,96,128]{2,1,0:T(8,128)(2,1)S(1)}, bf16[9,96,128]{2,1,0:T(8,128)(2,1)S(1)}, u32[]{:S(2)}, u32[]{:S(2)}) %collective-permute-start.4) | collective-permute-done | bytes 221216 | tf_op jit(solution)/shard_map/ppermute | solution.py:341
  45.0 1.2 shard_map.80
  46.2 7.2 %all-to-all-start = ((bf16[16,272,128]{2,1,0:T(8,128)(2,1)}), bf16[16,272,128]{2,1,0:T(8,128)(2,1)}, u32[]{:S(2)}, u32[]{:S(2)}) async-start(bf16[16,272,128]{2,1,0:T(8,128)(2,1)} %bitcast.11), calls=%async_computation | async-start | bytes 2228224 | tf_op jit(solution)/shard_map/all_to_all | solution.py:345
  53.5 1.2 copy-done.3
  54.7 2.6 %shard_map.79 = (bf16[4,512,128]{2,1,0:T(8,128)(2,1)S(1)}, bf16[512,128]{1,0:T(8,128)(2,1)S(1)}, bf16[512,128]{1,0:T(8,128)(2,1)S(1)}) custom-call(bf16[4,544,256]{2,1,0:T(8,128)(2,1)S(1)} %copy-done.3, bf16[9,256,256]{2,1,0:T(8,128)(2,1)S(1)} %copy-done), custom_call_target="tpu_custom_call" | custom-call | flops 2415919104 | bytes 4000000 | tf_op jit(solution)/shard_map/pallas_call | solution.py:270
  57.3 3.5 %collective-permute-start.6 = (bf16[512,128]{1,0:T(8,128)(2,1)S(1)}, bf16[512,128]{1,0:T(8,128)(2,1)S(1)}, u32[]{:S(2)}, u32[]{:S(2)}) collective-permute-start(bf16[512,128]{1,0:T(8,128)(2,1)S(1)} %get-tuple-element.41), channel_id=1, source_target_pairs={{0,4},{4,8},{8,12},{12,16},{16,20},{20,24},{24,28},{28,32},{32,36}... | collective-permute-start | bytes 393224 | tf_op jit(solution)/shard_map/ppermute | solution.py:362
  60.9 1.3 %collective-permute-start.7 = (bf16[512,128]{1,0:T(8,128)(2,1)S(1)}, bf16[512,128]{1,0:T(8,128)(2,1)S(1)}, u32[]{:S(2)}, u32[]{:S(2)}) collective-permute-start(bf16[512,128]{1,0:T(8,128)(2,1)S(1)} %get-tuple-element.42), channel_id=1, source_target_pairs={{4,0},{8,4},{12,8},{16,12},{20,16},{24,20},{28,24},{32,28},{36,32}... | collective-permute-start | bytes 393224 | tf_op jit(solution)/shard_map/ppermute | solution.py:362
  62.2 1.1 collective-permute-done.6
  63.3 3.9 %collective-permute-done.7 = bf16[512,128]{1,0:T(8,128)(2,1)S(1)} collective-permute-done((bf16[512,128]{1,0:T(8,128)(2,1)S(1)}, bf16[512,128]{1,0:T(8,128)(2,1)S(1)}, u32[]{:S(2)}, u32[]{:S(2)}) %collective-permute-start.7) | collective-permute-done | bytes 131104 | tf_op jit(solution)/shard_map/ppermute | solution.py:362
  67.2 3.5 %all-to-all-done = bf16[16,272,128]{2,1,0:T(8,128)(2,1)} async-done(((bf16[16,272,128]{2,1,0:T(8,128)(2,1)}), bf16[16,272,128]{2,1,0:T(8,128)(2,1)}, u32[]{:S(2)}, u32[]{:S(2)}) %all-to-all-start) | async-done | bytes 1114144 | tf_op jit(solution)/shard_map/all_to_all | solution.py:345
  70.7 1.4 %reduce_sum.24 = bf16[272,128]{1,0:T(8,128)(2,1)S(1)} reduce(bf16[16,272,128]{2,1,0:T(8,128)(2,1)} %all-to-all-done, bf16[]{:T(256)} %constant.21.clone.1), dimensions={0}, to_apply=%region_0.1 | reduce | flops 522240 | bytes 1183746 | tf_op jit(solution)/shard_map/reduce_sum | solution.py:349
  72.2 26.0 %all_to_all.15 = bf16[8,272,128]{2,1,0:T(8,128)(2,1)S(1)} all-to-all(bf16[8,272,128]{2,1,0:T(8,128)(2,1)S(1)} %broadcast_in_dim.33), channel_id=1, replica_groups={{0,4,8,12,2,6,10,14},{1,5,9,13,3,7,11,15},{16,20,24,28,18,22,26,30},{17..., dimensions={0} | all-to-all | bytes 1114112 | tf_op jit(solution)/shard_map/all_to_all | solution.py:345
  98.4 20.4 %all_to_all.16 = bf16[16,272,128]{2,1,0:T(8,128)(2,1)S(1)} all-to-all(bf16[16,272,128]{2,1,0:T(8,128)(2,1)S(1)} %broadcast_in_dim.34), channel_id=1, replica_groups={{0,16,32,48,64,80,96,112,128,144,160,176,192,208,224,240},{1,17,33,49,6..., dimensions={0} | all-to-all | bytes 2228224 | tf_op jit(solution)/shard_map/all_to_all | solution.py:345
  118.8 5.2 %collective-permute-start.8 = (bf16[4352,128]{1,0:T(8,128)(2,1)S(1)}, bf16[4352,128]{1,0:T(8,128)(2,1)S(1)}, u32[]{:S(2)}, u32[]{:S(2)}) collective-permute-start(bf16[4352,128]{1,0:T(8,128)(2,1)S(1)} %bitcast.32), channel_id=1, source_target_pairs={{0,1},{1,0},{2,3},{3,2},{4,5},{5,4},{6,7},{7,6},{8,9},{9,8},{10,11... | collective-permute-start | bytes 3342344 | tf_op jit(solution)/shard_map/ppermute | solution.py:341
  124.2 1.4 %reshape.57 = bf16[1,4,32,32,64]{4,3,2,1,0:T(8,128)(2,1)} reshape(bf16[4,512,128]{2,1,0:T(8,128)(2,1)S(1)} %pad_maximum_fusion) | data formatting | bytes 1048576 | tf_op jit(solution)/shard_map/reshape | solution.py:396
  125.6 0.8 collective-permute-done.8.away_ref
  126.4 2.4 %shard_map.81 = (f32[9,2,96,128]{3,2,1,0:T(8,128)}, f32[9,384,256]{2,1,0:T(8,128)}) custom-call(s32[1]{0:T(128)} %bitcast.core_ref, bf16[4352,128]{1,0:T(8,128)(2,1)S(1)} %bitcast.33, bf16[4352,128]{1,0:T(8,128)(2,1)S(1)} %collective-permute-done.8.away_ref), custom_call_target="tpu_custom_call" | custom-call | bytes 7000000 | tf_op jit(solution)/shard_map/pallas_call | solution.py:322
  (37 shorter events, 2.2 us)
Async XLA Ops:
  0.6 7.3 %copy-start.4 = (bf16[1,4,32,32,64]{4,3,2,1,0:T(8,128)(2,1)S(1)}, bf16[1,4,32,32,64]{4,3,2,1,0:T(8,128)(2,1)}, u32[]{:S(2)}) copy-start(bf16[1,4,32,32,64]{4,3,2,1,0:T(8,128)(2,1)} %param.4) | copy-start | bytes 1572868
  0.6 1.5 %copy-start.6 = (bf16[1,1,8,8,256]{4,3,2,1,0:T(8,128)(2,1)S(1)}, bf16[1,1,8,8,256]{4,3,2,1,0:T(8,128)(2,1)}, u32[]{:S(2)}) copy-start(bf16[1,1,8,8,256]{4,3,2,1,0:T(8,128)(2,1)} %param.7) | copy-start | bytes 98308
  1.8 6.6 %copy-start.5 = (bf16[3,3,3,64,128]{4,3,2,1,0:T(8,128)(2,1)S(1)}, bf16[3,3,3,64,128]{4,3,2,1,0:T(8,128)(2,1)}, u32[]{:S(2)}) copy-start(bf16[3,3,3,64,128]{4,3,2,1,0:T(8,128)(2,1)} %param.5) | copy-start | bytes 1327108
  2.2 11.1 %collective-permute-start = (bf16[640,128]{1,0:T(8,128)(2,1)S(1)}, bf16[640,128]{1,0:T(8,128)(2,1)S(1)}, u32[]{:S(2)}, u32[]{:S(2)}) collective-permute-start(bf16[640,128]{1,0:T(8,128)(2,1)S(1)} %get-tuple-element.60), channel_id=1, source_target_pairs={{0,4},{4,8},{8,12},{12,16},{16,20},{20,24},{24,28},{28,32},{32,36}... | collective-permute-start | bytes 491528 | tf_op jit(solution)/shard_map/ppermute | solution.py:362
  6.6 10.9 %collective-permute-start.1 = (bf16[640,128]{1,0:T(8,128)(2,1)S(1)}, bf16[640,128]{1,0:T(8,128)(2,1)S(1)}, u32[]{:S(2)}, u32[]{:S(2)}) collective-permute-start(bf16[640,128]{1,0:T(8,128)(2,1)S(1)} %get-tuple-element.59), channel_id=1, source_target_pairs={{4,0},{8,4},{12,8},{16,12},{20,16},{24,20},{28,24},{32,28},{36,32}... | collective-permute-start | bytes 491528 | tf_op jit(solution)/shard_map/ppermute | solution.py:362
  9.6 7.8 %copy-start = (bf16[9,256,256]{2,1,0:T(8,128)(2,1)S(1)}, bf16[9,256,256]{2,1,0:T(8,128)(2,1)}, u32[]{:S(2)}) copy-start(bf16[9,256,256]{2,1,0:T(8,128)(2,1)} %maximum_maximum_fusion.weight_ref) | copy-start | bytes 3538948
  13.3 5.1 %copy-start.1 = (bf16[4,544,256]{2,1,0:T(8,128)(2,1)}, bf16[4,544,256]{2,1,0:T(8,128)(2,1)S(1)}, u32[]{:S(2)}) copy-start(bf16[4,544,256]{2,1,0:T(8,128)(2,1)S(1)} %get-tuple-element.33.window_ref) | copy-start | bytes 3342340
  18.4 5.4 %collective-permute-start.2 = (bf16[2,256,128]{2,1,0:T(8,128)(2,1)S(1)}, bf16[2,256,128]{2,1,0:T(8,128)(2,1)S(1)}, u32[]{:S(2)}, u32[]{:S(2)}) collective-permute-start(bf16[2,256,128]{2,1,0:T(8,128)(2,1)S(1)} %get-tuple-element.28.cells_ref), channel_id=1, source_target_pairs={{0,4},{4,8},{8,12},{12,16},{16,20},{20,24},{24,28},{28,32},{32,36}... | collective-permute-start | bytes 393224 | tf_op jit(solution)/shard_map/ppermute | solution.py:362
  20.6 9.4 %collective-permute-start.3 = (bf16[2,256,128]{2,1,0:T(8,128)(2,1)S(1)}, bf16[2,256,128]{2,1,0:T(8,128)(2,1)S(1)}, u32[]{:S(2)}, u32[]{:S(2)}) collective-permute-start(bf16[2,256,128]{2,1,0:T(8,128)(2,1)S(1)} %get-tuple-element.28.cells_ref), channel_id=1, source_target_pairs={{4,0},{8,4},{12,8},{16,12},{20,16},{24,20},{28,24},{32,28},{36,32}... | collective-permute-start | bytes 393224 | tf_op jit(solution)/shard_map/ppermute | solution.py:362
  36.7 8.3 %collective-permute-start.5 = (bf16[9,384,128]{2,1,0:T(8,128)(2,1)S(1)}, bf16[9,384,128]{2,1,0:T(8,128)(2,1)S(1)}, u32[]{:S(2)}, u32[]{:S(2)}) collective-permute-start(bf16[9,384,128]{2,1,0:T(8,128)(2,1)S(1)} %get-tuple-element.40), channel_id=1, source_target_pairs={{0,1},{1,0},{2,3},{3,2},{4,5},{5,4},{6,7},{7,6},{8,9},{9,8},{10,11... | collective-permute-start | bytes 2654216 | tf_op jit(solution)/shard_map/ppermute | solution.py:341
  42.5 1.0 copy-start.2
  43.5 1.5 %collective-permute-start.4 = (bf16[9,96,128]{2,1,0:T(8,128)(2,1)S(1)}, bf16[9,96,128]{2,1,0:T(8,128)(2,1)S(1)}, u32[]{:S(2)}, u32[]{:S(2)}) collective-permute-start(bf16[9,96,128]{2,1,0:T(8,128)(2,1)S(1)} %get-tuple-element.38), channel_id=1, source_target_pairs={{0,1},{1,0},{2,3},{3,2},{4,5},{5,4},{6,7},{7,6},{8,9},{9,8},{10,11... | collective-permute-start | bytes 663560 | tf_op jit(solution)/shard_map/ppermute | solution.py:341
  46.2 24.5 %all-to-all-start = ((bf16[16,272,128]{2,1,0:T(8,128)(2,1)}), bf16[16,272,128]{2,1,0:T(8,128)(2,1)}, u32[]{:S(2)}, u32[]{:S(2)}) async-start(bf16[16,272,128]{2,1,0:T(8,128)(2,1)} %bitcast.11), calls=%async_computation | async-start | bytes 2228224 | tf_op jit(solution)/shard_map/all_to_all | solution.py:345
  53.4 1.3 copy-start.3
  57.3 5.9 %collective-permute-start.6 = (bf16[512,128]{1,0:T(8,128)(2,1)S(1)}, bf16[512,128]{1,0:T(8,128)(2,1)S(1)}, u32[]{:S(2)}, u32[]{:S(2)}) collective-permute-start(bf16[512,128]{1,0:T(8,128)(2,1)S(1)} %get-tuple-element.41), channel_id=1, source_target_pairs={{0,4},{4,8},{8,12},{12,16},{16,20},{20,24},{24,28},{28,32},{32,36}... | collective-permute-start | bytes 393224 | tf_op jit(solution)/shard_map/ppermute | solution.py:362
  60.9 6.3 %collective-permute-start.7 = (bf16[512,128]{1,0:T(8,128)(2,1)S(1)}, bf16[512,128]{1,0:T(8,128)(2,1)S(1)}, u32[]{:S(2)}, u32[]{:S(2)}) collective-permute-start(bf16[512,128]{1,0:T(8,128)(2,1)S(1)} %get-tuple-element.42), channel_id=1, source_target_pairs={{4,0},{8,4},{12,8},{16,12},{20,16},{24,20},{28,24},{32,28},{36,32}... | collective-permute-start | bytes 393224 | tf_op jit(solution)/shard_map/ppermute | solution.py:362
  118.8 7.6 %collective-permute-start.8 = (bf16[4352,128]{1,0:T(8,128)(2,1)S(1)}, bf16[4352,128]{1,0:T(8,128)(2,1)S(1)}, u32[]{:S(2)}, u32[]{:S(2)}) collective-permute-start(bf16[4352,128]{1,0:T(8,128)(2,1)S(1)} %bitcast.32), channel_id=1, source_target_pairs={{0,1},{1,0},{2,3},{3,2},{4,5},{5,4},{6,7},{7,6},{8,9},{9,8},{10,11... | collective-permute-start | bytes 3342344 | tf_op jit(solution)/shard_map/ppermute | solution.py:341

commit v6 on v5

--- a/solution.py
+++ b/solution.py
@@ -349,12 +349,6 @@
     return jnp.sum(blocks.astype(F32), axis=0).astype(BF16)
 
 
-def reduce_over_chips(blocks):
-    part = total_of(blocks)
-    part = total_of(exchange(jnp.broadcast_to(part, (8, 272, 128)), ALONG))
-    return exchange(jnp.broadcast_to(part, (16, 272, 128)), ACROSS).reshape(4352, 128)
-
-
 def neighbours(to_left, to_right):
     count = lax.axis_size("slab")
     up = [(i, i + 1) for i in range(count - 1)]
@@ -381,11 +375,15 @@
     grad_pre, keep_a, send_a = kernel_a(core, grad_pooled, slope_a, ends, window, sides)
     other_a = other_core(send_a)
     inner, to_left, to_right = back_a(grad_pre, pair_weight)
-    from_left, from_right = neighbours(to_left, to_right)
     rows = merge(keep_a, other_a, keep_b, other_b)
     blocks = exchange(rows.reshape(16, 272, 128), ACROSS)
+    blocks, to_left, to_right = lax.optimization_barrier((blocks, to_left, to_right))
+    blocks = exchange(jnp.broadcast_to(total_of(blocks), (8, 272, 128)), ALONG)
+    blocks, to_left, to_right = lax.optimization_barrier((blocks, to_left, to_right))
+    from_left, from_right = neighbours(to_left, to_right)
+    blocks = exchange(jnp.broadcast_to(total_of(blocks), (16, 272, 128)), ACROSS)
     blocks, from_left, from_right = lax.optimization_barrier((blocks, from_left, from_right))
-    mine = reduce_over_chips(blocks)
+    mine = blocks.reshape(4352, 128)
     away = other_core(mine)
     first = (inner[:1].astype(F32) + from_left.astype(F32)).astype(BF16)
     last = (inner[3:].astype(F32) + from_right.astype(F32)).astype(BF16)

time: 129 us -> 130 us (level)
  blocking collectives: 46.4 us -> 26.2 us
  waiting for transfers between devices: 21.2 us -> 35.5 us
  starting transfers between devices: 27.8 us -> 34 us
    all_to_all x2 -> x1, blocking collectives: 46.4 us -> 26.2 us  [exchange(): lax.all_to_all(blocks, AXES, 0, 0, axis_index_groups=groups, tiled=True)]
    all_to_all x1 -> x2, waiting for transfers between devices: 3.54 us -> 16.8 us  [exchange(): lax.all_to_all(blocks, AXES, 0, 0, axis_index_groups=groups, tiled=True)]
    all_to_all x1 -> x2, starting transfers between devices: 7.19 us -> 11.7 us  [exchange(): lax.all_to_all(blocks, AXES, 0, 0, axis_index_groups=groups, tiled=True)]
    ppermute x3, starting transfers between devices: 6.69 us -> 9.39 us  [other_core(): return lax.ppermute(value, AXES, CORES)]
    ppermute x3, waiting for transfers between devices: 14.2 us -> 15.8 us  [neighbours(): lax.ppermute(to_left, 'slab', down)]
  transfers between devices with their start and end apart: 10 -> 11, of which waited for: 7 -> 8; matrix products, arithmetic and copies ran while one was open for 4% -> 4% of each run, Pallas kernels for 8% -> 8%
where the time goes in v6:
time: 130 us; the launch traced here: 129 us
  waiting for transfers between devices  35.5 us (27%)
  starting transfers between devices  34 us (26%)
  blocking collectives  26.2 us (20%)
  Pallas kernels  22 us (17%)
  local copies, waits for them, and re-layouts  8.7 us (7%)
  other arithmetic  1.55 us (1%)
    all_to_all x1, blocking collectives, exchange(): lax.all_to_all(blocks, AXES, 0, 0, axis_index_groups=groups, tiled=True)  26.2 us
    all_to_all x2, waiting for transfers between devices, exchange(): lax.all_to_all(blocks, AXES, 0, 0, axis_index_groups=groups, tiled=True)  16.8 us
    ppermute x3, waiting for transfers between devices, neighbours(): lax.ppermute(to_left, 'slab', down)  15.8 us
    all_to_all x2, starting transfers between devices, exchange(): lax.all_to_all(blocks, AXES, 0, 0, axis_index_groups=groups, tiled=True)  11.7 us
    ppermute x3, starting transfers between devices, other_core(): return lax.ppermute(value, AXES, CORES)  9.39 us
    ppermute x3, starting transfers between devices, neighbours(): lax.ppermute(to_right, 'slab', up)  9.07 us
    pallas_call x1, Pallas kernels, block_b(): pl.pallas_call(block_b_kernel, in_specs=[SCALAR] + [WHOLE] * 5, out_shape...  6.66 us
    pallas_call x1, Pallas kernels, kernel_a(): pl.pallas_call(kernel_a_kernel, in_specs=[SCALAR] + [WHOLE] * 5, out_spec...  4.34 us
  transfers between devices with their start and end apart: 11, of which 8 were waited for; matrix products, arithmetic and copies ran while one was open for 4% of the time, Pallas kernels for 8%

profile of v6, /device:TPU:1, one launch (start us, length us, event | category | flops | bytes accessed | tf_op | source)
XLA Modules:
  0.0 128.9 jit_solution(4064413074291106113)
XLA Ops:
  0.7 1.2 fusion.2
  2.2 4.4 %collective-permute-start = (bf16[640,128]{1,0:T(8,128)(2,1)S(1)}, bf16[640,128]{1,0:T(8,128)(2,1)S(1)}, u32[]{:S(2)}, u32[]{:S(2)}) collective-permute-start(bf16[640,128]{1,0:T(8,128)(2,1)S(1)} %get-tuple-element.72), channel_id=1, source_target_pairs={{0,4},{4,8},{8,12},{12,16},{16,20},{20,24},{24,28},{28,32},{32,36}... | collective-permute-start | bytes 491528 | tf_op jit(solution)/shard_map/ppermute | solution.py:356
  6.6 1.3 %collective-permute-start.1 = (bf16[640,128]{1,0:T(8,128)(2,1)S(1)}, bf16[640,128]{1,0:T(8,128)(2,1)S(1)}, u32[]{:S(2)}, u32[]{:S(2)}) collective-permute-start(bf16[640,128]{1,0:T(8,128)(2,1)S(1)} %get-tuple-element.71), channel_id=1, source_target_pairs={{4,0},{8,4},{12,8},{16,12},{20,16},{24,20},{28,24},{32,28},{36,32}... | collective-permute-start | bytes 491528 | tf_op jit(solution)/shard_map/ppermute | solution.py:356
  8.5 1.1 maximum_maximum_fusion.weight_ref
  9.6 3.7 %shard_map.75 = (bf16[4,544,256]{2,1,0:T(8,128)(2,1)S(1)}, f32[2,512,256]{2,1,0:T(8,128)S(1)}, bf16[2,512,256]{2,1,0:T(8,128)(2,1)S(1)}, f32[2,256,128]{2,1,0:T(8,128)S(1)}) custom-call(bf16[4,512,128]{2,1,0:T(8,128)(2,1)S(1)} %reshape.52.cells_ref, bf16[9,256,256]{2,1,0:T(8,128)(2,1)} %maximum_maximum_fusion.weight_ref), custom_call_target="tpu_custom_call" | custom-call | flops 2415919104 | bytes 6000000 | tf_op jit(solution)/shard_map/pallas_call | solution.py:85
  13.4 4.1 %collective-permute-done.1 = bf16[640,128]{1,0:T(8,128)(2,1)S(1)} collective-permute-done((bf16[640,128]{1,0:T(8,128)(2,1)S(1)}, bf16[640,128]{1,0:T(8,128)(2,1)S(1)}, u32[]{:S(2)}, u32[]{:S(2)}) %collective-permute-start.1) | collective-permute-done | bytes 163872 | tf_op jit(solution)/shard_map/ppermute | solution.py:356
  17.5 1.0 shard_map.76
  18.4 2.2 %collective-permute-start.2 = (bf16[2,256,128]{2,1,0:T(8,128)(2,1)S(1)}, bf16[2,256,128]{2,1,0:T(8,128)(2,1)S(1)}, u32[]{:S(2)}, u32[]{:S(2)}) collective-permute-start(bf16[2,256,128]{2,1,0:T(8,128)(2,1)S(1)} %get-tuple-element.34.cells_ref), channel_id=1, source_target_pairs={{0,4},{4,8},{8,12},{12,16},{16,20},{20,24},{24,28},{28,32},{32,36}... | collective-permute-start | bytes 393224 | tf_op jit(solution)/shard_map/ppermute | solution.py:356
  20.6 1.3 %collective-permute-start.3 = (bf16[2,256,128]{2,1,0:T(8,128)(2,1)S(1)}, bf16[2,256,128]{2,1,0:T(8,128)(2,1)S(1)}, u32[]{:S(2)}, u32[]{:S(2)}) collective-permute-start(bf16[2,256,128]{2,1,0:T(8,128)(2,1)S(1)} %get-tuple-element.34.cells_ref), channel_id=1, source_target_pairs={{4,0},{8,4},{12,8},{16,12},{20,16},{24,20},{28,24},{32,28},{36,32}... | collective-permute-start | bytes 393224 | tf_op jit(solution)/shard_map/ppermute | solution.py:356
  22.8 1.0 reshape.54.cot_ref
  23.8 6.3 %collective-permute-done.3.right_ref = bf16[2,256,128]{2,1,0:T(8,128)(2,1)S(1)} collective-permute-done((bf16[2,256,128]{2,1,0:T(8,128)(2,1)S(1)}, bf16[2,256,128]{2,1,0:T(8,128)(2,1)S(1)}, u32[]{:S(2)}, u32[]{:S(2)}) %collective-permute-start.3) | collective-permute-done | bytes 131104 | tf_op jit(solution)/shard_map/ppermute | solution.py:356
  30.1 6.7 %shard_map.77 = (bf16[64,256]{1,0:T(8,128)(2,1)}, bf16[9,384,128]{2,1,0:T(8,128)(2,1)S(1)}, bf16[9,384,128]{2,1,0:T(8,128)(2,1)S(1)}, bf16[2,256,128]{2,1,0:T(8,128)(2,1)S(1)}) custom-call(s32[1]{0:T(128)} %bitcast.core_ref, bf16[2,256,128]{2,1,0:T(8,128)(2,1)S(1)} %collective-permute-done.2.left_ref, bf16[2,256,128]{2,1,0:T(8,128)(2,1)S(1)} %get-tuple-element.34.cells_ref, ...), custom_call_target="tpu_custom_call" | custom-call | flops 3623878656 | bytes 5000000 | tf_op jit(solution)/shard_map/pallas_call | solution.py:181
  36.7 1.5 %collective-permute-start.5 = (bf16[9,384,128]{2,1,0:T(8,128)(2,1)S(1)}, bf16[9,384,128]{2,1,0:T(8,128)(2,1)S(1)}, u32[]{:S(2)}, u32[]{:S(2)}) collective-permute-start(bf16[9,384,128]{2,1,0:T(8,128)(2,1)S(1)} %get-tuple-element.46), channel_id=1, source_target_pairs={{0,1},{1,0},{2,3},{3,2},{4,5},{5,4},{6,7},{7,6},{8,9},{9,8},{10,11... | collective-permute-start | bytes 2654216 | tf_op jit(solution)/shard_map/ppermute | solution.py:341
  38.2 4.3 %shard_map.78 = (bf16[4,544,256]{2,1,0:T(8,128)(2,1)S(1)}, bf16[9,96,128]{2,1,0:T(8,128)(2,1)S(1)}, bf16[9,96,128]{2,1,0:T(8,128)(2,1)S(1)}) custom-call(s32[1]{0:T(128)} %bitcast.core_ref, bf16[2,256,128]{2,1,0:T(8,128)(2,1)S(1)} %get-tuple-element.36.grad_ref, bf16[2,512,256]{2,1,0:T(8,128)(2,1)S(1)} %get-tuple-element.37.slope_ref, ...), custom_call_target="tpu_custom_call" | custom-call | flops 2415919104 | bytes 6000000 | tf_op jit(solution)/shard_map/pallas_call | solution.py:233
  42.5 1.0 copy-done.2
  43.5 1.5 %collective-permute-done.4.other_a_ref = bf16[9,96,128]{2,1,0:T(8,128)(2,1)S(1)} collective-permute-done((bf16[9,96,128]{2,1,0:T(8,128)(2,1)S(1)}, bf16[9,96,128]{2,1,0:T(8,128)(2,1)S(1)}, u32[]{:S(2)}, u32[]{:S(2)}) %collective-permute-start.4) | collective-permute-done | bytes 221216 | tf_op jit(solution)/shard_map/ppermute | solution.py:341
  45.0 1.3 shard_map.80
  46.3 7.1 %all-to-all-start = ((bf16[16,272,128]{2,1,0:T(8,128)(2,1)}), bf16[16,272,128]{2,1,0:T(8,128)(2,1)S(1)}, u32[]{:S(2)}, u32[]{:S(2)}) async-start(bf16[16,272,128]{2,1,0:T(8,128)(2,1)} %bitcast.11), calls=%async_computation | async-start | bytes 2228224 | tf_op jit(solution)/shard_map/all_to_all | solution.py:345
  53.4 1.2 copy-done.3
  54.7 2.6 %shard_map.79 = (bf16[4,512,128]{2,1,0:T(8,128)(2,1)S(1)}, bf16[512,128]{1,0:T(8,128)(2,1)S(1)}, bf16[512,128]{1,0:T(8,128)(2,1)S(1)}) custom-call(bf16[4,544,256]{2,1,0:T(8,128)(2,1)S(1)} %copy-done.3, bf16[9,256,256]{2,1,0:T(8,128)(2,1)S(1)} %copy-done), custom_call_target="tpu_custom_call" | custom-call | flops 2415919104 | bytes 4000000 | tf_op jit(solution)/shard_map/pallas_call | solution.py:270
  57.3 13.1 %all-to-all-done = bf16[16,272,128]{2,1,0:T(8,128)(2,1)S(1)} async-done(((bf16[16,272,128]{2,1,0:T(8,128)(2,1)}), bf16[16,272,128]{2,1,0:T(8,128)(2,1)S(1)}, u32[]{:S(2)}, u32[]{:S(2)}) %all-to-all-start) | async-done | bytes 1114144 | tf_op jit(solution)/shard_map/all_to_all | solution.py:345
  70.6 26.2 %all_to_all.15 = bf16[8,272,128]{2,1,0:T(8,128)(2,1)S(1)} all-to-all(bf16[8,272,128]{2,1,0:T(8,128)(2,1)S(1)} %broadcast_in_dim.29), channel_id=1, replica_groups={{0,4,8,12,2,6,10,14},{1,5,9,13,3,7,11,15},{16,20,24,28,18,22,26,30},{17..., dimensions={0} | all-to-all | bytes 1114112 | tf_op jit(solution)/shard_map/all_to_all | solution.py:345
  96.9 1.1 broadcast_in_dim.30
  98.1 4.5 %all-to-all-start.2 = ((bf16[16,272,128]{2,1,0:T(8,128)(2,1)}), bf16[16,272,128]{2,1,0:T(8,128)(2,1)S(1)}, u32[]{:S(2)}, u32[]{:S(2)}) async-start(bf16[16,272,128]{2,1,0:T(8,128)(2,1)} %broadcast_in_dim.30), calls=%async_computation.2 | async-start | bytes 2228224 | tf_op jit(solution)/shard_map/all_to_all | solution.py:345
  102.6 2.5 %collective-permute-start.6 = (bf16[512,128]{1,0:T(8,128)(2,1)S(1)}, bf16[512,128]{1,0:T(8,128)(2,1)S(1)}, u32[]{:S(2)}, u32[]{:S(2)}) collective-permute-start(bf16[512,128]{1,0:T(8,128)(2,1)S(1)} %get-tuple-element.53), channel_id=1, source_target_pairs={{0,4},{4,8},{8,12},{12,16},{16,20},{20,24},{24,28},{28,32},{32,36}... | collective-permute-start | bytes 393224 | tf_op jit(solution)/shard_map/ppermute | solution.py:356
  105.1 1.3 %collective-permute-start.7 = (bf16[512,128]{1,0:T(8,128)(2,1)S(1)}, bf16[512,128]{1,0:T(8,128)(2,1)S(1)}, u32[]{:S(2)}, u32[]{:S(2)}) collective-permute-start(bf16[512,128]{1,0:T(8,128)(2,1)S(1)} %get-tuple-element.54), channel_id=1, source_target_pairs={{4,0},{8,4},{12,8},{16,12},{20,16},{24,20},{28,24},{32,28},{36,32}... | collective-permute-start | bytes 393224 | tf_op jit(solution)/shard_map/ppermute | solution.py:356
  107.0 5.5 %collective-permute-done.7 = bf16[512,128]{1,0:T(8,128)(2,1)S(1)} collective-permute-done((bf16[512,128]{1,0:T(8,128)(2,1)S(1)}, bf16[512,128]{1,0:T(8,128)(2,1)S(1)}, u32[]{:S(2)}, u32[]{:S(2)}) %collective-permute-start.7) | collective-permute-done | bytes 131104 | tf_op jit(solution)/shard_map/ppermute | solution.py:356
  112.5 3.7 %all-to-all-done.2 = bf16[16,272,128]{2,1,0:T(8,128)(2,1)S(1)} async-done(((bf16[16,272,128]{2,1,0:T(8,128)(2,1)}), bf16[16,272,128]{2,1,0:T(8,128)(2,1)S(1)}, u32[]{:S(2)}, u32[]{:S(2)}) %all-to-all-start.2) | async-done | bytes 1114144 | tf_op jit(solution)/shard_map/all_to_all | solution.py:345
  116.2 7.9 %collective-permute-start.8 = (bf16[4352,128]{1,0:T(8,128)(2,1)S(1)}, bf16[4352,128]{1,0:T(8,128)(2,1)S(1)}, u32[]{:S(2)}, u32[]{:S(2)}) collective-permute-start(bf16[4352,128]{1,0:T(8,128)(2,1)S(1)} %bitcast.32), channel_id=1, source_target_pairs={{0,1},{1,0},{2,3},{3,2},{4,5},{5,4},{6,7},{7,6},{8,9},{9,8},{10,11... | collective-permute-start | bytes 3342344 | tf_op jit(solution)/shard_map/ppermute | solution.py:341
  124.3 1.4 %reshape.57 = bf16[1,4,32,32,64]{4,3,2,1,0:T(8,128)(2,1)} reshape(bf16[4,512,128]{2,1,0:T(8,128)(2,1)S(1)} %pad_maximum_fusion) | data formatting | bytes 1048576 | tf_op jit(solution)/shard_map/reshape | solution.py:394
  125.7 0.8 collective-permute-done.8.away_ref
  126.5 2.4 %shard_map.81 = (f32[9,2,96,128]{3,2,1,0:T(8,128)}, f32[9,384,256]{2,1,0:T(8,128)}) custom-call(s32[1]{0:T(128)} %bitcast.core_ref, bf16[4352,128]{1,0:T(8,128)(2,1)S(1)} %bitcast.33, bf16[4352,128]{1,0:T(8,128)(2,1)S(1)} %collective-permute-done.8.away_ref), custom_call_target="tpu_custom_call" | custom-call | bytes 7000000 | tf_op jit(solution)/shard_map/pallas_call | solution.py:322
  (38 shorter events, 2.9 us)
Async XLA Ops:
  0.6 7.3 %copy-start.4 = (bf16[1,4,32,32,64]{4,3,2,1,0:T(8,128)(2,1)S(1)}, bf16[1,4,32,32,64]{4,3,2,1,0:T(8,128)(2,1)}, u32[]{:S(2)}) copy-start(bf16[1,4,32,32,64]{4,3,2,1,0:T(8,128)(2,1)} %param.4) | copy-start | bytes 1572868
  0.6 1.5 %copy-start.6 = (bf16[1,1,8,8,256]{4,3,2,1,0:T(8,128)(2,1)S(1)}, bf16[1,1,8,8,256]{4,3,2,1,0:T(8,128)(2,1)}, u32[]{:S(2)}) copy-start(bf16[1,1,8,8,256]{4,3,2,1,0:T(8,128)(2,1)} %param.7) | copy-start | bytes 98308
  1.8 6.6 %copy-start.5 = (bf16[3,3,3,64,128]{4,3,2,1,0:T(8,128)(2,1)S(1)}, bf16[3,3,3,64,128]{4,3,2,1,0:T(8,128)(2,1)}, u32[]{:S(2)}) copy-start(bf16[3,3,3,64,128]{4,3,2,1,0:T(8,128)(2,1)} %param.5) | copy-start | bytes 1327108
  2.2 11.1 %collective-permute-start = (bf16[640,128]{1,0:T(8,128)(2,1)S(1)}, bf16[640,128]{1,0:T(8,128)(2,1)S(1)}, u32[]{:S(2)}, u32[]{:S(2)}) collective-permute-start(bf16[640,128]{1,0:T(8,128)(2,1)S(1)} %get-tuple-element.72), channel_id=1, source_target_pairs={{0,4},{4,8},{8,12},{12,16},{16,20},{20,24},{24,28},{28,32},{32,36}... | collective-permute-start | bytes 491528 | tf_op jit(solution)/shard_map/ppermute | solution.py:356
  6.6 10.9 %collective-permute-start.1 = (bf16[640,128]{1,0:T(8,128)(2,1)S(1)}, bf16[640,128]{1,0:T(8,128)(2,1)S(1)}, u32[]{:S(2)}, u32[]{:S(2)}) collective-permute-start(bf16[640,128]{1,0:T(8,128)(2,1)S(1)} %get-tuple-element.71), channel_id=1, source_target_pairs={{4,0},{8,4},{12,8},{16,12},{20,16},{24,20},{28,24},{32,28},{36,32}... | collective-permute-start | bytes 491528 | tf_op jit(solution)/shard_map/ppermute | solution.py:356
  9.6 7.8 %copy-start = (bf16[9,256,256]{2,1,0:T(8,128)(2,1)S(1)}, bf16[9,256,256]{2,1,0:T(8,128)(2,1)}, u32[]{:S(2)}) copy-start(bf16[9,256,256]{2,1,0:T(8,128)(2,1)} %maximum_maximum_fusion.weight_ref) | copy-start | bytes 3538948
  13.3 5.1 %copy-start.1 = (bf16[4,544,256]{2,1,0:T(8,128)(2,1)}, bf16[4,544,256]{2,1,0:T(8,128)(2,1)S(1)}, u32[]{:S(2)}) copy-start(bf16[4,544,256]{2,1,0:T(8,128)(2,1)S(1)} %get-tuple-element.39.window_ref) | copy-start | bytes 3342340
  18.4 5.4 %collective-permute-start.2 = (bf16[2,256,128]{2,1,0:T(8,128)(2,1)S(1)}, bf16[2,256,128]{2,1,0:T(8,128)(2,1)S(1)}, u32[]{:S(2)}, u32[]{:S(2)}) collective-permute-start(bf16[2,256,128]{2,1,0:T(8,128)(2,1)S(1)} %get-tuple-element.34.cells_ref), channel_id=1, source_target_pairs={{0,4},{4,8},{8,12},{12,16},{16,20},{20,24},{24,28},{28,32},{32,36}... | collective-permute-start | bytes 393224 | tf_op jit(solution)/shard_map/ppermute | solution.py:356
  20.6 9.4 %collective-permute-start.3 = (bf16[2,256,128]{2,1,0:T(8,128)(2,1)S(1)}, bf16[2,256,128]{2,1,0:T(8,128)(2,1)S(1)}, u32[]{:S(2)}, u32[]{:S(2)}) collective-permute-start(bf16[2,256,128]{2,1,0:T(8,128)(2,1)S(1)} %get-tuple-element.34.cells_ref), channel_id=1, source_target_pairs={{4,0},{8,4},{12,8},{16,12},{20,16},{24,20},{28,24},{32,28},{36,32}... | collective-permute-start | bytes 393224 | tf_op jit(solution)/shard_map/ppermute | solution.py:356
  36.7 8.3 %collective-permute-start.5 = (bf16[9,384,128]{2,1,0:T(8,128)(2,1)S(1)}, bf16[9,384,128]{2,1,0:T(8,128)(2,1)S(1)}, u32[]{:S(2)}, u32[]{:S(2)}) collective-permute-start(bf16[9,384,128]{2,1,0:T(8,128)(2,1)S(1)} %get-tuple-element.46), channel_id=1, source_target_pairs={{0,1},{1,0},{2,3},{3,2},{4,5},{5,4},{6,7},{7,6},{8,9},{9,8},{10,11... | collective-permute-start | bytes 2654216 | tf_op jit(solution)/shard_map/ppermute | solution.py:341
  42.5 1.0 copy-start.2
  43.5 1.5 %collective-permute-start.4 = (bf16[9,96,128]{2,1,0:T(8,128)(2,1)S(1)}, bf16[9,96,128]{2,1,0:T(8,128)(2,1)S(1)}, u32[]{:S(2)}, u32[]{:S(2)}) collective-permute-start(bf16[9,96,128]{2,1,0:T(8,128)(2,1)S(1)} %get-tuple-element.44), channel_id=1, source_target_pairs={{0,1},{1,0},{2,3},{3,2},{4,5},{5,4},{6,7},{7,6},{8,9},{9,8},{10,11... | collective-permute-start | bytes 663560 | tf_op jit(solution)/shard_map/ppermute | solution.py:341
  46.3 24.1 %all-to-all-start = ((bf16[16,272,128]{2,1,0:T(8,128)(2,1)}), bf16[16,272,128]{2,1,0:T(8,128)(2,1)S(1)}, u32[]{:S(2)}, u32[]{:S(2)}) async-start(bf16[16,272,128]{2,1,0:T(8,128)(2,1)} %bitcast.11), calls=%async_computation | async-start | bytes 2228224 | tf_op jit(solution)/shard_map/all_to_all | solution.py:345
  53.4 1.3 copy-start.3
  98.1 18.2 %all-to-all-start.2 = ((bf16[16,272,128]{2,1,0:T(8,128)(2,1)}), bf16[16,272,128]{2,1,0:T(8,128)(2,1)S(1)}, u32[]{:S(2)}, u32[]{:S(2)}) async-start(bf16[16,272,128]{2,1,0:T(8,128)(2,1)} %broadcast_in_dim.30), calls=%async_computation.2 | async-start | bytes 2228224 | tf_op jit(solution)/shard_map/all_to_all | solution.py:345
  102.6 4.4 %collective-permute-start.6 = (bf16[512,128]{1,0:T(8,128)(2,1)S(1)}, bf16[512,128]{1,0:T(8,128)(2,1)S(1)}, u32[]{:S(2)}, u32[]{:S(2)}) collective-permute-start(bf16[512,128]{1,0:T(8,128)(2,1)S(1)} %get-tuple-element.53), channel_id=1, source_target_pairs={{0,4},{4,8},{8,12},{12,16},{16,20},{20,24},{24,28},{28,32},{32,36}... | collective-permute-start | bytes 393224 | tf_op jit(solution)/shard_map/ppermute | solution.py:356
  105.1 7.4 %collective-permute-start.7 = (bf16[512,128]{1,0:T(8,128)(2,1)S(1)}, bf16[512,128]{1,0:T(8,128)(2,1)S(1)}, u32[]{:S(2)}, u32[]{:S(2)}) collective-permute-start(bf16[512,128]{1,0:T(8,128)(2,1)S(1)} %get-tuple-element.54), channel_id=1, source_target_pairs={{4,0},{8,4},{12,8},{16,12},{20,16},{24,20},{28,24},{32,28},{36,32}... | collective-permute-start | bytes 393224 | tf_op jit(solution)/shard_map/ppermute | solution.py:356
  116.2 10.3 %collective-permute-start.8 = (bf16[4352,128]{1,0:T(8,128)(2,1)S(1)}, bf16[4352,128]{1,0:T(8,128)(2,1)S(1)}, u32[]{:S(2)}, u32[]{:S(2)}) collective-permute-start(bf16[4352,128]{1,0:T(8,128)(2,1)S(1)} %bitcast.32), channel_id=1, source_target_pairs={{0,1},{1,0},{2,3},{3,2},{4,5},{5,4},{6,7},{7,6},{8,9},{9,8},{10,11... | collective-permute-start | bytes 3342344 | tf_op jit(solution)/shard_map/ppermute | solution.py:341

commit v7 on v6

--- a/solution.py
+++ b/solution.py
@@ -378,12 +378,10 @@
     rows = merge(keep_a, other_a, keep_b, other_b)
     blocks = exchange(rows.reshape(16, 272, 128), ACROSS)
     blocks, to_left, to_right = lax.optimization_barrier((blocks, to_left, to_right))
+    from_left, from_right = neighbours(to_left, to_right)
     blocks = exchange(jnp.broadcast_to(total_of(blocks), (8, 272, 128)), ALONG)
-    blocks, to_left, to_right = lax.optimization_barrier((blocks, to_left, to_right))
-    from_left, from_right = neighbours(to_left, to_right)
-    blocks = exchange(jnp.broadcast_to(total_of(blocks), (16, 272, 128)), ACROSS)
     blocks, from_left, from_right = lax.optimization_barrier((blocks, from_left, from_right))
-    mine = blocks.reshape(4352, 128)
+    mine = exchange(jnp.broadcast_to(total_of(blocks), (16, 272, 128)), ACROSS).reshape(4352, 128)
     away = other_core(mine)
     first = (inner[:1].astype(F32) + from_left.astype(F32)).astype(BF16)
     last = (inner[3:].astype(F32) + from_right.astype(F32)).astype(BF16)

time: 130 us -> 131 us (level)
  blocking collectives: 26.2 us -> 18.9 us
  starting transfers between devices: 34 us -> 39.4 us
    all_to_all x1, blocking collectives: 26.2 us -> 18.9 us  [exchange(): lax.all_to_all(blocks, AXES, 0, 0, axis_index_groups=groups, tiled=True)]
    all_to_all x2, starting transfers between devices: 11.7 us -> 18.8 us  [exchange(): lax.all_to_all(blocks, AXES, 0, 0, axis_index_groups=groups, tiled=True)]
    ppermute x3, waiting for transfers between devices: 0.63 us -> 7.06 us  [neighbours(): lax.ppermute(to_right, 'slab', up)]
    ppermute x3, waiting for transfers between devices: 15.8 us -> 13 us  [neighbours(): lax.ppermute(to_left, 'slab', down)]
    ppermute x3, starting transfers between devices: 9.39 us -> 6.76 us  [other_core(): return lax.ppermute(value, AXES, CORES)]
    all_to_all x2, waiting for transfers between devices: 16.8 us -> 14.2 us  [exchange(): lax.all_to_all(blocks, AXES, 0, 0, axis_index_groups=groups, tiled=True)]
where the time goes in v7:
time: 131 us; the launch traced here: 129 us
  starting transfers between devices  39.4 us (30%)
  waiting for transfers between devices  36.5 us (28%)
  Pallas kernels  21.9 us (17%)
  blocking collectives  18.9 us (14%)
  local copies, waits for them, and re-layouts  8.51 us (6%)
  other arithmetic  2.8 us (2%)
    all_to_all x1, blocking collectives, exchange(): lax.all_to_all(blocks, AXES, 0, 0, axis_index_groups=groups, tiled=True)  18.9 us
    all_to_all x2, starting transfers between devices, exchange(): lax.all_to_all(blocks, AXES, 0, 0, axis_index_groups=groups, tiled=True)  18.8 us
    all_to_all x2, waiting for transfers between devices, exchange(): lax.all_to_all(blocks, AXES, 0, 0, axis_index_groups=groups, tiled=True)  14.2 us
    ppermute x3, waiting for transfers between devices, neighbours(): lax.ppermute(to_left, 'slab', down)  13 us
    ppermute x3, starting transfers between devices, neighbours(): lax.ppermute(to_right, 'slab', up)  9.94 us
    ppermute x3, waiting for transfers between devices, neighbours(): lax.ppermute(to_right, 'slab', up)  7.06 us
    ppermute x3, starting transfers between devices, other_core(): return lax.ppermute(value, AXES, CORES)  6.76 us
    pallas_call x1, Pallas kernels, block_b(): pl.pallas_call(block_b_kernel, in_specs=[SCALAR] + [WHOLE] * 5, out_shape...  6.66 us
  transfers between devices with their start and end apart: 11, of which 8 were waited for; matrix products, arithmetic and copies ran while one was open for 4% of the time, Pallas kernels for 8%

profile of v7, /device:TPU:1, one launch (start us, length us, event | category | flops | bytes accessed | tf_op | source)
XLA Modules:
  0.0 129.1 jit_solution(4180616167804343572)
XLA Ops:
  0.7 1.2 fusion.2
  2.2 4.4 %collective-permute-start = (bf16[640,128]{1,0:T(8,128)(2,1)S(1)}, bf16[640,128]{1,0:T(8,128)(2,1)S(1)}, u32[]{:S(2)}, u32[]{:S(2)}) collective-permute-start(bf16[640,128]{1,0:T(8,128)(2,1)S(1)} %get-tuple-element.66), channel_id=1, source_target_pairs={{0,4},{4,8},{8,12},{12,16},{16,20},{20,24},{24,28},{28,32},{32,36}... | collective-permute-start | bytes 491528 | tf_op jit(solution)/shard_map/ppermute | solution.py:356
  6.6 1.3 %collective-permute-start.1 = (bf16[640,128]{1,0:T(8,128)(2,1)S(1)}, bf16[640,128]{1,0:T(8,128)(2,1)S(1)}, u32[]{:S(2)}, u32[]{:S(2)}) collective-permute-start(bf16[640,128]{1,0:T(8,128)(2,1)S(1)} %get-tuple-element.65), channel_id=1, source_target_pairs={{4,0},{8,4},{12,8},{16,12},{20,16},{24,20},{28,24},{32,28},{36,32}... | collective-permute-start | bytes 491528 | tf_op jit(solution)/shard_map/ppermute | solution.py:356
  8.5 1.1 maximum_maximum_fusion.weight_ref
  9.6 3.7 %shard_map.75 = (bf16[4,544,256]{2,1,0:T(8,128)(2,1)S(1)}, f32[2,512,256]{2,1,0:T(8,128)S(1)}, bf16[2,512,256]{2,1,0:T(8,128)(2,1)S(1)}, f32[2,256,128]{2,1,0:T(8,128)S(1)}) custom-call(bf16[4,512,128]{2,1,0:T(8,128)(2,1)S(1)} %reshape.52.cells_ref, bf16[9,256,256]{2,1,0:T(8,128)(2,1)} %maximum_maximum_fusion.weight_ref), custom_call_target="tpu_custom_call" | custom-call | flops 2415919104 | bytes 6000000 | tf_op jit(solution)/shard_map/pallas_call | solution.py:85
  13.4 4.1 %collective-permute-done.1 = bf16[640,128]{1,0:T(8,128)(2,1)S(1)} collective-permute-done((bf16[640,128]{1,0:T(8,128)(2,1)S(1)}, bf16[640,128]{1,0:T(8,128)(2,1)S(1)}, u32[]{:S(2)}, u32[]{:S(2)}) %collective-permute-start.1) | collective-permute-done | bytes 163872 | tf_op jit(solution)/shard_map/ppermute | solution.py:356
  17.5 1.0 shard_map.76
  18.4 2.2 %collective-permute-start.2 = (bf16[2,256,128]{2,1,0:T(8,128)(2,1)S(1)}, bf16[2,256,128]{2,1,0:T(8,128)(2,1)S(1)}, u32[]{:S(2)}, u32[]{:S(2)}) collective-permute-start(bf16[2,256,128]{2,1,0:T(8,128)(2,1)S(1)} %get-tuple-element.31.cells_ref), channel_id=1, source_target_pairs={{0,4},{4,8},{8,12},{12,16},{16,20},{20,24},{24,28},{28,32},{32,36}... | collective-permute-start | bytes 393224 | tf_op jit(solution)/shard_map/ppermute | solution.py:356
  20.6 1.3 %collective-permute-start.3 = (bf16[2,256,128]{2,1,0:T(8,128)(2,1)S(1)}, bf16[2,256,128]{2,1,0:T(8,128)(2,1)S(1)}, u32[]{:S(2)}, u32[]{:S(2)}) collective-permute-start(bf16[2,256,128]{2,1,0:T(8,128)(2,1)S(1)} %get-tuple-element.31.cells_ref), channel_id=1, source_target_pairs={{4,0},{8,4},{12,8},{16,12},{20,16},{24,20},{28,24},{32,28},{36,32}... | collective-permute-start | bytes 393224 | tf_op jit(solution)/shard_map/ppermute | solution.py:356
  22.8 1.0 reshape.54.cot_ref
  23.8 6.3 %collective-permute-done.3.right_ref = bf16[2,256,128]{2,1,0:T(8,128)(2,1)S(1)} collective-permute-done((bf16[2,256,128]{2,1,0:T(8,128)(2,1)S(1)}, bf16[2,256,128]{2,1,0:T(8,128)(2,1)S(1)}, u32[]{:S(2)}, u32[]{:S(2)}) %collective-permute-start.3) | collective-permute-done | bytes 131104 | tf_op jit(solution)/shard_map/ppermute | solution.py:356
  30.1 6.7 %shard_map.77 = (bf16[64,256]{1,0:T(8,128)(2,1)}, bf16[9,384,128]{2,1,0:T(8,128)(2,1)S(1)}, bf16[9,384,128]{2,1,0:T(8,128)(2,1)S(1)}, bf16[2,256,128]{2,1,0:T(8,128)(2,1)S(1)}) custom-call(s32[1]{0:T(128)} %bitcast.core_ref, bf16[2,256,128]{2,1,0:T(8,128)(2,1)S(1)} %collective-permute-done.2.left_ref, bf16[2,256,128]{2,1,0:T(8,128)(2,1)S(1)} %get-tuple-element.31.cells_ref, ...), custom_call_target="tpu_custom_call" | custom-call | flops 3623878656 | bytes 5000000 | tf_op jit(solution)/shard_map/pallas_call | solution.py:181
  36.7 1.5 %collective-permute-start.5 = (bf16[9,384,128]{2,1,0:T(8,128)(2,1)S(1)}, bf16[9,384,128]{2,1,0:T(8,128)(2,1)S(1)}, u32[]{:S(2)}, u32[]{:S(2)}) collective-permute-start(bf16[9,384,128]{2,1,0:T(8,128)(2,1)S(1)} %get-tuple-element.43), channel_id=1, source_target_pairs={{0,1},{1,0},{2,3},{3,2},{4,5},{5,4},{6,7},{7,6},{8,9},{9,8},{10,11... | collective-permute-start | bytes 2654216 | tf_op jit(solution)/shard_map/ppermute | solution.py:341
  38.2 4.3 %shard_map.78 = (bf16[4,544,256]{2,1,0:T(8,128)(2,1)S(1)}, bf16[9,96,128]{2,1,0:T(8,128)(2,1)S(1)}, bf16[9,96,128]{2,1,0:T(8,128)(2,1)S(1)}) custom-call(s32[1]{0:T(128)} %bitcast.core_ref, bf16[2,256,128]{2,1,0:T(8,128)(2,1)S(1)} %get-tuple-element.33.grad_ref, bf16[2,512,256]{2,1,0:T(8,128)(2,1)S(1)} %get-tuple-element.34.slope_ref, ...), custom_call_target="tpu_custom_call" | custom-call | flops 2415919104 | bytes 6000000 | tf_op jit(solution)/shard_map/pallas_call | solution.py:233
  42.5 1.0 copy-done.2
  43.5 1.5 %collective-permute-done.4.other_a_ref = bf16[9,96,128]{2,1,0:T(8,128)(2,1)S(1)} collective-permute-done((bf16[9,96,128]{2,1,0:T(8,128)(2,1)S(1)}, bf16[9,96,128]{2,1,0:T(8,128)(2,1)S(1)}, u32[]{:S(2)}, u32[]{:S(2)}) %collective-permute-start.4) | collective-permute-done | bytes 221216 | tf_op jit(solution)/shard_map/ppermute | solution.py:341
  45.0 1.2 shard_map.80
  46.2 7.2 %all-to-all-start = ((bf16[16,272,128]{2,1,0:T(8,128)(2,1)}), bf16[16,272,128]{2,1,0:T(8,128)(2,1)}, u32[]{:S(2)}, u32[]{:S(2)}) async-start(bf16[16,272,128]{2,1,0:T(8,128)(2,1)} %bitcast.11), calls=%async_computation | async-start | bytes 2228224 | tf_op jit(solution)/shard_map/all_to_all | solution.py:345
  53.4 1.2 copy-done.3
  54.7 2.6 %shard_map.79 = (bf16[4,512,128]{2,1,0:T(8,128)(2,1)S(1)}, bf16[512,128]{1,0:T(8,128)(2,1)S(1)}, bf16[512,128]{1,0:T(8,128)(2,1)S(1)}) custom-call(bf16[4,544,256]{2,1,0:T(8,128)(2,1)S(1)} %copy-done.3, bf16[9,256,256]{2,1,0:T(8,128)(2,1)S(1)} %copy-done), custom_call_target="tpu_custom_call" | custom-call | flops 2415919104 | bytes 4000000 | tf_op jit(solution)/shard_map/pallas_call | solution.py:270
  57.3 13.1 %all-to-all-done = bf16[16,272,128]{2,1,0:T(8,128)(2,1)} async-done(((bf16[16,272,128]{2,1,0:T(8,128)(2,1)}), bf16[16,272,128]{2,1,0:T(8,128)(2,1)}, u32[]{:S(2)}, u32[]{:S(2)}) %all-to-all-start) | async-done | bytes 1114144 | tf_op jit(solution)/shard_map/all_to_all | solution.py:345
  70.5 1.4 %reduce_sum.24 = bf16[272,128]{1,0:T(8,128)(2,1)S(1)} reduce(bf16[16,272,128]{2,1,0:T(8,128)(2,1)} %all-to-all-done, bf16[]{:T(256)} %constant.21.clone.1), dimensions={0}, to_apply=%region_0.1 | reduce | flops 522240 | bytes 1183746 | tf_op jit(solution)/shard_map/reduce_sum | solution.py:349
  72.8 11.6 %all-to-all-start.1 = ((bf16[8,272,128]{2,1,0:T(8,128)(2,1)}), bf16[8,272,128]{2,1,0:T(8,128)(2,1)S(1)}, u32[]{:S(2)}, u32[]{:S(2)}) async-start(bf16[8,272,128]{2,1,0:T(8,128)(2,1)} %broadcast_in_dim.29), calls=%async_computation.1 | async-start | bytes 1114112 | tf_op jit(solution)/shard_map/all_to_all | solution.py:345
  84.4 3.4 %collective-permute-start.6 = (bf16[512,128]{1,0:T(8,128)(2,1)S(1)}, bf16[512,128]{1,0:T(8,128)(2,1)S(1)}, u32[]{:S(2)}, u32[]{:S(2)}) collective-permute-start(bf16[512,128]{1,0:T(8,128)(2,1)S(1)} %get-tuple-element.47), channel_id=1, source_target_pairs={{0,4},{4,8},{8,12},{12,16},{16,20},{20,24},{24,28},{28,32},{32,36}... | collective-permute-start | bytes 393224 | tf_op jit(solution)/shard_map/ppermute | solution.py:356
  87.8 1.3 %collective-permute-start.7 = (bf16[512,128]{1,0:T(8,128)(2,1)S(1)}, bf16[512,128]{1,0:T(8,128)(2,1)S(1)}, u32[]{:S(2)}, u32[]{:S(2)}) collective-permute-start(bf16[512,128]{1,0:T(8,128)(2,1)S(1)} %get-tuple-element.48), channel_id=1, source_target_pairs={{4,0},{8,4},{12,8},{16,12},{20,16},{24,20},{28,24},{32,28},{36,32}... | collective-permute-start | bytes 393224 | tf_op jit(solution)/shard_map/ppermute | solution.py:356
  89.1 7.1 %collective-permute-done.6 = bf16[512,128]{1,0:T(8,128)(2,1)S(1)} collective-permute-done((bf16[512,128]{1,0:T(8,128)(2,1)S(1)}, bf16[512,128]{1,0:T(8,128)(2,1)S(1)}, u32[]{:S(2)}, u32[]{:S(2)}) %collective-permute-start.6) | collective-permute-done | bytes 131104 | tf_op jit(solution)/shard_map/ppermute | solution.py:356
  96.1 2.6 %collective-permute-done.7 = bf16[512,128]{1,0:T(8,128)(2,1)S(1)} collective-permute-done((bf16[512,128]{1,0:T(8,128)(2,1)S(1)}, bf16[512,128]{1,0:T(8,128)(2,1)S(1)}, u32[]{:S(2)}, u32[]{:S(2)}) %collective-permute-start.7) | collective-permute-done | bytes 131104 | tf_op jit(solution)/shard_map/ppermute | solution.py:356
  98.8 1.1 all-to-all-done.1
  100.1 18.9 %all_to_all.15 = bf16[16,272,128]{2,1,0:T(8,128)(2,1)S(1)} all-to-all(bf16[16,272,128]{2,1,0:T(8,128)(2,1)S(1)} %broadcast_in_dim.34), channel_id=1, replica_groups={{0,16,32,48,64,80,96,112,128,144,160,176,192,208,224,240},{1,17,33,49,6..., dimensions={0} | all-to-all | bytes 2228224 | tf_op jit(solution)/shard_map/all_to_all | solution.py:345
  119.0 5.3 %collective-permute-start.8 = (bf16[4352,128]{1,0:T(8,128)(2,1)S(1)}, bf16[4352,128]{1,0:T(8,128)(2,1)S(1)}, u32[]{:S(2)}, u32[]{:S(2)}) collective-permute-start(bf16[4352,128]{1,0:T(8,128)(2,1)S(1)} %bitcast.32), channel_id=1, source_target_pairs={{0,1},{1,0},{2,3},{3,2},{4,5},{5,4},{6,7},{7,6},{8,9},{9,8},{10,11... | collective-permute-start | bytes 3342344 | tf_op jit(solution)/shard_map/ppermute | solution.py:341
  124.4 1.4 %reshape.57 = bf16[1,4,32,32,64]{4,3,2,1,0:T(8,128)(2,1)} reshape(bf16[4,512,128]{2,1,0:T(8,128)(2,1)S(1)} %pad_maximum_fusion) | data formatting | bytes 1048576 | tf_op jit(solution)/shard_map/reshape | solution.py:392
  126.6 2.4 %shard_map.81 = (f32[9,2,96,128]{3,2,1,0:T(8,128)}, f32[9,384,256]{2,1,0:T(8,128)}) custom-call(s32[1]{0:T(128)} %bitcast.core_ref, bf16[4352,128]{1,0:T(8,128)(2,1)S(1)} %bitcast.33, bf16[4352,128]{1,0:T(8,128)(2,1)S(1)} %collective-permute-done.8.away_ref), custom_call_target="tpu_custom_call" | custom-call | bytes 7000000 | tf_op jit(solution)/shard_map/pallas_call | solution.py:322
  (38 shorter events, 3.8 us)
Async XLA Ops:
  0.6 7.3 %copy-start.4 = (bf16[1,4,32,32,64]{4,3,2,1,0:T(8,128)(2,1)S(1)}, bf16[1,4,32,32,64]{4,3,2,1,0:T(8,128)(2,1)}, u32[]{:S(2)}) copy-start(bf16[1,4,32,32,64]{4,3,2,1,0:T(8,128)(2,1)} %param.4) | copy-start | bytes 1572868
  0.6 1.5 %copy-start.6 = (bf16[1,1,8,8,256]{4,3,2,1,0:T(8,128)(2,1)S(1)}, bf16[1,1,8,8,256]{4,3,2,1,0:T(8,128)(2,1)}, u32[]{:S(2)}) copy-start(bf16[1,1,8,8,256]{4,3,2,1,0:T(8,128)(2,1)} %param.7) | copy-start | bytes 98308
  1.8 6.6 %copy-start.5 = (bf16[3,3,3,64,128]{4,3,2,1,0:T(8,128)(2,1)S(1)}, bf16[3,3,3,64,128]{4,3,2,1,0:T(8,128)(2,1)}, u32[]{:S(2)}) copy-start(bf16[3,3,3,64,128]{4,3,2,1,0:T(8,128)(2,1)} %param.5) | copy-start | bytes 1327108
  2.2 11.1 %collective-permute-start = (bf16[640,128]{1,0:T(8,128)(2,1)S(1)}, bf16[640,128]{1,0:T(8,128)(2,1)S(1)}, u32[]{:S(2)}, u32[]{:S(2)}) collective-permute-start(bf16[640,128]{1,0:T(8,128)(2,1)S(1)} %get-tuple-element.66), channel_id=1, source_target_pairs={{0,4},{4,8},{8,12},{12,16},{16,20},{20,24},{24,28},{28,32},{32,36}... | collective-permute-start | bytes 491528 | tf_op jit(solution)/shard_map/ppermute | solution.py:356
  6.6 10.9 %collective-permute-start.1 = (bf16[640,128]{1,0:T(8,128)(2,1)S(1)}, bf16[640,128]{1,0:T(8,128)(2,1)S(1)}, u32[]{:S(2)}, u32[]{:S(2)}) collective-permute-start(bf16[640,128]{1,0:T(8,128)(2,1)S(1)} %get-tuple-element.65), channel_id=1, source_target_pairs={{4,0},{8,4},{12,8},{16,12},{20,16},{24,20},{28,24},{32,28},{36,32}... | collective-permute-start | bytes 491528 | tf_op jit(solution)/shard_map/ppermute | solution.py:356
  9.6 7.8 %copy-start = (bf16[9,256,256]{2,1,0:T(8,128)(2,1)S(1)}, bf16[9,256,256]{2,1,0:T(8,128)(2,1)}, u32[]{:S(2)}) copy-start(bf16[9,256,256]{2,1,0:T(8,128)(2,1)} %maximum_maximum_fusion.weight_ref) | copy-start | bytes 3538948
  13.3 5.1 %copy-start.1 = (bf16[4,544,256]{2,1,0:T(8,128)(2,1)}, bf16[4,544,256]{2,1,0:T(8,128)(2,1)S(1)}, u32[]{:S(2)}) copy-start(bf16[4,544,256]{2,1,0:T(8,128)(2,1)S(1)} %get-tuple-element.36.window_ref) | copy-start | bytes 3342340
  18.4 5.4 %collective-permute-start.2 = (bf16[2,256,128]{2,1,0:T(8,128)(2,1)S(1)}, bf16[2,256,128]{2,1,0:T(8,128)(2,1)S(1)}, u32[]{:S(2)}, u32[]{:S(2)}) collective-permute-start(bf16[2,256,128]{2,1,0:T(8,128)(2,1)S(1)} %get-tuple-element.31.cells_ref), channel_id=1, source_target_pairs={{0,4},{4,8},{8,12},{12,16},{16,20},{20,24},{24,28},{28,32},{32,36}... | collective-permute-start | bytes 393224 | tf_op jit(solution)/shard_map/ppermute | solution.py:356
  20.6 9.4 %collective-permute-start.3 = (bf16[2,256,128]{2,1,0:T(8,128)(2,1)S(1)}, bf16[2,256,128]{2,1,0:T(8,128)(2,1)S(1)}, u32[]{:S(2)}, u32[]{:S(2)}) collective-permute-start(bf16[2,256,128]{2,1,0:T(8,128)(2,1)S(1)} %get-tuple-element.31.cells_ref), channel_id=1, source_target_pairs={{4,0},{8,4},{12,8},{16,12},{20,16},{24,20},{28,24},{32,28},{36,32}... | collective-permute-start | bytes 393224 | tf_op jit(solution)/shard_map/ppermute | solution.py:356
  36.7 8.3 %collective-permute-start.5 = (bf16[9,384,128]{2,1,0:T(8,128)(2,1)S(1)}, bf16[9,384,128]{2,1,0:T(8,128)(2,1)S(1)}, u32[]{:S(2)}, u32[]{:S(2)}) collective-permute-start(bf16[9,384,128]{2,1,0:T(8,128)(2,1)S(1)} %get-tuple-element.43), channel_id=1, source_target_pairs={{0,1},{1,0},{2,3},{3,2},{4,5},{5,4},{6,7},{7,6},{8,9},{9,8},{10,11... | collective-permute-start | bytes 2654216 | tf_op jit(solution)/shard_map/ppermute | solution.py:341
  42.5 1.0 copy-start.2
  43.5 1.5 %collective-permute-start.4 = (bf16[9,96,128]{2,1,0:T(8,128)(2,1)S(1)}, bf16[9,96,128]{2,1,0:T(8,128)(2,1)S(1)}, u32[]{:S(2)}, u32[]{:S(2)}) collective-permute-start(bf16[9,96,128]{2,1,0:T(8,128)(2,1)S(1)} %get-tuple-element.41), channel_id=1, source_target_pairs={{0,1},{1,0},{2,3},{3,2},{4,5},{5,4},{6,7},{7,6},{8,9},{9,8},{10,11... | collective-permute-start | bytes 663560 | tf_op jit(solution)/shard_map/ppermute | solution.py:341
  46.2 24.2 %all-to-all-start = ((bf16[16,272,128]{2,1,0:T(8,128)(2,1)}), bf16[16,272,128]{2,1,0:T(8,128)(2,1)}, u32[]{:S(2)}, u32[]{:S(2)}) async-start(bf16[16,272,128]{2,1,0:T(8,128)(2,1)} %bitcast.11), calls=%async_computation | async-start | bytes 2228224 | tf_op jit(solution)/shard_map/all_to_all | solution.py:345
  53.4 1.3 copy-start.3
  72.8 27.1 %all-to-all-start.1 = ((bf16[8,272,128]{2,1,0:T(8,128)(2,1)}), bf16[8,272,128]{2,1,0:T(8,128)(2,1)S(1)}, u32[]{:S(2)}, u32[]{:S(2)}) async-start(bf16[8,272,128]{2,1,0:T(8,128)(2,1)} %broadcast_in_dim.29), calls=%async_computation.1 | async-start | bytes 1114112 | tf_op jit(solution)/shard_map/all_to_all | solution.py:345
  84.4 11.7 %collective-permute-start.6 = (bf16[512,128]{1,0:T(8,128)(2,1)S(1)}, bf16[512,128]{1,0:T(8,128)(2,1)S(1)}, u32[]{:S(2)}, u32[]{:S(2)}) collective-permute-start(bf16[512,128]{1,0:T(8,128)(2,1)S(1)} %get-tuple-element.47), channel_id=1, source_target_pairs={{0,4},{4,8},{8,12},{12,16},{16,20},{20,24},{24,28},{28,32},{32,36}... | collective-permute-start | bytes 393224 | tf_op jit(solution)/shard_map/ppermute | solution.py:356
  87.8 11.0 %collective-permute-start.7 = (bf16[512,128]{1,0:T(8,128)(2,1)S(1)}, bf16[512,128]{1,0:T(8,128)(2,1)S(1)}, u32[]{:S(2)}, u32[]{:S(2)}) collective-permute-start(bf16[512,128]{1,0:T(8,128)(2,1)S(1)} %get-tuple-element.48), channel_id=1, source_target_pairs={{4,0},{8,4},{12,8},{16,12},{20,16},{24,20},{28,24},{32,28},{36,32}... | collective-permute-start | bytes 393224 | tf_op jit(solution)/shard_map/ppermute | solution.py:356
  119.0 7.7 %collective-permute-start.8 = (bf16[4352,128]{1,0:T(8,128)(2,1)S(1)}, bf16[4352,128]{1,0:T(8,128)(2,1)S(1)}, u32[]{:S(2)}, u32[]{:S(2)}) collective-permute-start(bf16[4352,128]{1,0:T(8,128)(2,1)S(1)} %bitcast.32), channel_id=1, source_target_pairs={{0,1},{1,0},{2,3},{3,2},{4,5},{5,4},{6,7},{7,6},{8,9},{9,8},{10,11... | collective-permute-start | bytes 3342344 | tf_op jit(solution)/shard_map/ppermute | solution.py:341

commit v8 on v6

--- a/solution.py
+++ b/solution.py
@@ -349,11 +349,16 @@
     return jnp.sum(blocks.astype(F32), axis=0).astype(BF16)
 
 
+def move_up(value):
+    return lax.ppermute(value, "slab", [(i, i + 1) for i in range(lax.axis_size("slab") - 1)])
+
+
+def move_down(value):
+    return lax.ppermute(value, "slab", [(i + 1, i) for i in range(lax.axis_size("slab") - 1)])
+
+
 def neighbours(to_left, to_right):
-    count = lax.axis_size("slab")
-    up = [(i, i + 1) for i in range(count - 1)]
-    down = [(i + 1, i) for i in range(count - 1)]
-    return lax.ppermute(to_right, "slab", up), lax.ppermute(to_left, "slab", down)
+    return move_up(to_right), move_down(to_left)
 
 
 def shards(cubes, weight_a, weight_b, cotangent):
@@ -377,12 +382,13 @@
     inner, to_left, to_right = back_a(grad_pre, pair_weight)
     rows = merge(keep_a, other_a, keep_b, other_b)
     blocks = exchange(rows.reshape(16, 272, 128), ACROSS)
-    blocks, to_left, to_right = lax.optimization_barrier((blocks, to_left, to_right))
+    from_right = move_down(to_left)
+    blocks, from_right, to_right = lax.optimization_barrier((blocks, from_right, to_right))
     blocks = exchange(jnp.broadcast_to(total_of(blocks), (8, 272, 128)), ALONG)
-    blocks, to_left, to_right = lax.optimization_barrier((blocks, to_left, to_right))
-    from_left, from_right = neighbours(to_left, to_right)
+    blocks, to_right = lax.optimization_barrier((blocks, to_right))
+    from_left = move_up(to_right)
     blocks = exchange(jnp.broadcast_to(total_of(blocks), (16, 272, 128)), ACROSS)
-    blocks, from_left, from_right = lax.optimization_barrier((blocks, from_left, from_right))
+    blocks, from_left = lax.optimization_barrier((blocks, from_left))
     mine = blocks.reshape(4352, 128)
     away = other_core(mine)
     first = (inner[:1].astype(F32) + from_left.astype(F32)).astype(BF16)

time: 130 us -> 132 us (1.015)
  starting transfers between devices: 34 us -> 35.5 us
    all_to_all x2, starting transfers between devices: 11.7 us -> 13.8 us  [exchange(): lax.all_to_all(blocks, AXES, 0, 0, axis_index_groups=groups, tiled=True)]
    ppermute x6, waiting for transfers between devices: 16.5 us -> 17.8 us  [the longest x3 15.9 us: move_down(): lax.ppermute(value, 'slab', [(i + 1, i) for i in range(lax.axis_size('sla...]
where the time goes in v8:
time: 132 us
  waiting for transfers between devices  35.6 us (27%)
  starting transfers between devices  35.5 us (27%)
  blocking collectives  26 us (20%)
  Pallas kernels  21.9 us (17%)
  local copies, waits for them, and re-layouts  8.7 us (7%)
  other arithmetic  2.8 us (2%)
    all_to_all x1, blocking collectives, exchange(): lax.all_to_all(blocks, AXES, 0, 0, axis_index_groups=groups, tiled=True)  26 us
    ppermute x3, waiting for transfers between devices, move_down(): lax.ppermute(value, 'slab', [(i + 1, i) for i in range(lax.axis_size('sla...  15.9 us
    all_to_all x2, waiting for transfers between devices, exchange(): lax.all_to_all(blocks, AXES, 0, 0, axis_index_groups=groups, tiled=True)  15.5 us
    all_to_all x2, starting transfers between devices, exchange(): lax.all_to_all(blocks, AXES, 0, 0, axis_index_groups=groups, tiled=True)  13.8 us
    ppermute x3, starting transfers between devices, move_up(): lax.ppermute(value, 'slab', [(i, i + 1) for i in range(lax.axis_size('sla...  9.07 us
    ppermute x3, starting transfers between devices, other_core(): return lax.ppermute(value, AXES, CORES)  8.72 us
    pallas_call x1, Pallas kernels, block_b(): pl.pallas_call(block_b_kernel, in_specs=[SCALAR] + [WHOLE] * 5, out_shape...  6.66 us
    pallas_call x1, Pallas kernels, kernel_a(): pl.pallas_call(kernel_a_kernel, in_specs=[SCALAR] + [WHOLE] * 5, out_spec...  4.34 us
  transfers between devices with their start and end apart: 11, of which 8 were waited for; matrix products, arithmetic and copies ran while one was open for 4% of the time, Pallas kernels for 8%

profile of v8, /device:TPU:1, one launch (start us, length us, event | category | flops | bytes accessed | tf_op | source)
XLA Modules:
  0.0 131.5 jit_solution(2830807339495927575)
XLA Ops:
  0.7 1.2 fusion.2
  2.2 4.4 %collective-permute-start = (bf16[640,128]{1,0:T(8,128)(2,1)S(1)}, bf16[640,128]{1,0:T(8,128)(2,1)S(1)}, u32[]{:S(2)}, u32[]{:S(2)}) collective-permute-start(bf16[640,128]{1,0:T(8,128)(2,1)S(1)} %get-tuple-element.68), channel_id=1, source_target_pairs={{0,4},{4,8},{8,12},{12,16},{16,20},{20,24},{24,28},{28,32},{32,36}... | collective-permute-start | bytes 491528 | tf_op jit(solution)/shard_map/ppermute | solution.py:353
  6.6 1.3 collective-permute-start.1
  8.5 1.1 maximum_maximum_fusion.weight_ref
  9.6 3.7 %shard_map.75 = (bf16[4,544,256]{2,1,0:T(8,128)(2,1)S(1)}, f32[2,512,256]{2,1,0:T(8,128)S(1)}, bf16[2,512,256]{2,1,0:T(8,128)(2,1)S(1)}, f32[2,256,128]{2,1,0:T(8,128)S(1)}) custom-call(bf16[4,512,128]{2,1,0:T(8,128)(2,1)S(1)} %reshape.52.cells_ref, bf16[9,256,256]{2,1,0:T(8,128)(2,1)} %maximum_maximum_fusion.weight_ref), custom_call_target="tpu_custom_call" | custom-call | flops 2415919104 | bytes 6000000 | tf_op jit(solution)/shard_map/pallas_call | solution.py:85
  13.4 4.1 %collective-permute-done.1 = bf16[640,128]{1,0:T(8,128)(2,1)S(1)} collective-permute-done((bf16[640,128]{1,0:T(8,128)(2,1)S(1)}, bf16[640,128]{1,0:T(8,128)(2,1)S(1)}, u32[]{:S(2)}, u32[]{:S(2)}) %collective-permute-start.1) | collective-permute-done | bytes 163872 | tf_op jit(solution)/shard_map/ppermute | solution.py:357
  18.4 2.2 %collective-permute-start.2 = (bf16[2,256,128]{2,1,0:T(8,128)(2,1)S(1)}, bf16[2,256,128]{2,1,0:T(8,128)(2,1)S(1)}, u32[]{:S(2)}, u32[]{:S(2)}) collective-permute-start(bf16[2,256,128]{2,1,0:T(8,128)(2,1)S(1)} %get-tuple-element.32.cells_ref), channel_id=1, source_target_pairs={{0,4},{4,8},{8,12},{12,16},{16,20},{20,24},{24,28},{28,32},{32,36}... | collective-permute-start | bytes 393224 | tf_op jit(solution)/shard_map/ppermute | solution.py:353
  20.6 1.3 collective-permute-start.3
  22.8 1.0 reshape.54.cot_ref
  23.8 6.3 %collective-permute-done.3.right_ref = bf16[2,256,128]{2,1,0:T(8,128)(2,1)S(1)} collective-permute-done((bf16[2,256,128]{2,1,0:T(8,128)(2,1)S(1)}, bf16[2,256,128]{2,1,0:T(8,128)(2,1)S(1)}, u32[]{:S(2)}, u32[]{:S(2)}) %collective-permute-start.3) | collective-permute-done | bytes 131104 | tf_op jit(solution)/shard_map/ppermute | solution.py:357
  30.1 6.7 %shard_map.77 = (bf16[64,256]{1,0:T(8,128)(2,1)}, bf16[9,384,128]{2,1,0:T(8,128)(2,1)S(1)}, bf16[9,384,128]{2,1,0:T(8,128)(2,1)S(1)}, bf16[2,256,128]{2,1,0:T(8,128)(2,1)S(1)}) custom-call(s32[1]{0:T(128)} %bitcast.core_ref, bf16[2,256,128]{2,1,0:T(8,128)(2,1)S(1)} %collective-permute-done.2.left_ref, bf16[2,256,128]{2,1,0:T(8,128)(2,1)S(1)} %get-tuple-element.32.cells_ref, ...), custom_call_target="tpu_custom_call" | custom-call | flops 3623878656 | bytes 5000000 | tf_op jit(solution)/shard_map/pallas_call | solution.py:181
  36.7 1.5 %collective-permute-start.5 = (bf16[9,384,128]{2,1,0:T(8,128)(2,1)S(1)}, bf16[9,384,128]{2,1,0:T(8,128)(2,1)S(1)}, u32[]{:S(2)}, u32[]{:S(2)}) collective-permute-start(bf16[9,384,128]{2,1,0:T(8,128)(2,1)S(1)} %get-tuple-element.44), channel_id=1, source_target_pairs={{0,1},{1,0},{2,3},{3,2},{4,5},{5,4},{6,7},{7,6},{8,9},{9,8},{10,11... | collective-permute-start | bytes 2654216 | tf_op jit(solution)/shard_map/ppermute | solution.py:341
  38.2 4.3 %shard_map.78 = (bf16[4,544,256]{2,1,0:T(8,128)(2,1)S(1)}, bf16[9,96,128]{2,1,0:T(8,128)(2,1)S(1)}, bf16[9,96,128]{2,1,0:T(8,128)(2,1)S(1)}) custom-call(s32[1]{0:T(128)} %bitcast.core_ref, bf16[2,256,128]{2,1,0:T(8,128)(2,1)S(1)} %get-tuple-element.34.grad_ref, bf16[2,512,256]{2,1,0:T(8,128)(2,1)S(1)} %get-tuple-element.35.slope_ref, ...), custom_call_target="tpu_custom_call" | custom-call | flops 2415919104 | bytes 6000000 | tf_op jit(solution)/shard_map/pallas_call | solution.py:233
  42.5 1.0 copy-done.2
  43.5 1.5 %collective-permute-done.4.other_a_ref = bf16[9,96,128]{2,1,0:T(8,128)(2,1)S(1)} collective-permute-done((bf16[9,96,128]{2,1,0:T(8,128)(2,1)S(1)}, bf16[9,96,128]{2,1,0:T(8,128)(2,1)S(1)}, u32[]{:S(2)}, u32[]{:S(2)}) %collective-permute-start.4) | collective-permute-done | bytes 221216 | tf_op jit(solution)/shard_map/ppermute | solution.py:341
  45.0 1.2 shard_map.80
  46.2 7.2 %all-to-all-start = ((bf16[16,272,128]{2,1,0:T(8,128)(2,1)}), bf16[16,272,128]{2,1,0:T(8,128)(2,1)}, u32[]{:S(2)}, u32[]{:S(2)}) async-start(bf16[16,272,128]{2,1,0:T(8,128)(2,1)} %bitcast.11), calls=%async_computation | async-start | bytes 2228224 | tf_op jit(solution)/shard_map/all_to_all | solution.py:345
  53.4 1.2 copy-done.3
  54.7 2.6 %shard_map.79 = (bf16[4,512,128]{2,1,0:T(8,128)(2,1)S(1)}, bf16[512,128]{1,0:T(8,128)(2,1)S(1)}, bf16[512,128]{1,0:T(8,128)(2,1)S(1)}) custom-call(bf16[4,544,256]{2,1,0:T(8,128)(2,1)S(1)} %copy-done.3, bf16[9,256,256]{2,1,0:T(8,128)(2,1)S(1)} %copy-done), custom_call_target="tpu_custom_call" | custom-call | flops 2415919104 | bytes 4000000 | tf_op jit(solution)/shard_map/pallas_call | solution.py:270
  57.3 1.3 collective-permute-start.6
  58.6 5.5 %collective-permute-done.6 = bf16[512,128]{1,0:T(8,128)(2,1)S(1)} collective-permute-done((bf16[512,128]{1,0:T(8,128)(2,1)S(1)}, bf16[512,128]{1,0:T(8,128)(2,1)S(1)}, u32[]{:S(2)}, u32[]{:S(2)}) %collective-permute-start.6) | collective-permute-done | bytes 131104 | tf_op jit(solution)/shard_map/ppermute | solution.py:357
  64.2 6.3 %all-to-all-done = bf16[16,272,128]{2,1,0:T(8,128)(2,1)} async-done(((bf16[16,272,128]{2,1,0:T(8,128)(2,1)}), bf16[16,272,128]{2,1,0:T(8,128)(2,1)}, u32[]{:S(2)}, u32[]{:S(2)}) %all-to-all-start) | async-done | bytes 1114144 | tf_op jit(solution)/shard_map/all_to_all | solution.py:345
  70.5 1.4 %reduce_sum.24 = bf16[272,128]{1,0:T(8,128)(2,1)S(1)} reduce(bf16[16,272,128]{2,1,0:T(8,128)(2,1)} %all-to-all-done, bf16[]{:T(256)} %constant.21.clone.1), dimensions={0}, to_apply=%region_0.1 | reduce | flops 522240 | bytes 1183746 | tf_op jit(solution)/shard_map/reduce_sum | solution.py:349
  72.0 26.0 %all_to_all.15 = bf16[8,272,128]{2,1,0:T(8,128)(2,1)S(1)} all-to-all(bf16[8,272,128]{2,1,0:T(8,128)(2,1)S(1)} %broadcast_in_dim.29), channel_id=1, replica_groups={{0,4,8,12,2,6,10,14},{1,5,9,13,3,7,11,15},{16,20,24,28,18,22,26,30},{17..., dimensions={0} | all-to-all | bytes 1114112 | tf_op jit(solution)/shard_map/all_to_all | solution.py:345
  98.1 1.1 broadcast_in_dim.30
  99.2 6.6 %all-to-all-start.2 = ((bf16[16,272,128]{2,1,0:T(8,128)(2,1)}), bf16[16,272,128]{2,1,0:T(8,128)(2,1)S(1)}, u32[]{:S(2)}, u32[]{:S(2)}) async-start(bf16[16,272,128]{2,1,0:T(8,128)(2,1)} %broadcast_in_dim.30), calls=%async_computation.2 | async-start | bytes 2228224 | tf_op jit(solution)/shard_map/all_to_all | solution.py:345
  105.9 2.5 %collective-permute-start.7 = (bf16[512,128]{1,0:T(8,128)(2,1)S(1)}, bf16[512,128]{1,0:T(8,128)(2,1)S(1)}, u32[]{:S(2)}, u32[]{:S(2)}) collective-permute-start(bf16[512,128]{1,0:T(8,128)(2,1)S(1)} %get-tuple-element.50), channel_id=1, source_target_pairs={{0,4},{4,8},{8,12},{12,16},{16,20},{20,24},{24,28},{28,32},{32,36}... | collective-permute-start | bytes 393224 | tf_op jit(solution)/shard_map/ppermute | solution.py:353
  108.4 1.9 %collective-permute-done.7 = bf16[512,128]{1,0:T(8,128)(2,1)S(1)} collective-permute-done((bf16[512,128]{1,0:T(8,128)(2,1)S(1)}, bf16[512,128]{1,0:T(8,128)(2,1)S(1)}, u32[]{:S(2)}, u32[]{:S(2)}) %collective-permute-start.7) | collective-permute-done | bytes 131104 | tf_op jit(solution)/shard_map/ppermute | solution.py:353
  110.3 9.2 %all-to-all-done.2 = bf16[16,272,128]{2,1,0:T(8,128)(2,1)S(1)} async-done(((bf16[16,272,128]{2,1,0:T(8,128)(2,1)}), bf16[16,272,128]{2,1,0:T(8,128)(2,1)S(1)}, u32[]{:S(2)}, u32[]{:S(2)}) %all-to-all-start.2) | async-done | bytes 1114144 | tf_op jit(solution)/shard_map/all_to_all | solution.py:345
  119.5 7.2 %collective-permute-start.8 = (bf16[4352,128]{1,0:T(8,128)(2,1)S(1)}, bf16[4352,128]{1,0:T(8,128)(2,1)S(1)}, u32[]{:S(2)}, u32[]{:S(2)}) collective-permute-start(bf16[4352,128]{1,0:T(8,128)(2,1)S(1)} %bitcast.32), channel_id=1, source_target_pairs={{0,1},{1,0},{2,3},{3,2},{4,5},{5,4},{6,7},{7,6},{8,9},{9,8},{10,11... | collective-permute-start | bytes 3342344 | tf_op jit(solution)/shard_map/ppermute | solution.py:341
  126.9 1.4 %reshape.57 = bf16[1,4,32,32,64]{4,3,2,1,0:T(8,128)(2,1)} reshape(bf16[4,512,128]{2,1,0:T(8,128)(2,1)S(1)} %pad_maximum_fusion) | data formatting | bytes 1048576 | tf_op jit(solution)/shard_map/reshape | solution.py:400
  129.1 2.4 %shard_map.81 = (f32[9,2,96,128]{3,2,1,0:T(8,128)}, f32[9,384,256]{2,1,0:T(8,128)}) custom-call(s32[1]{0:T(128)} %bitcast.core_ref, bf16[4352,128]{1,0:T(8,128)(2,1)S(1)} %bitcast.33, bf16[4352,128]{1,0:T(8,128)(2,1)S(1)} %collective-permute-done.8.away_ref), custom_call_target="tpu_custom_call" | custom-call | bytes 7000000 | tf_op jit(solution)/shard_map/pallas_call | solution.py:322
  (38 shorter events, 3.9 us)
Async XLA Ops:
  0.6 7.3 %copy-start.4 = (bf16[1,4,32,32,64]{4,3,2,1,0:T(8,128)(2,1)S(1)}, bf16[1,4,32,32,64]{4,3,2,1,0:T(8,128)(2,1)}, u32[]{:S(2)}) copy-start(bf16[1,4,32,32,64]{4,3,2,1,0:T(8,128)(2,1)} %param.4) | copy-start | bytes 1572868
  0.6 1.5 %copy-start.6 = (bf16[1,1,8,8,256]{4,3,2,1,0:T(8,128)(2,1)S(1)}, bf16[1,1,8,8,256]{4,3,2,1,0:T(8,128)(2,1)}, u32[]{:S(2)}) copy-start(bf16[1,1,8,8,256]{4,3,2,1,0:T(8,128)(2,1)} %param.7) | copy-start | bytes 98308
  1.8 6.6 %copy-start.5 = (bf16[3,3,3,64,128]{4,3,2,1,0:T(8,128)(2,1)S(1)}, bf16[3,3,3,64,128]{4,3,2,1,0:T(8,128)(2,1)}, u32[]{:S(2)}) copy-start(bf16[3,3,3,64,128]{4,3,2,1,0:T(8,128)(2,1)} %param.5) | copy-start | bytes 1327108
  2.2 11.1 %collective-permute-start = (bf16[640,128]{1,0:T(8,128)(2,1)S(1)}, bf16[640,128]{1,0:T(8,128)(2,1)S(1)}, u32[]{:S(2)}, u32[]{:S(2)}) collective-permute-start(bf16[640,128]{1,0:T(8,128)(2,1)S(1)} %get-tuple-element.68), channel_id=1, source_target_pairs={{0,4},{4,8},{8,12},{12,16},{16,20},{20,24},{24,28},{28,32},{32,36}... | collective-permute-start | bytes 491528 | tf_op jit(solution)/shard_map/ppermute | solution.py:353
  6.6 10.9 %collective-permute-start.1 = (bf16[640,128]{1,0:T(8,128)(2,1)S(1)}, bf16[640,128]{1,0:T(8,128)(2,1)S(1)}, u32[]{:S(2)}, u32[]{:S(2)}) collective-permute-start(bf16[640,128]{1,0:T(8,128)(2,1)S(1)} %get-tuple-element.67), channel_id=1, source_target_pairs={{4,0},{8,4},{12,8},{16,12},{20,16},{24,20},{28,24},{32,28},{36,32}... | collective-permute-start | bytes 491528 | tf_op jit(solution)/shard_map/ppermute | solution.py:357
  9.6 7.8 %copy-start = (bf16[9,256,256]{2,1,0:T(8,128)(2,1)S(1)}, bf16[9,256,256]{2,1,0:T(8,128)(2,1)}, u32[]{:S(2)}) copy-start(bf16[9,256,256]{2,1,0:T(8,128)(2,1)} %maximum_maximum_fusion.weight_ref) | copy-start | bytes 3538948
  13.3 5.1 %copy-start.1 = (bf16[4,544,256]{2,1,0:T(8,128)(2,1)}, bf16[4,544,256]{2,1,0:T(8,128)(2,1)S(1)}, u32[]{:S(2)}) copy-start(bf16[4,544,256]{2,1,0:T(8,128)(2,1)S(1)} %get-tuple-element.37.window_ref) | copy-start | bytes 3342340
  18.4 5.4 %collective-permute-start.2 = (bf16[2,256,128]{2,1,0:T(8,128)(2,1)S(1)}, bf16[2,256,128]{2,1,0:T(8,128)(2,1)S(1)}, u32[]{:S(2)}, u32[]{:S(2)}) collective-permute-start(bf16[2,256,128]{2,1,0:T(8,128)(2,1)S(1)} %get-tuple-element.32.cells_ref), channel_id=1, source_target_pairs={{0,4},{4,8},{8,12},{12,16},{16,20},{20,24},{24,28},{28,32},{32,36}... | collective-permute-start | bytes 393224 | tf_op jit(solution)/shard_map/ppermute | solution.py:353
  20.6 9.4 %collective-permute-start.3 = (bf16[2,256,128]{2,1,0:T(8,128)(2,1)S(1)}, bf16[2,256,128]{2,1,0:T(8,128)(2,1)S(1)}, u32[]{:S(2)}, u32[]{:S(2)}) collective-permute-start(bf16[2,256,128]{2,1,0:T(8,128)(2,1)S(1)} %get-tuple-element.32.cells_ref), channel_id=1, source_target_pairs={{4,0},{8,4},{12,8},{16,12},{20,16},{24,20},{28,24},{32,28},{36,32}... | collective-permute-start | bytes 393224 | tf_op jit(solution)/shard_map/ppermute | solution.py:357
  36.7 8.3 %collective-permute-start.5 = (bf16[9,384,128]{2,1,0:T(8,128)(2,1)S(1)}, bf16[9,384,128]{2,1,0:T(8,128)(2,1)S(1)}, u32[]{:S(2)}, u32[]{:S(2)}) collective-permute-start(bf16[9,384,128]{2,1,0:T(8,128)(2,1)S(1)} %get-tuple-element.44), channel_id=1, source_target_pairs={{0,1},{1,0},{2,3},{3,2},{4,5},{5,4},{6,7},{7,6},{8,9},{9,8},{10,11... | collective-permute-start | bytes 2654216 | tf_op jit(solution)/shard_map/ppermute | solution.py:341
  42.5 1.0 copy-start.2
  43.5 1.5 %collective-permute-start.4 = (bf16[9,96,128]{2,1,0:T(8,128)(2,1)S(1)}, bf16[9,96,128]{2,1,0:T(8,128)(2,1)S(1)}, u32[]{:S(2)}, u32[]{:S(2)}) collective-permute-start(bf16[9,96,128]{2,1,0:T(8,128)(2,1)S(1)} %get-tuple-element.42), channel_id=1, source_target_pairs={{0,1},{1,0},{2,3},{3,2},{4,5},{5,4},{6,7},{7,6},{8,9},{9,8},{10,11... | collective-permute-start | bytes 663560 | tf_op jit(solution)/shard_map/ppermute | solution.py:341
  46.2 24.2 %all-to-all-start = ((bf16[16,272,128]{2,1,0:T(8,128)(2,1)}), bf16[16,272,128]{2,1,0:T(8,128)(2,1)}, u32[]{:S(2)}, u32[]{:S(2)}) async-start(bf16[16,272,128]{2,1,0:T(8,128)(2,1)} %bitcast.11), calls=%async_computation | async-start | bytes 2228224 | tf_op jit(solution)/shard_map/all_to_all | solution.py:345
  53.4 1.3 copy-start.3
  57.3 6.8 %collective-permute-start.6 = (bf16[512,128]{1,0:T(8,128)(2,1)S(1)}, bf16[512,128]{1,0:T(8,128)(2,1)S(1)}, u32[]{:S(2)}, u32[]{:S(2)}) collective-permute-start(bf16[512,128]{1,0:T(8,128)(2,1)S(1)} %get-tuple-element.45), channel_id=1, source_target_pairs={{4,0},{8,4},{12,8},{16,12},{20,16},{24,20},{28,24},{32,28},{36,32}... | collective-permute-start | bytes 393224 | tf_op jit(solution)/shard_map/ppermute | solution.py:357
  99.2 20.3 %all-to-all-start.2 = ((bf16[16,272,128]{2,1,0:T(8,128)(2,1)}), bf16[16,272,128]{2,1,0:T(8,128)(2,1)S(1)}, u32[]{:S(2)}, u32[]{:S(2)}) async-start(bf16[16,272,128]{2,1,0:T(8,128)(2,1)} %broadcast_in_dim.30), calls=%async_computation.2 | async-start | bytes 2228224 | tf_op jit(solution)/shard_map/all_to_all | solution.py:345
  105.9 4.4 %collective-permute-start.7 = (bf16[512,128]{1,0:T(8,128)(2,1)S(1)}, bf16[512,128]{1,0:T(8,128)(2,1)S(1)}, u32[]{:S(2)}, u32[]{:S(2)}) collective-permute-start(bf16[512,128]{1,0:T(8,128)(2,1)S(1)} %get-tuple-element.50), channel_id=1, source_target_pairs={{0,4},{4,8},{8,12},{12,16},{16,20},{20,24},{24,28},{28,32},{32,36}... | collective-permute-start | bytes 393224 | tf_op jit(solution)/shard_map/ppermute | solution.py:353
  119.5 9.6 %collective-permute-start.8 = (bf16[4352,128]{1,0:T(8,128)(2,1)S(1)}, bf16[4352,128]{1,0:T(8,128)(2,1)S(1)}, u32[]{:S(2)}, u32[]{:S(2)}) collective-permute-start(bf16[4352,128]{1,0:T(8,128)(2,1)S(1)} %bitcast.32), channel_id=1, source_target_pairs={{0,1},{1,0},{2,3},{3,2},{4,5},{5,4},{6,7},{7,6},{8,9},{9,8},{10,11... | collective-permute-start | bytes 3342344 | tf_op jit(solution)/shard_map/ppermute | solution.py:341

commit v9 on v6

--- a/solution.py
+++ b/solution.py
@@ -305,27 +305,59 @@
     )(keep_a, other_a, keep_b, other_b)
 
 
-def unpack_kernel(core_ref, mine_ref, away_ref, sum_a_ref, sum_b_ref):
+def total_kernel(blocks_ref, copies_ref):
+    total = blocks_ref[0].astype(F32)
+    for block in range(1, blocks_ref.shape[0]):
+        total = total + blocks_ref[block].astype(F32)
+    total = total.astype(BF16)
+    for copy in range(copies_ref.shape[0]):
+        copies_ref[copy] = total
+
+
+def total_copies(blocks, count):
+    return pl.pallas_call(
+        total_kernel,
+        out_shape=jax.ShapeDtypeStruct((count, 272, 128), BF16),
+        compiler_params=pltpu.CompilerParams(vmem_limit_bytes=ROOM),
+        cost_estimate=pl.CostEstimate(flops=10**6, bytes_accessed=2 * 10**6, transcendentals=0),
+    )(blocks)
+
+
+def unpack_kernel(core_ref, mine_ref, away_ref, sum_a_out, sum_b_out, sum_a_ref, sum_b_ref, sems):
     core = core_ref[0]
+    copies = []
+    for tap in range(9):
+        rows = slice(864 + 384 * tap, 1248 + 384 * tap)
+        mine, away = mine_ref[rows].astype(F32), away_ref[rows].astype(F32)
+        sum_b_ref[tap, :, 0:128] = jnp.where(core == 0, mine, away)
+        sum_b_ref[tap, :, 128:256] = jnp.where(core == 0, away, mine)
+        copies.append(pltpu.make_async_copy(sum_b_ref.at[tap], sum_b_out.at[tap], sems.at[tap]))
+        copies[-1].start()
     for tap in range(9):
         rows = slice(96 * tap, 96 * tap + 96)
         mine, away = mine_ref[rows].astype(F32), away_ref[rows].astype(F32)
         sum_a_ref[tap, 0] = jnp.where(core == 0, mine, away)
         sum_a_ref[tap, 1] = jnp.where(core == 0, away, mine)
-        rows = slice(864 + 384 * tap, 1248 + 384 * tap)
-        mine, away = mine_ref[rows].astype(F32), away_ref[rows].astype(F32)
-        sum_b_ref[tap, :, 0:128] = jnp.where(core == 0, mine, away)
-        sum_b_ref[tap, :, 128:256] = jnp.where(core == 0, away, mine)
+    copies.append(pltpu.make_async_copy(sum_a_ref, sum_a_out, sems.at[9]))
+    copies[-1].start()
+    for copy in copies:
+        copy.wait()
 
 
 def unpack(core, mine, away):
     return pl.pallas_call(
         unpack_kernel,
         in_specs=[SCALAR] + [WHOLE] * 2,
+        out_specs=(APART, APART),
         out_shape=(
             jax.ShapeDtypeStruct((9, 2, 96, 128), F32),
             jax.ShapeDtypeStruct((9, 384, 256), F32),
         ),
+        scratch_shapes=[
+            pltpu.VMEM((9, 2, 96, 128), F32),
+            pltpu.VMEM((9, 384, 256), F32),
+            pltpu.SemaphoreType.DMA((10,)),
+        ],
         compiler_params=pltpu.CompilerParams(vmem_limit_bytes=ROOM),
         cost_estimate=pl.CostEstimate(flops=0, bytes_accessed=7 * 10**6, transcendentals=0),
     )(core, mine, away)
@@ -343,10 +375,6 @@
 
 def exchange(blocks, groups):
     return lax.all_to_all(blocks, AXES, 0, 0, axis_index_groups=groups, tiled=True)
-
-
-def total_of(blocks):
-    return jnp.sum(blocks.astype(F32), axis=0).astype(BF16)
 
 
 def neighbours(to_left, to_right):
@@ -378,10 +406,10 @@
     rows = merge(keep_a, other_a, keep_b, other_b)
     blocks = exchange(rows.reshape(16, 272, 128), ACROSS)
     blocks, to_left, to_right = lax.optimization_barrier((blocks, to_left, to_right))
-    blocks = exchange(jnp.broadcast_to(total_of(blocks), (8, 272, 128)), ALONG)
+    blocks = exchange(total_copies(blocks, 8), ALONG)
     blocks, to_left, to_right = lax.optimization_barrier((blocks, to_left, to_right))
     from_left, from_right = neighbours(to_left, to_right)
-    blocks = exchange(jnp.broadcast_to(total_of(blocks), (16, 272, 128)), ACROSS)
+    blocks = exchange(total_copies(blocks, 16), ACROSS)
     blocks, from_left, from_right = lax.optimization_barrier((blocks, from_left, from_right))
     mine = blocks.reshape(4352, 128)
     away = other_core(mine)

time: 130 us -> 131 us (level)
    unnamed x15 -> x25, local copies, waits for them, and re-layouts: 2.28 us -> 3.73 us
    pallas_call x1 -> x3, Pallas kernels: 2.44 us -> 3.42 us  [the longest x1 2.2 us: unpack(): pl.pallas_call(unpack_kernel, in_specs=[SCALAR] + [WHOLE] * 2, out_specs=...]
  transfers between devices with their start and end apart: 11 -> 11, of which waited for: 8 -> 9; matrix products, arithmetic and copies ran while one was open for 4% -> 3% of each run, Pallas kernels for 8% -> 8%
where the time goes in v9:
time: 131 us; the launch traced here: 130 us
  waiting for transfers between devices  36.4 us (28%)
  starting transfers between devices  34.1 us (26%)
  blocking collectives  26.2 us (20%)
  Pallas kernels  23.1 us (18%)
  local copies, waits for them, and re-layouts  8.07 us (6%)
  other arithmetic  1.32 us (1%)
    all_to_all x1, blocking collectives, exchange(): lax.all_to_all(blocks, AXES, 0, 0, axis_index_groups=groups, tiled=True)  26.2 us
    all_to_all x2, waiting for transfers between devices, exchange(): lax.all_to_all(blocks, AXES, 0, 0, axis_index_groups=groups, tiled=True)  16.8 us
    ppermute x3, waiting for transfers between devices, neighbours(): lax.ppermute(to_left, 'slab', down)  16.6 us
    all_to_all x2, starting transfers between devices, exchange(): lax.all_to_all(blocks, AXES, 0, 0, axis_index_groups=groups, tiled=True)  11.8 us
    ppermute x3, starting transfers between devices, other_core(): return lax.ppermute(value, AXES, CORES)  9.39 us
    ppermute x3, starting transfers between devices, neighbours(): lax.ppermute(to_right, 'slab', up)  9.05 us
    pallas_call x1, Pallas kernels, block_b(): pl.pallas_call(block_b_kernel, in_specs=[SCALAR] + [WHOLE] * 5, out_shape...  6.76 us
    pallas_call x1, Pallas kernels, kernel_a(): pl.pallas_call(kernel_a_kernel, in_specs=[SCALAR] + [WHOLE] * 5, out_spec...  4.34 us
  transfers between devices with their start and end apart: 11, of which 9 were waited for; matrix products, arithmetic and copies ran while one was open for 3% of the time, Pallas kernels for 8%

profile of v9, /device:TPU:1, one launch (start us, length us, event | category | flops | bytes accessed | tf_op | source)
XLA Modules:
  0.0 130.3 jit_solution(14187647534377872610)
XLA Ops:
  0.7 1.2 fusion.2
  2.2 4.4 %collective-permute-start = (bf16[640,128]{1,0:T(8,128)(2,1)S(1)}, bf16[640,128]{1,0:T(8,128)(2,1)S(1)}, u32[]{:S(2)}, u32[]{:S(2)}) collective-permute-start(bf16[640,128]{1,0:T(8,128)(2,1)S(1)} %get-tuple-element.72), channel_id=1, source_target_pairs={{0,4},{4,8},{8,12},{12,16},{16,20},{20,24},{24,28},{28,32},{32,36}... | collective-permute-start | bytes 491528 | tf_op jit(solution)/shard_map/ppermute | solution.py:384
  6.6 1.3 collective-permute-start.1
  8.5 1.1 maximum_maximum_fusion.weight_ref
  9.6 3.7 %shard_map.75 = (bf16[4,544,256]{2,1,0:T(8,128)(2,1)S(1)}, f32[2,512,256]{2,1,0:T(8,128)S(1)}, bf16[2,512,256]{2,1,0:T(8,128)(2,1)S(1)}, f32[2,256,128]{2,1,0:T(8,128)S(1)}) custom-call(bf16[4,512,128]{2,1,0:T(8,128)(2,1)S(1)} %reshape.52.cells_ref, bf16[9,256,256]{2,1,0:T(8,128)(2,1)} %maximum_maximum_fusion.weight_ref), custom_call_target="tpu_custom_call" | custom-call | flops 2415919104 | bytes 6000000 | tf_op jit(solution)/shard_map/pallas_call | solution.py:85
  13.4 4.1 %collective-permute-done.1 = bf16[640,128]{1,0:T(8,128)(2,1)S(1)} collective-permute-done((bf16[640,128]{1,0:T(8,128)(2,1)S(1)}, bf16[640,128]{1,0:T(8,128)(2,1)S(1)}, u32[]{:S(2)}, u32[]{:S(2)}) %collective-permute-start.1) | collective-permute-done | bytes 163872 | tf_op jit(solution)/shard_map/ppermute | solution.py:384
  18.1 0.9 shard_map.76
  19.1 0.8 copy-done.1
  19.9 2.2 %collective-permute-start.2 = (bf16[2,256,128]{2,1,0:T(8,128)(2,1)S(1)}, bf16[2,256,128]{2,1,0:T(8,128)(2,1)S(1)}, u32[]{:S(2)}, u32[]{:S(2)}) collective-permute-start(bf16[2,256,128]{2,1,0:T(8,128)(2,1)S(1)} %get-tuple-element.34.cells_ref), channel_id=1, source_target_pairs={{0,4},{4,8},{8,12},{12,16},{16,20},{20,24},{24,28},{28,32},{32,36}... | collective-permute-start | bytes 393224 | tf_op jit(solution)/shard_map/ppermute | solution.py:384
  22.1 1.3 collective-permute-start.3
  24.4 7.1 %collective-permute-done.3.right_ref = bf16[2,256,128]{2,1,0:T(8,128)(2,1)S(1)} collective-permute-done((bf16[2,256,128]{2,1,0:T(8,128)(2,1)S(1)}, bf16[2,256,128]{2,1,0:T(8,128)(2,1)S(1)}, u32[]{:S(2)}, u32[]{:S(2)}) %collective-permute-start.3) | collective-permute-done | bytes 131104 | tf_op jit(solution)/shard_map/ppermute | solution.py:384
  31.5 6.8 %shard_map.77 = (bf16[64,256]{1,0:T(8,128)(2,1)}, bf16[9,384,128]{2,1,0:T(8,128)(2,1)S(1)}, bf16[9,384,128]{2,1,0:T(8,128)(2,1)S(1)}, bf16[2,256,128]{2,1,0:T(8,128)(2,1)S(1)}) custom-call(s32[1]{0:T(128)} %bitcast.core_ref, bf16[2,256,128]{2,1,0:T(8,128)(2,1)S(1)} %collective-permute-done.2.left_ref, bf16[2,256,128]{2,1,0:T(8,128)(2,1)S(1)} %get-tuple-element.34.cells_ref, ...), custom_call_target="tpu_custom_call" | custom-call | flops 3623878656 | bytes 5000000 | tf_op jit(solution)/shard_map/pallas_call | solution.py:181
  38.3 1.5 %collective-permute-start.5 = (bf16[9,384,128]{2,1,0:T(8,128)(2,1)S(1)}, bf16[9,384,128]{2,1,0:T(8,128)(2,1)S(1)}, u32[]{:S(2)}, u32[]{:S(2)}) collective-permute-start(bf16[9,384,128]{2,1,0:T(8,128)(2,1)S(1)} %get-tuple-element.46), channel_id=1, source_target_pairs={{0,1},{1,0},{2,3},{3,2},{4,5},{5,4},{6,7},{7,6},{8,9},{9,8},{10,11... | collective-permute-start | bytes 2654216 | tf_op jit(solution)/shard_map/ppermute | solution.py:373
  39.7 4.3 %shard_map.78 = (bf16[4,544,256]{2,1,0:T(8,128)(2,1)S(1)}, bf16[9,96,128]{2,1,0:T(8,128)(2,1)S(1)}, bf16[9,96,128]{2,1,0:T(8,128)(2,1)S(1)}) custom-call(s32[1]{0:T(128)} %bitcast.core_ref, bf16[2,256,128]{2,1,0:T(8,128)(2,1)S(1)} %get-tuple-element.36.grad_ref, bf16[2,512,256]{2,1,0:T(8,128)(2,1)S(1)} %copy-done.7, bf16[2,512,256]{2,1,0:T(8,128)(2,1)S(1)} %copy-done.2, ...), custom_call_target="tpu_custom_call" | custom-call | flops 2415919104 | bytes 6000000 | tf_op jit(solution)/shard_map/pallas_call | solution.py:233
  44.1 1.0 copy-done.4
  45.1 1.4 %collective-permute-done.4.other_a_ref = bf16[9,96,128]{2,1,0:T(8,128)(2,1)S(1)} collective-permute-done((bf16[9,96,128]{2,1,0:T(8,128)(2,1)S(1)}, bf16[9,96,128]{2,1,0:T(8,128)(2,1)S(1)}, u32[]{:S(2)}, u32[]{:S(2)}) %collective-permute-start.4) | collective-permute-done | bytes 221216 | tf_op jit(solution)/shard_map/ppermute | solution.py:373
  46.5 1.3 shard_map.80
  47.8 7.3 %all-to-all-start = ((bf16[16,272,128]{2,1,0:T(8,128)(2,1)}), bf16[16,272,128]{2,1,0:T(8,128)(2,1)S(1)}, u32[]{:S(2)}, u32[]{:S(2)}) async-start(bf16[16,272,128]{2,1,0:T(8,128)(2,1)} %bitcast.11), calls=%async_computation | async-start | bytes 2228224 | tf_op jit(solution)/shard_map/all_to_all | solution.py:377
  55.1 1.2 copy-done.5
  56.3 2.6 %shard_map.79 = (bf16[4,512,128]{2,1,0:T(8,128)(2,1)S(1)}, bf16[512,128]{1,0:T(8,128)(2,1)S(1)}, bf16[512,128]{1,0:T(8,128)(2,1)S(1)}) custom-call(bf16[4,544,256]{2,1,0:T(8,128)(2,1)S(1)} %copy-done.5, bf16[9,256,256]{2,1,0:T(8,128)(2,1)S(1)} %copy-done), custom_call_target="tpu_custom_call" | custom-call | flops 2415919104 | bytes 4000000 | tf_op jit(solution)/shard_map/pallas_call | solution.py:270
  59.0 13.1 %all-to-all-done.blocks_ref = bf16[16,272,128]{2,1,0:T(8,128)(2,1)S(1)} async-done(((bf16[16,272,128]{2,1,0:T(8,128)(2,1)}), bf16[16,272,128]{2,1,0:T(8,128)(2,1)S(1)}, u32[]{:S(2)}, u32[]{:S(2)}) %all-to-all-start) | async-done | bytes 1114144 | tf_op jit(solution)/shard_map/all_to_all | solution.py:377
  72.2 26.2 %all_to_all.15.blocks_ref = bf16[8,272,128]{2,1,0:T(8,128)(2,1)S(1)} all-to-all(bf16[8,272,128]{2,1,0:T(8,128)(2,1)S(1)} %shard_map.81), channel_id=1, replica_groups={{0,4,8,12,2,6,10,14},{1,5,9,13,3,7,11,15},{16,20,24,28,18,22,26,30},{17..., dimensions={0} | all-to-all | bytes 1114112 | tf_op jit(solution)/shard_map/all_to_all | solution.py:377
  98.4 1.1 shard_map.82
  99.5 4.5 %all-to-all-start.2 = ((bf16[16,272,128]{2,1,0:T(8,128)(2,1)}), bf16[16,272,128]{2,1,0:T(8,128)(2,1)S(1)}, u32[]{:S(2)}, u32[]{:S(2)}) async-start(bf16[16,272,128]{2,1,0:T(8,128)(2,1)} %shard_map.82), calls=%async_computation.2 | async-start | bytes 2228224 | tf_op jit(solution)/shard_map/all_to_all | solution.py:377
  104.0 2.5 %collective-permute-start.6 = (bf16[512,128]{1,0:T(8,128)(2,1)S(1)}, bf16[512,128]{1,0:T(8,128)(2,1)S(1)}, u32[]{:S(2)}, u32[]{:S(2)}) collective-permute-start(bf16[512,128]{1,0:T(8,128)(2,1)S(1)} %get-tuple-element.53), channel_id=1, source_target_pairs={{0,4},{4,8},{8,12},{12,16},{16,20},{20,24},{24,28},{28,32},{32,36}... | collective-permute-start | bytes 393224 | tf_op jit(solution)/shard_map/ppermute | solution.py:384
  106.5 1.3 collective-permute-start.7
  108.5 5.5 %collective-permute-done.7 = bf16[512,128]{1,0:T(8,128)(2,1)S(1)} collective-permute-done((bf16[512,128]{1,0:T(8,128)(2,1)S(1)}, bf16[512,128]{1,0:T(8,128)(2,1)S(1)}, u32[]{:S(2)}, u32[]{:S(2)}) %collective-permute-start.7) | collective-permute-done | bytes 131104 | tf_op jit(solution)/shard_map/ppermute | solution.py:384
  114.0 3.7 %all-to-all-done.2 = bf16[16,272,128]{2,1,0:T(8,128)(2,1)S(1)} async-done(((bf16[16,272,128]{2,1,0:T(8,128)(2,1)}), bf16[16,272,128]{2,1,0:T(8,128)(2,1)S(1)}, u32[]{:S(2)}, u32[]{:S(2)}) %all-to-all-start.2) | async-done | bytes 1114144 | tf_op jit(solution)/shard_map/all_to_all | solution.py:377
  117.7 7.9 %collective-permute-start.8 = (bf16[4352,128]{1,0:T(8,128)(2,1)S(1)}, bf16[4352,128]{1,0:T(8,128)(2,1)S(1)}, u32[]{:S(2)}, u32[]{:S(2)}) collective-permute-start(bf16[4352,128]{1,0:T(8,128)(2,1)S(1)} %bitcast.32), channel_id=1, source_target_pairs={{0,1},{1,0},{2,3},{3,2},{4,5},{5,4},{6,7},{7,6},{8,9},{9,8},{10,11... | collective-permute-start | bytes 3342344 | tf_op jit(solution)/shard_map/ppermute | solution.py:373
  125.7 1.4 %reshape.57 = bf16[1,4,32,32,64]{4,3,2,1,0:T(8,128)(2,1)} reshape(bf16[4,512,128]{2,1,0:T(8,128)(2,1)S(1)} %pad_maximum_fusion) | data formatting | bytes 1048576 | tf_op jit(solution)/shard_map/reshape | solution.py:422
  127.1 0.8 collective-permute-done.8.away_ref
  127.9 2.2 %shard_map.83 = (f32[9,2,96,128]{3,2,1,0:T(8,128)}, f32[9,384,256]{2,1,0:T(8,128)}) custom-call(s32[1]{0:T(128)} %bitcast.core_ref, bf16[4352,128]{1,0:T(8,128)(2,1)S(1)} %bitcast.33, bf16[4352,128]{1,0:T(8,128)(2,1)S(1)} %collective-permute-done.8.away_ref), custom_call_target="tpu_custom_call" | custom-call | bytes 7000000 | tf_op jit(solution)/shard_map/pallas_call | solution.py:348
  (46 shorter events, 3.6 us)
Async XLA Ops:
  0.6 7.3 %copy-start.8 = (bf16[1,4,32,32,64]{4,3,2,1,0:T(8,128)(2,1)S(1)}, bf16[1,4,32,32,64]{4,3,2,1,0:T(8,128)(2,1)}, u32[]{:S(2)}) copy-start(bf16[1,4,32,32,64]{4,3,2,1,0:T(8,128)(2,1)} %param.4) | copy-start | bytes 1572868
  0.6 1.5 %copy-start.11 = (bf16[1,1,8,8,256]{4,3,2,1,0:T(8,128)(2,1)S(1)}, bf16[1,1,8,8,256]{4,3,2,1,0:T(8,128)(2,1)}, u32[]{:S(2)}) copy-start(bf16[1,1,8,8,256]{4,3,2,1,0:T(8,128)(2,1)} %param.7) | copy-start | bytes 98308
  1.8 6.6 %copy-start.9 = (bf16[3,3,3,64,128]{4,3,2,1,0:T(8,128)(2,1)S(1)}, bf16[3,3,3,64,128]{4,3,2,1,0:T(8,128)(2,1)}, u32[]{:S(2)}) copy-start(bf16[3,3,3,64,128]{4,3,2,1,0:T(8,128)(2,1)} %param.5) | copy-start | bytes 1327108
  2.2 11.2 %collective-permute-start = (bf16[640,128]{1,0:T(8,128)(2,1)S(1)}, bf16[640,128]{1,0:T(8,128)(2,1)S(1)}, u32[]{:S(2)}, u32[]{:S(2)}) collective-permute-start(bf16[640,128]{1,0:T(8,128)(2,1)S(1)} %get-tuple-element.72), channel_id=1, source_target_pairs={{0,4},{4,8},{8,12},{12,16},{16,20},{20,24},{24,28},{28,32},{32,36}... | collective-permute-start | bytes 491528 | tf_op jit(solution)/shard_map/ppermute | solution.py:384
  6.6 10.9 %collective-permute-start.1 = (bf16[640,128]{1,0:T(8,128)(2,1)S(1)}, bf16[640,128]{1,0:T(8,128)(2,1)S(1)}, u32[]{:S(2)}, u32[]{:S(2)}) collective-permute-start(bf16[640,128]{1,0:T(8,128)(2,1)S(1)} %get-tuple-element.71), channel_id=1, source_target_pairs={{4,0},{8,4},{12,8},{16,12},{20,16},{24,20},{28,24},{32,28},{36,32}... | collective-permute-start | bytes 491528 | tf_op jit(solution)/shard_map/ppermute | solution.py:384
  9.6 8.5 %copy-start = (bf16[9,256,256]{2,1,0:T(8,128)(2,1)S(1)}, bf16[9,256,256]{2,1,0:T(8,128)(2,1)}, u32[]{:S(2)}) copy-start(bf16[9,256,256]{2,1,0:T(8,128)(2,1)} %maximum_maximum_fusion.weight_ref) | copy-start | bytes 3538948
  13.3 5.7 %copy-start.3 = (bf16[4,544,256]{2,1,0:T(8,128)(2,1)}, bf16[4,544,256]{2,1,0:T(8,128)(2,1)S(1)}, u32[]{:S(2)}) copy-start(bf16[4,544,256]{2,1,0:T(8,128)(2,1)S(1)} %get-tuple-element.39.window_ref) | copy-start | bytes 3342340
  13.3 5.7 %copy-start.6 = (bf16[2,512,256]{2,1,0:T(8,128)(2,1)}, bf16[2,512,256]{2,1,0:T(8,128)(2,1)S(1)}, u32[]{:S(2)}) copy-start(bf16[2,512,256]{2,1,0:T(8,128)(2,1)S(1)} %get-tuple-element.37.slope_ref) | copy-start | bytes 1572868
  17.4 0.7 copy-start.10
  19.1 0.8 copy-start.1
  19.9 4.5 %collective-permute-start.2 = (bf16[2,256,128]{2,1,0:T(8,128)(2,1)S(1)}, bf16[2,256,128]{2,1,0:T(8,128)(2,1)S(1)}, u32[]{:S(2)}, u32[]{:S(2)}) collective-permute-start(bf16[2,256,128]{2,1,0:T(8,128)(2,1)S(1)} %get-tuple-element.34.cells_ref), channel_id=1, source_target_pairs={{0,4},{4,8},{8,12},{12,16},{16,20},{20,24},{24,28},{28,32},{32,36}... | collective-permute-start | bytes 393224 | tf_op jit(solution)/shard_map/ppermute | solution.py:384
  22.1 9.4 %collective-permute-start.3 = (bf16[2,256,128]{2,1,0:T(8,128)(2,1)S(1)}, bf16[2,256,128]{2,1,0:T(8,128)(2,1)S(1)}, u32[]{:S(2)}, u32[]{:S(2)}) collective-permute-start(bf16[2,256,128]{2,1,0:T(8,128)(2,1)S(1)} %get-tuple-element.34.cells_ref), channel_id=1, source_target_pairs={{4,0},{8,4},{12,8},{16,12},{20,16},{24,20},{28,24},{32,28},{36,32}... | collective-permute-start | bytes 393224 | tf_op jit(solution)/shard_map/ppermute | solution.py:384
  31.5 8.2 %copy-start.2 = (bf16[2,512,256]{2,1,0:T(8,128)(2,1)S(1)}, bf16[2,512,256]{2,1,0:T(8,128)(2,1)}, u32[]{:S(2)}) copy-start(bf16[2,512,256]{2,1,0:T(8,128)(2,1)} %copy-done.1) | copy-start | bytes 1572868
  31.5 8.2 %copy-start.7 = (bf16[2,512,256]{2,1,0:T(8,128)(2,1)S(1)}, bf16[2,512,256]{2,1,0:T(8,128)(2,1)}, u32[]{:S(2)}) copy-start(bf16[2,512,256]{2,1,0:T(8,128)(2,1)} %copy-done.6) | copy-start | bytes 1572868
  38.3 8.3 %collective-permute-start.5 = (bf16[9,384,128]{2,1,0:T(8,128)(2,1)S(1)}, bf16[9,384,128]{2,1,0:T(8,128)(2,1)S(1)}, u32[]{:S(2)}, u32[]{:S(2)}) collective-permute-start(bf16[9,384,128]{2,1,0:T(8,128)(2,1)S(1)} %get-tuple-element.46), channel_id=1, source_target_pairs={{0,1},{1,0},{2,3},{3,2},{4,5},{5,4},{6,7},{7,6},{8,9},{9,8},{10,11... | collective-permute-start | bytes 2654216 | tf_op jit(solution)/shard_map/ppermute | solution.py:373
  44.1 1.0 copy-start.4
  45.1 1.5 %collective-permute-start.4 = (bf16[9,96,128]{2,1,0:T(8,128)(2,1)S(1)}, bf16[9,96,128]{2,1,0:T(8,128)(2,1)S(1)}, u32[]{:S(2)}, u32[]{:S(2)}) collective-permute-start(bf16[9,96,128]{2,1,0:T(8,128)(2,1)S(1)} %get-tuple-element.44), channel_id=1, source_target_pairs={{0,1},{1,0},{2,3},{3,2},{4,5},{5,4},{6,7},{7,6},{8,9},{9,8},{10,11... | collective-permute-start | bytes 663560 | tf_op jit(solution)/shard_map/ppermute | solution.py:373
  47.8 24.2 %all-to-all-start = ((bf16[16,272,128]{2,1,0:T(8,128)(2,1)}), bf16[16,272,128]{2,1,0:T(8,128)(2,1)S(1)}, u32[]{:S(2)}, u32[]{:S(2)}) async-start(bf16[16,272,128]{2,1,0:T(8,128)(2,1)} %bitcast.11), calls=%async_computation | async-start | bytes 2228224 | tf_op jit(solution)/shard_map/all_to_all | solution.py:377
  55.1 1.3 copy-start.5
  99.5 18.2 %all-to-all-start.2 = ((bf16[16,272,128]{2,1,0:T(8,128)(2,1)}), bf16[16,272,128]{2,1,0:T(8,128)(2,1)S(1)}, u32[]{:S(2)}, u32[]{:S(2)}) async-start(bf16[16,272,128]{2,1,0:T(8,128)(2,1)} %shard_map.82), calls=%async_computation.2 | async-start | bytes 2228224 | tf_op jit(solution)/shard_map/all_to_all | solution.py:377
  104.0 4.4 %collective-permute-start.6 = (bf16[512,128]{1,0:T(8,128)(2,1)S(1)}, bf16[512,128]{1,0:T(8,128)(2,1)S(1)}, u32[]{:S(2)}, u32[]{:S(2)}) collective-permute-start(bf16[512,128]{1,0:T(8,128)(2,1)S(1)} %get-tuple-element.53), channel_id=1, source_target_pairs={{0,4},{4,8},{8,12},{12,16},{16,20},{20,24},{24,28},{28,32},{32,36}... | collective-permute-start | bytes 393224 | tf_op jit(solution)/shard_map/ppermute | solution.py:384
  106.5 7.4 %collective-permute-start.7 = (bf16[512,128]{1,0:T(8,128)(2,1)S(1)}, bf16[512,128]{1,0:T(8,128)(2,1)S(1)}, u32[]{:S(2)}, u32[]{:S(2)}) collective-permute-start(bf16[512,128]{1,0:T(8,128)(2,1)S(1)} %get-tuple-element.54), channel_id=1, source_target_pairs={{4,0},{8,4},{12,8},{16,12},{20,16},{24,20},{28,24},{32,28},{36,32}... | collective-permute-start | bytes 393224 | tf_op jit(solution)/shard_map/ppermute | solution.py:384
  117.7 10.3 %collective-permute-start.8 = (bf16[4352,128]{1,0:T(8,128)(2,1)S(1)}, bf16[4352,128]{1,0:T(8,128)(2,1)S(1)}, u32[]{:S(2)}, u32[]{:S(2)}) collective-permute-start(bf16[4352,128]{1,0:T(8,128)(2,1)S(1)} %bitcast.32), channel_id=1, source_target_pairs={{0,1},{1,0},{2,3},{3,2},{4,5},{5,4},{6,7},{7,6},{8,9},{9,8},{10,11... | collective-permute-start | bytes 3342344 | tf_op jit(solution)/shard_map/ppermute | solution.py:373
